TPU v7x, 512 devices: a whole 4x8x8 slice. The times are simulated.
512 devices in a mesh: shot: 16 (over x_lo, z), tile: 32 (over y, x_hi, core).
Axes of the slice: x: 4 (x_hi: 2, x_lo: 2; x = x_hi * 2 + x_lo), y: 8, z: 8, core: 2. Of those that a mesh axis runs over, the one named last changes fastest.
Arguments:
- latent: bfloat16 [96, 16, 64, 64], P('tile', 'shot'), may hold values from -6 to 6
- kernel: bfloat16 [27, 64, 64], replicated, may hold values from -0.15625 to 0.15625
- conv_bias: float32 [64], replicated, may hold values from -3 to 3
- head_weight: bfloat16 [64], replicated, may hold values from -0.75 to 0.75
- density: float32 [192, 32, 128], P('tile'), may hold values from 1 to 2.5
- wave_prev: float32 [16, 192, 32, 128], P('shot', 'tile'), may hold values from -6 to 6
- wave_now: float32 [16, 192, 32, 128], P('shot', 'tile'), may hold values from -6 to 6
- adjoint_next: float32 [16, 192, 32, 128], P('shot', 'tile'), may hold values from -6 to 6
- adjoint_after: float32 [16, 192, 32, 128], P('shot', 'tile'), may hold values from -6 to 6
- source_cell: int32 [16], P('shot'), may hold values from 0 to 786431
- wavelet: float32 [16, 3], P('shot'), may hold values from -24 to 24
- receiver_cells: int32 [16, 128], P('shot'), may hold values from 0 to 786431
- observed: float32 [16, 3, 128], P('shot'), may hold values from -6 to 6
Outputs:
- latent_grad: float32 [96, 16, 64, 64], P('tile', 'shot')
- kernel_grad: float32 [27, 64, 64], replicated
- head_grad: float32 [64], replicated
- bias_grad: float32 [64], replicated
All inputs are finite; a program needn't handle non-finite values.
Results may differ from a plain program's by a relative error of at most 0.0034.
The roundings to bfloat16 on the way count: a program that leaves them out, or rounds other values in their place, can miss the bound.
Values may be sent and summed in bfloat16 or wider, within the bound.
No kernel may reach another device: no remote copies, remote signals or barrier semaphores. Data moves between devices by JAX's collectives and lax.ppermute only.
A program may use at most 64 MiB of HBM per device.

v0:
```python
import jax
import jax.numpy as jnp
from jax import lax
from jax.sharding import PartitionSpec as P

courant = 0.005
speed_low = 1.5
speed_span = 3.0


def padded_2(cells, sides, width):
    for axis, dim in sides:
        count = lax.axis_size(axis)
        ends = count - 1
        head = lax.slice_in_dim(cells, 0, width, axis=dim)
        tail = lax.slice_in_dim(cells, cells.shape[dim] - width, cells.shape[dim], axis=dim)
        cells = jnp.concatenate(
            [
                lax.ppermute(tail, axis, [(i, (i + 1) % count) for i in range(ends)]),
                cells,
                lax.ppermute(head, axis, [((i + 1) % count, i) for i in range(ends)]),
            ],
            axis=dim,
        )
    return cells


def upsample(coarse):
    coarse_x, coarse_z, channels, coarse_y = coarse.shape
    spread = jnp.broadcast_to(
        coarse[:, None, :, None, :, :, None], (coarse_x, 2, coarse_z, 2, channels, coarse_y, 2)
    )
    return spread.reshape(coarse_x * 2, coarse_z * 2, channels, coarse_y * 2)


def fold_children(fine):
    fine_x, fine_z, channels, fine_y = fine.shape
    grouped = fine.reshape(fine_x // 2, 2, fine_z // 2, 2, channels, fine_y // 2, 2)
    return jnp.sum(grouped, axis=(1, 3, 6))


def shifted_stack(padded, start_x, start_z, starts_y, cells_x, cells_z, cells_y):
    return jnp.concatenate(
        [
            padded[
                start_x : start_x + cells_x,
                start_z : start_z + cells_z,
                :,
                start_y : start_y + cells_y,
            ]
            for start_y in starts_y
        ],
        axis=2,
    )


def convolve(padded, kernel):
    cells_x = padded.shape[0] - 2
    cells_z = padded.shape[1] - 2
    channels = padded.shape[2]
    cells_y = padded.shape[3] - 2
    tap_table = kernel.reshape(3, 3, 3, channels, channels)
    result = jnp.zeros((cells_x, cells_z, channels, cells_y), jnp.float32)
    for offset_x in range(3):
        for offset_z in range(3):
            stacked = shifted_stack(
                padded, offset_x, offset_z, (0, 1, 2), cells_x, cells_z, cells_y
            )
            matrix = jnp.transpose(tap_table[offset_x, offset_z], (1, 0, 2)).reshape(
                channels, 3 * channels
            )
            result = result + jnp.einsum(
                "ok,abky->aboy", matrix, stacked, preferred_element_type=jnp.float32
            )
    return result


def kernel_terms(padded, grad_low):
    cells_x, cells_z, channels, cells_y = grad_low.shape
    pieces = []
    for offset_x in range(3):
        for offset_z in range(3):
            stacked = shifted_stack(
                padded, offset_x, offset_z, (0, 1, 2), cells_x, cells_z, cells_y
            )
            product = jnp.einsum(
                "aboy,abky->ok", grad_low, stacked, preferred_element_type=jnp.float32
            )
            pieces.append(jnp.transpose(product.reshape(channels, 3, channels), (1, 0, 2)))
    return jnp.stack(pieces).reshape(27, channels, channels)


def transposed(grad_padded, kernel):
    cells_x = grad_padded.shape[0] - 2
    cells_z = grad_padded.shape[1] - 2
    channels = grad_padded.shape[2]
    cells_y = grad_padded.shape[3] - 2
    tap_table = kernel.reshape(3, 3, 3, channels, channels)
    result = jnp.zeros((cells_x, cells_z, channels, cells_y), jnp.float32)
    for offset_x in range(3):
        for offset_z in range(3):
            stacked = shifted_stack(
                grad_padded, 2 - offset_x, 2 - offset_z, (2, 1, 0), cells_x, cells_z, cells_y
            )
            matrix = tap_table[offset_x, offset_z].reshape(3 * channels, channels)
            result = result + jnp.einsum(
                "kc,abky->abcy", matrix, stacked, preferred_element_type=jnp.float32
            )
    return result


def neighbours(padded):
    return (
        padded[2:, 1:-1, 1:-1],
        padded[:-2, 1:-1, 1:-1],
        padded[1:-1, 2:, 1:-1],
        padded[1:-1, :-2, 1:-1],
        padded[1:-1, 1:-1, 2:],
        padded[1:-1, 1:-1, :-2],
    )


def face_weights(padded_buoyancy):
    centre = padded_buoyancy[1:-1, 1:-1, 1:-1]
    return tuple((0.5 * (centre + beside) for beside in neighbours(padded_buoyancy)))


def apply_faces(padded, faces):
    centre = padded[1:-1, 1:-1, 1:-1]
    result = jnp.zeros_like(centre)
    for weight, beside in zip(faces, neighbours(padded)):
        result = result + weight * (beside - centre)
    return result


def propagate(
    laplace,
    coefficient,
    previous,
    current,
    following,
    beyond,
    anchor,
    source_cell,
    wavelet,
    receiver_cells,
    observed,
):
    field_shape = previous.shape
    field_cells = previous.size
    source_local = source_cell[0] - anchor
    source_owned = jnp.logical_and(source_local >= 0, source_local < field_cells).astype(
        jnp.float32
    )
    source_spot = jnp.clip(source_local, 0, field_cells - 1)
    receiver_local = receiver_cells[0] - anchor
    receiver_owned = jnp.logical_and(receiver_local >= 0, receiver_local < field_cells).astype(
        jnp.float32
    )
    receiver_spot = jnp.clip(receiver_local, 0, field_cells - 1)
    count_steps = wavelet.shape[1]
    laplacians = []
    residuals = []
    for instant in range(count_steps):
        laplacian = laplace(current)
        laplacians.append(laplacian)
        advanced = 2.0 * current - previous + coefficient * laplacian
        advanced = (
            advanced.reshape(-1)
            .at[source_spot]
            .add(source_owned * wavelet[0, instant])
            .reshape(field_shape)
        )
        residuals.append(
            receiver_owned * (advanced.reshape(-1)[receiver_spot] - observed[0, instant])
        )
        previous, current = (current, advanced)
    laplacians.append(laplace(current))
    coef_grad = following * laplacians[count_steps]
    for instant in reversed(range(count_steps)):
        preceding = 2.0 * following - beyond + laplace(coefficient * following)
        preceding = (
            preceding.reshape(-1).at[receiver_spot].add(residuals[instant]).reshape(field_shape)
        )
        coef_grad = coef_grad + preceding * laplacians[instant]
        beyond, following = (following, preceding)
    return coef_grad


def per_device(
    latent,
    kernel,
    conv_bias,
    head_weight,
    density,
    wave_prev,
    wave_now,
    adjoint_next,
    adjoint_after,
    source_cell,
    wavelet,
    receiver_cells,
    observed,
):
    extended = padded_2(upsample(latent), (("shot", 1), ("tile", 0)), 1)
    padded = jnp.pad(extended, ((0, 0), (0, 0), (0, 0), (1, 1)))
    pre_act = convolve(padded, kernel) + conv_bias[None, None, :, None]
    hidden = jax.nn.silu(pre_act).astype(jnp.bfloat16)
    logit = jnp.einsum("abcy,c->aby", hidden, head_weight, preferred_element_type=jnp.float32)
    squash = jax.nn.sigmoid(logit)
    velocity = speed_low + speed_span * squash
    tile_speed = lax.all_gather(velocity, "shot", axis=1, tiled=True)
    tile_cells = tile_speed.size
    buoyancy = 1.0 / density
    coefficient = courant * tile_speed * tile_speed * density
    factor = 2.0 * courant * tile_speed * density
    buoyancy_edges = padded_2(buoyancy, (("tile", 0),), 1)
    faces = face_weights(jnp.pad(buoyancy_edges, ((0, 0), (1, 1), (1, 1))))

    def laplace(field):
        field_edges = padded_2(field, (("tile", 0),), 1)
        return apply_faces(jnp.pad(field_edges, ((0, 0), (1, 1), (1, 1))), faces)

    anchor = lax.axis_index("tile") * tile_cells
    coef_grad = propagate(
        laplace,
        coefficient,
        wave_prev[0],
        wave_now[0],
        adjoint_next[0],
        adjoint_after[0],
        anchor,
        source_cell,
        wavelet,
        receiver_cells,
        observed,
    )
    strip_grad = lax.psum_scatter(coef_grad * factor, "shot", scatter_dimension=1, tiled=True)
    logit_grad = strip_grad * speed_span * squash * (1.0 - squash)
    head_part = jnp.einsum(
        "abcy,aby->c", hidden.astype(jnp.float32), logit_grad, precision=lax.Precision.HIGHEST
    )
    gate = jax.nn.sigmoid(pre_act)
    pre_grad = (
        logit_grad[:, :, None, :]
        * head_weight.astype(jnp.float32)[None, None, :, None]
        * (gate * (1.0 + pre_act * (1.0 - gate)))
    )
    bias_part = jnp.sum(pre_grad, axis=(0, 1, 3))
    grad_low = pre_grad.astype(jnp.bfloat16)
    kernel_part = kernel_terms(padded, grad_low)
    grad_edges = padded_2(grad_low, (("shot", 1), ("tile", 0)), 1)
    grad_padded = jnp.pad(grad_edges, ((0, 0), (0, 0), (0, 0), (1, 1)))
    latent_grad = fold_children(transposed(grad_padded, kernel))
    kernel_grad, head_grad, bias_grad = lax.psum(
        (kernel_part, head_part, bias_part), ("shot", "tile")
    )
    return (latent_grad, kernel_grad, head_grad, bias_grad)


def solution(mesh):
    return jax.shard_map(
        per_device,
        mesh=mesh,
        in_specs=(
            P("tile", "shot", None, None),
            P(),
            P(),
            P(),
            P("tile", None, None),
            P("shot", "tile", None, None),
            P("shot", "tile", None, None),
            P("shot", "tile", None, None),
            P("shot", "tile", None, None),
            P("shot"),
            P("shot", None),
            P("shot", None),
            P("shot", None, None),
        ),
        out_specs=(P("tile", "shot", None, None), P(), P(), P()),
        check_vma=False,
    )
```

profile of v0, /device:TPU:1, one launch (start us, length us, event | category | flops | bytes accessed | tf_op | source)
XLA Modules:
  0.0 590.1 jit_solution(18035886360403443610)
XLA Ops:
  7.2 0.9 copy.175
  8.4 4.8 collective-permute-start.1
  13.2 1.3 collective-permute-start.2
  14.5 0.7 slice_bitcast_fusion.6
  15.3 5.2 collective-permute-start.5
  20.5 2.2 collective-permute-start.7
  23.5 0.9 fusion.250
  26.8 2.4 collective-permute-start.3
  29.2 1.9 collective-permute-start.4
  31.4 5.0 collective-permute-done.4
  36.9 1.0 fusion.245
  42.4 32.4 %all_gather.3 = f32[6,32,128]{2,0,1:T(8,128)S(1)} all-gather(f32[6,2,128]{2,0,1:T(8,128)S(1)} %multiply_add_fusion.2), channel_id=1, replica_groups=mesh['shot'=16,'tile'=32] {'shot'}, dimensions={1}, use_global_device_ids=true | all-gather | bytes 104448 | tf_op jit(solution)/shard_map/all_gather | solution.py:212
  74.9 5.3 collective-permute-start
  80.3 6.1 %collective-permute-start.6 = (f32[1,32,128]{2,1,0:T(8,128)S(1)}, f32[1,32,128]{2,1,0:T(8,128)S(1)}, u32[]{:S(2)}, u32[]{:S(2)}) collective-permute-start(f32[1,32,128]{2,1,0:T(8,128)S(1)} %get-tuple-element.149), channel_id=1, source_target_pairs={{0,1},{1,2},{2,3},{3,4},{4,5},{5,6},{6,7},{7,8},{8,9},{9,10},{10,1... | collective-permute-start | bytes 49160 | tf_op jit(solution)/shard_map/ppermute | solution.py:19
  86.4 1.9 collective-permute-start.14
  88.4 5.1 collective-permute-start.15
  95.2 1.9 collective-permute-start.8
  97.1 5.7 collective-permute-start.9
  104.2 1.9 collective-permute-start.10
  106.1 5.7 collective-permute-start.11
  112.5 1.1 gather_fusion.2
  113.6 1.1 gather_fusion.1
  115.4 1.1 gather_fusion
  116.5 1.5 scatter_fusion
  118.1 1.9 collective-permute-start.16
  120.0 5.1 collective-permute-start.17
  125.2 1.9 collective-permute-start.12
  127.1 5.1 collective-permute-start.13
  132.6 1.5 scatter_fusion.1
  134.1 1.9 collective-permute-start.18
  136.0 5.4 collective-permute-start.19
  142.7 1.7 scatter_fusion.2
  144.3 0.9 fusion.136
  145.3 1.3 dynamic-slice.27
  147.2 136.4 %all-reduce.17.cloned.1.call-done = f32[6,32,128]{2,1,0:T(8,128)} async-done(((f32[6,32,128]{2,1,0:T(8,128)}), f32[6,32,128]{2,1,0:T(8,128)}) %all-reduce.17.cloned.1.call-update) | async-done | bytes 98320
  283.6 0.7 constant_dynamic-slice_fusion
  284.7 1.4 fusion.74
  292.0 1.7 collective-permute-start.20
  293.7 1.3 collective-permute-start.21
  295.8 1.2 copy.221
  297.0 2.1 collective-permute-done.21
  299.1 16.4 %collective-permute-start.22 = (bf16[1,4,64,128]{3,2,1,0:T(8,128)(2,1)S(1)}, bf16[1,4,64,128]{3,2,1,0:T(8,128)(2,1)S(1)}, u32[]{:S(2)}, u32[]{:S(2)}) collective-permute-start(bf16[1,4,64,128]{3,2,1,0:T(8,128)(2,1)S(1)} %get-tuple-element.129), channel_id=1, source_target_pairs={{0,1},{1,2},{2,3},{3,4},{4,5},{5,6},{6,7},{7,8},{8,9},{9,10},{10,1... | collective-permute-start | bytes 196616 | tf_op jit(solution)/shard_map/ppermute | solution.py:19
  315.5 1.9 collective-permute-start.23
  317.7 101.1 %all-reduce.11 = (f32[64]{0:T(128)}, f32[64]{0:T(128)}) all-reduce(f32[64]{0:T(128)S(1)} %convolution_bitcast_fusion, f32[64]{0:T(128)S(1)} %get-tuple-element.46), channel_id=1, replica_groups=mesh['shot'=16,'tile'=32] {'shot','tile'}, use_global_device_ids=true, to_apply=%region_7.8 | all-reduce | flops 128 | bytes 1024 | tf_op jit(solution)/shard_map/psum | solution.py:255
  419.6 1.0 fusion.244
  426.0 0.7 copy.222
  426.7 154.3 %all-reduce.15.cloned.1.call-done = f32[27,64,64]{2,1,0:T(8,128)} async-done(((f32[27,64,64]{2,1,0:T(8,128)}), f32[27,64,64]{2,1,0:T(8,128)}) %all-reduce.15.cloned.1.call-update) | async-done | bytes 442384 | tf_op jit(solution)/shard_map/psum | solution.py:255
  581.0 2.2 copy.315
  (240 shorter events, 24.4 us)
Async XLA Ops:
  7.2 16.3 %copy-start.3 = (bf16[27,64,64]{2,1,0:T(8,128)(2,1)S(1)}, bf16[27,64,64]{2,1,0:T(8,128)(2,1)}, u32[]{:S(2)}) copy-start(bf16[27,64,64]{2,1,0:T(8,128)(2,1)} %param.20) | copy-start | bytes 663556
  7.2 276.5 %all-reduce.17.cloned.1.call-start = ((), (), s32[]{:S(2)}) async-start(), calls=%async_computation.1 | async-start | bytes 196608
  8.4 18.3 %collective-permute-start.1 = (bf16[6,1,64,128]{3,2,1,0:T(8,128)(2,1)S(1)}, bf16[6,1,64,128]{3,2,1,0:T(8,128)(2,1)S(1)}, u32[]{:S(2)}, u32[]{:S(2)}) collective-permute-start(bf16[6,1,64,128]{3,2,1,0:T(8,128)(2,1)S(1)} %copy.176), channel_id=1, source_target_pairs={{0,32},{32,64},{64,96},{96,128},{128,160},{160,192},{192,224},{224... | collective-permute-start | bytes 294920 | tf_op jit(solution)/shard_map/ppermute | solution.py:19
  13.2 13.5 %collective-permute-start.2 = (bf16[6,1,64,128]{3,2,1,0:T(8,128)(2,1)S(1)}, bf16[6,1,64,128]{3,2,1,0:T(8,128)(2,1)S(1)}, u32[]{:S(2)}, u32[]{:S(2)}) collective-permute-start(bf16[6,1,64,128]{3,2,1,0:T(8,128)(2,1)S(1)} %copy.176), channel_id=1, source_target_pairs={{32,0},{64,32},{96,64},{128,96},{160,128},{192,160},{224,192},{256... | collective-permute-start | bytes 294920 | tf_op jit(solution)/shard_map/ppermute | solution.py:21
  15.3 15.9 %collective-permute-start.5 = (f32[1,32,128]{2,1,0:T(8,128)S(1)}, f32[1,32,128]{2,1,0:T(8,128)S(1)}, u32[]{:S(2)}, u32[]{:S(2)}) collective-permute-start(f32[1,32,128]{2,1,0:T(8,128)S(1)} %get-tuple-element.148), channel_id=1, source_target_pairs={{1,0},{2,1},{3,2},{4,3},{5,4},{6,5},{7,6},{8,7},{9,8},{10,9},{11,1... | collective-permute-start | bytes 49160 | tf_op jit(solution)/shard_map/ppermute | solution.py:21
  20.5 10.6 %collective-permute-start.7 = (f32[1,32,128]{2,1,0:T(8,128)S(1)}, f32[1,32,128]{2,1,0:T(8,128)S(1)}, u32[]{:S(2)}, u32[]{:S(2)}) collective-permute-start(f32[1,32,128]{2,1,0:T(8,128)S(1)} %get-tuple-element.147), channel_id=1, source_target_pairs={{0,1},{1,2},{2,3},{3,4},{4,5},{5,6},{6,7},{7,8},{8,9},{9,10},{10,1... | collective-permute-start | bytes 49160 | tf_op jit(solution)/shard_map/ppermute | solution.py:19
  23.5 1.9 copy-start.53
  24.4 6.7 %copy-start = (f32[1,6,32,128]{3,2,1,0:T(8,128)S(1)}, f32[1,6,32,128]{3,2,1,0:T(8,128)}, u32[]{:S(2)}) copy-start(f32[1,6,32,128]{3,2,1,0:T(8,128)} %param.25) | copy-start | bytes 294916
  26.8 4.5 collective-permute-start.3
  29.2 7.1 %collective-permute-start.4 = (bf16[1,4,64,128]{3,2,1,0:T(8,128)(2,1)S(1)}, bf16[1,4,64,128]{3,2,1,0:T(8,128)(2,1)S(1)}, u32[]{:S(2)}, u32[]{:S(2)}) collective-permute-start(bf16[1,4,64,128]{3,2,1,0:T(8,128)(2,1)S(1)} %get-tuple-element.134), channel_id=1, source_target_pairs={{1,0},{2,1},{3,2},{4,3},{5,4},{6,5},{7,6},{8,7},{9,8},{10,9},{11,1... | collective-permute-start | bytes 196616 | tf_op jit(solution)/shard_map/ppermute | solution.py:21
  38.0 2.1 copy-start.4
  38.0 2.1 copy-start.6
  38.0 2.7 copy-start.20
  38.0 2.7 copy-start.22
  38.0 3.0 copy-start.24
  38.0 3.0 copy-start.26
  38.0 3.3 copy-start.28
  38.0 3.3 copy-start.29
  38.4 2.3 copy-start.36
  38.4 2.6 copy-start.38
  38.4 2.9 copy-start.40
  41.6 33.2 %copy-start.1 = (f32[1,6,32,128]{3,2,1,0:T(8,128)S(1)}, f32[1,6,32,128]{3,2,1,0:T(8,128)}, u32[]{:S(2)}) copy-start(f32[1,6,32,128]{3,2,1,0:T(8,128)} %param.26) | copy-start | bytes 294916
  41.6 33.2 %copy-start.2 = (f32[6,32,128]{2,1,0:T(8,128)S(1)}, f32[6,32,128]{2,1,0:T(8,128)}, u32[]{:S(2)}) copy-start(f32[6,32,128]{2,1,0:T(8,128)} %param.23) | copy-start | bytes 294916
  42.0 52.4 %copy-start.41 = (bf16[6,2,64,128]{3,2,1,0:T(8,128)(2,1)}, bf16[6,2,64,128]{3,2,1,0:T(8,128)(2,1)S(1)}, u32[]{:S(2)}) copy-start(bf16[6,2,64,128]{3,2,1,0:T(8,128)(2,1)S(1)} %get-tuple-element.160) | copy-start | bytes 589828
  42.0 52.6 %copy-start.43 = (f32[1,6,32,128]{3,2,1,0:T(8,128)S(1)}, f32[1,6,32,128]{3,2,1,0:T(8,128)}, u32[]{:S(2)}) copy-start(f32[1,6,32,128]{3,2,1,0:T(8,128)} %param.27) | copy-start | bytes 294916
  74.9 18.6 %collective-permute-start = (f32[1,32,128]{2,1,0:T(8,128)S(1)}, f32[1,32,128]{2,1,0:T(8,128)S(1)}, u32[]{:S(2)}, u32[]{:S(2)}) collective-permute-start(f32[1,32,128]{2,1,0:T(8,128)S(1)} %get-tuple-element.150), channel_id=1, source_target_pairs={{1,0},{2,1},{3,2},{4,3},{5,4},{6,5},{7,6},{8,7},{9,8},{10,9},{11,1... | collective-permute-start | bytes 49160 | tf_op jit(solution)/shard_map/ppermute | solution.py:21
  80.3 13.3 %collective-permute-start.6 = (f32[1,32,128]{2,1,0:T(8,128)S(1)}, f32[1,32,128]{2,1,0:T(8,128)S(1)}, u32[]{:S(2)}, u32[]{:S(2)}) collective-permute-start(f32[1,32,128]{2,1,0:T(8,128)S(1)} %get-tuple-element.149), channel_id=1, source_target_pairs={{0,1},{1,2},{2,3},{3,4},{4,5},{5,6},{6,7},{7,8},{8,9},{9,10},{10,1... | collective-permute-start | bytes 49160 | tf_op jit(solution)/shard_map/ppermute | solution.py:19
  86.4 7.3 %collective-permute-start.14 = (f32[1,32,128]{2,1,0:T(8,128)S(1)}, f32[1,32,128]{2,1,0:T(8,128)S(1)}, u32[]{:S(2)}, u32[]{:S(2)}) collective-permute-start(f32[1,32,128]{2,1,0:T(8,128)S(1)} %get-tuple-element.153), channel_id=1, source_target_pairs={{1,0},{2,1},{3,2},{4,3},{5,4},{6,5},{7,6},{8,7},{9,8},{10,9},{11,1... | collective-permute-start | bytes 49160 | tf_op jit(solution)/shard_map/ppermute | solution.py:21
  88.4 6.0 %collective-permute-start.15 = (f32[1,32,128]{2,1,0:T(8,128)S(1)}, f32[1,32,128]{2,1,0:T(8,128)S(1)}, u32[]{:S(2)}, u32[]{:S(2)}) collective-permute-start(f32[1,32,128]{2,1,0:T(8,128)S(1)} %get-tuple-element.152), channel_id=1, source_target_pairs={{0,1},{1,2},{2,3},{3,4},{4,5},{5,6},{6,7},{7,8},{8,9},{9,10},{10,1... | collective-permute-start | bytes 49160 | tf_op jit(solution)/shard_map/ppermute | solution.py:19
  94.8 8.0 %copy-start.56 = (s32[1,128]{1,0:T(1,128)S(1)}, s32[1,128]{1,0:T(1,128)}, u32[]{:S(2)}) copy-start(s32[1,128]{1,0:T(1,128)} %param.30) | copy-start | bytes 1540
  95.2 8.3 %collective-permute-start.8 = (f32[1,32,128]{2,1,0:T(8,128)S(1)}, f32[1,32,128]{2,1,0:T(8,128)S(1)}, u32[]{:S(2)}, u32[]{:S(2)}) collective-permute-start(f32[1,32,128]{2,1,0:T(8,128)S(1)} %get-tuple-element.146), channel_id=1, source_target_pairs={{1,0},{2,1},{3,2},{4,3},{5,4},{6,5},{7,6},{8,7},{9,8},{10,9},{11,1... | collective-permute-start | bytes 49160 | tf_op jit(solution)/shard_map/ppermute | solution.py:21
  97.1 6.6 %collective-permute-start.9 = (f32[1,32,128]{2,1,0:T(8,128)S(1)}, f32[1,32,128]{2,1,0:T(8,128)S(1)}, u32[]{:S(2)}, u32[]{:S(2)}) collective-permute-start(f32[1,32,128]{2,1,0:T(8,128)S(1)} %get-tuple-element.145), channel_id=1, source_target_pairs={{0,1},{1,2},{2,3},{3,4},{4,5},{5,6},{6,7},{7,8},{8,9},{9,10},{10,1... | collective-permute-start | bytes 49160 | tf_op jit(solution)/shard_map/ppermute | solution.py:19
  104.2 10.6 %collective-permute-start.10 = (f32[1,32,128]{2,1,0:T(8,128)S(1)}, f32[1,32,128]{2,1,0:T(8,128)S(1)}, u32[]{:S(2)}, u32[]{:S(2)}) collective-permute-start(f32[1,32,128]{2,1,0:T(8,128)S(1)} %get-tuple-element.144), channel_id=1, source_target_pairs={{1,0},{2,1},{3,2},{4,3},{5,4},{6,5},{7,6},{8,7},{9,8},{10,9},{11,1... | collective-permute-start | bytes 49160 | tf_op jit(solution)/shard_map/ppermute | solution.py:21
  106.1 8.7 %collective-permute-start.11 = (f32[1,32,128]{2,1,0:T(8,128)S(1)}, f32[1,32,128]{2,1,0:T(8,128)S(1)}, u32[]{:S(2)}, u32[]{:S(2)}) collective-permute-start(f32[1,32,128]{2,1,0:T(8,128)S(1)} %get-tuple-element.143), channel_id=1, source_target_pairs={{0,1},{1,2},{2,3},{3,4},{4,5},{5,6},{6,7},{7,8},{8,9},{9,10},{10,1... | collective-permute-start | bytes 49160 | tf_op jit(solution)/shard_map/ppermute | solution.py:19
  118.1 14.2 %collective-permute-start.16 = (f32[1,32,128]{2,1,0:T(8,128)S(1)}, f32[1,32,128]{2,1,0:T(8,128)S(1)}, u32[]{:S(2)}, u32[]{:S(2)}) collective-permute-start(f32[1,32,128]{2,1,0:T(8,128)S(1)} %get-tuple-element.140), channel_id=1, source_target_pairs={{1,0},{2,1},{3,2},{4,3},{5,4},{6,5},{7,6},{8,7},{9,8},{10,9},{11,1... | collective-permute-start | bytes 49160 | tf_op jit(solution)/shard_map/ppermute | solution.py:21
  120.0 12.3 %collective-permute-start.17 = (f32[1,32,128]{2,1,0:T(8,128)S(1)}, f32[1,32,128]{2,1,0:T(8,128)S(1)}, u32[]{:S(2)}, u32[]{:S(2)}) collective-permute-start(f32[1,32,128]{2,1,0:T(8,128)S(1)} %get-tuple-element.139), channel_id=1, source_target_pairs={{0,1},{1,2},{2,3},{3,4},{4,5},{5,6},{6,7},{7,8},{8,9},{9,10},{10,1... | collective-permute-start | bytes 49160 | tf_op jit(solution)/shard_map/ppermute | solution.py:19
  125.2 16.3 %collective-permute-start.12 = (f32[1,32,128]{2,1,0:T(8,128)S(1)}, f32[1,32,128]{2,1,0:T(8,128)S(1)}, u32[]{:S(2)}, u32[]{:S(2)}) collective-permute-start(f32[1,32,128]{2,1,0:T(8,128)S(1)} %get-tuple-element.142), channel_id=1, source_target_pairs={{1,0},{2,1},{3,2},{4,3},{5,4},{6,5},{7,6},{8,7},{9,8},{10,9},{11,1... | collective-permute-start | bytes 49160 | tf_op jit(solution)/shard_map/ppermute | solution.py:21
  127.1 14.4 %collective-permute-start.13 = (f32[1,32,128]{2,1,0:T(8,128)S(1)}, f32[1,32,128]{2,1,0:T(8,128)S(1)}, u32[]{:S(2)}, u32[]{:S(2)}) collective-permute-start(f32[1,32,128]{2,1,0:T(8,128)S(1)} %get-tuple-element.141), channel_id=1, source_target_pairs={{0,1},{1,2},{2,3},{3,4},{4,5},{5,6},{6,7},{7,8},{8,9},{9,10},{10,1... | collective-permute-start | bytes 49160 | tf_op jit(solution)/shard_map/ppermute | solution.py:19
  134.1 7.6 %collective-permute-start.18 = (f32[1,32,128]{2,1,0:T(8,128)S(1)}, f32[1,32,128]{2,1,0:T(8,128)S(1)}, u32[]{:S(2)}, u32[]{:S(2)}) collective-permute-start(f32[1,32,128]{2,1,0:T(8,128)S(1)} %get-tuple-element.138), channel_id=1, source_target_pairs={{1,0},{2,1},{3,2},{4,3},{5,4},{6,5},{7,6},{8,7},{9,8},{10,9},{11,1... | collective-permute-start | bytes 49160 | tf_op jit(solution)/shard_map/ppermute | solution.py:21
  136.0 6.3 %collective-permute-start.19 = (f32[1,32,128]{2,1,0:T(8,128)S(1)}, f32[1,32,128]{2,1,0:T(8,128)S(1)}, u32[]{:S(2)}, u32[]{:S(2)}) collective-permute-start(f32[1,32,128]{2,1,0:T(8,128)S(1)} %get-tuple-element.137), channel_id=1, source_target_pairs={{0,1},{1,2},{2,3},{3,4},{4,5},{5,6},{6,7},{7,8},{8,9},{9,10},{10,1... | collective-permute-start | bytes 49160 | tf_op jit(solution)/shard_map/ppermute | solution.py:19
  145.2 435.8 %all-reduce.15.cloned.1.call-start = ((), (), s32[]{:S(2)}) async-start(), calls=%async_computation | async-start | bytes 1769472 | tf_op jit(solution)/shard_map/psum | solution.py:255
  284.4 1.7 copy-start.25
  284.4 1.7 copy-start.27
  292.0 5.0 collective-permute-start.20
  293.7 5.4 collective-permute-start.21
  297.0 20.5 %copy-start.42 = (bf16[6,2,64,128]{3,2,1,0:T(8,128)(2,1)S(1)}, bf16[6,2,64,128]{3,2,1,0:T(8,128)(2,1)}, u32[]{:S(2)}) copy-start(bf16[6,2,64,128]{3,2,1,0:T(8,128)(2,1)} %copy-done.41) | copy-start | bytes 589828
  299.1 119.7 %collective-permute-start.22 = (bf16[1,4,64,128]{3,2,1,0:T(8,128)(2,1)S(1)}, bf16[1,4,64,128]{3,2,1,0:T(8,128)(2,1)S(1)}, u32[]{:S(2)}, u32[]{:S(2)}) collective-permute-start(bf16[1,4,64,128]{3,2,1,0:T(8,128)(2,1)S(1)} %get-tuple-element.129), channel_id=1, source_target_pairs={{0,1},{1,2},{2,3},{3,4},{4,5},{5,6},{6,7},{7,8},{8,9},{9,10},{10,1... | collective-permute-start | bytes 196616 | tf_op jit(solution)/shard_map/ppermute | solution.py:19
  315.5 103.3 %collective-permute-start.23 = (bf16[1,4,64,128]{3,2,1,0:T(8,128)(2,1)S(1)}, bf16[1,4,64,128]{3,2,1,0:T(8,128)(2,1)S(1)}, u32[]{:S(2)}, u32[]{:S(2)}) collective-permute-start(bf16[1,4,64,128]{3,2,1,0:T(8,128)(2,1)S(1)} %get-tuple-element.130), channel_id=1, source_target_pairs={{1,0},{2,1},{3,2},{4,3},{5,4},{6,5},{7,6},{8,7},{9,8},{10,9},{11,1... | collective-permute-start | bytes 196616 | tf_op jit(solution)/shard_map/ppermute | solution.py:21
  (36 other events, 36.2 us)
Sparse Core Ops, SparseCore 0:
  145.3 138.2 all-reduce.16
  297.1 283.8 all-reduce.14
where the time goes:
time: 592 us; the launch traced here: 590 us
  waiting for transfers between devices  299 us (51%)
  blocking collectives  134 us (23%)
  starting transfers between devices  94.6 us (16%)
  local copies, waits for them, and re-layouts  24.3 us (4%)
  between operations  18.9 us (3%)
  other arithmetic  10.4 us (2%)
  matrix products  9.01 us (2%)
    psum x1, waiting for transfers between devices, per_device(): lax.psum((kernel_part, head_part, bias_part), ('shot', 'tile'))  154 us
    unnamed x3, waiting for transfers between devices  136 us
    psum x1, blocking collectives, per_device(): lax.psum((kernel_part, head_part, bias_part), ('shot', 'tile'))  101 us
    ppermute x12, starting transfers between devices, padded_2(): lax.ppermute(tail, axis, [(i, (i + 1) % count) for i in range(ends)])  66 us
    all_gather x1, blocking collectives, per_device(): tile_speed = lax.all_gather(velocity, 'shot', axis=1, tiled=True)  32.4 us
    ppermute x12, starting transfers between devices, padded_2(): lax.ppermute(head, axis, [((i + 1) % count, i) for i in range(ends)])  28.5 us
    unnamed x128, local copies, waits for them, and re-layouts  12.5 us
  transfers between devices with their start and end apart: 26, of which 7 were waited for; matrix products, arithmetic and copies ran while one was open for 3% of the time, Pallas kernels for 0%

commit v1 on v0

v1 whole, which is shorter than its diff:
```python
import functools

import jax
import jax.numpy as jnp
from jax import lax
from jax.experimental import pallas as pl
from jax.experimental.pallas import tpu as pltpu
from jax.sharding import Mesh
from jax.sharding import PartitionSpec as P

SHOT = ("xlo", "z")
TILE = ("y", "xhi", "core")
NEAR = ("xlo", "xhi", "core")
F32 = jnp.float32
BF16 = jnp.bfloat16
courant = 0.005
speed_low = 1.5
speed_span = 3.0
ROWS = 112
NT = (((1,), (1,)), ((), ()))


def sigmoid(v):
    return 1.0 / (1.0 + jnp.exp(-v))


def split(v, parts):
    out = []
    for _ in range(parts):
        piece = v.astype(BF16)
        out.append(piece)
        v = v - piece.astype(F32)
    return out


def spread_matrix():
    coarse = lax.broadcasted_iota(jnp.int32, (64, 384), 0)
    lane = lax.broadcasted_iota(jnp.int32, (64, 384), 1)
    fine = (lane & 127) + (lane >> 7) - 1
    return jnp.where((fine >> 1) == coarse, 1.0, 0.0).astype(BF16)


Z_LINE = ((0, 0, 1), (0, 1, 1), (1, 1, 2), (1, 2, 2))


def decode_kernel(
    z_prev, own, z_next, wall, bias, head, speed_out, pre_out, logit_out, lines_out, lines, sums, row_logit
):
    spread = spread_matrix()
    for zi, ref in enumerate((z_prev, own, z_next)):
        fine = jnp.dot(ref[...].reshape(576, 64), spread, preferred_element_type=F32).astype(BF16)
        for x in range(9):
            for e in range(3):
                lines[x, 64 * e : 64 * e + 64, 128 * zi : 128 * zi + 128] = fine[
                    64 * x : 64 * x + 64, 128 * e : 128 * e + 128
                ]
        for x in range(2, 7):
            lines_out[zi, :, 128 * (x - 2) : 128 * (x - 1)] = lines[x, :, 128 * zi : 128 * zi + 128]

    def products(x, carry):
        product = jnp.dot(wall[...], lines[x], preferred_element_type=F32)
        for a in range(3):
            for zz in range(4):
                total = None
                for b in range(3):
                    zi = Z_LINE[zz][b]
                    term = product[64 * (3 * a + b) : 64 * (3 * a + b) + 64, 128 * zi : 128 * zi + 128]
                    total = term if total is None else total + term
                sums[x, 4 * a + zz] = total
        return carry

    lax.fori_loop(0, 9, products, 0)
    bias_wide = jnp.broadcast_to(bias[...], (64, 128))
    head_wide = jnp.broadcast_to(head[...], (64, 128))

    def line(r, zz):
        return (
            sums[(r - 1) // 2, zz] + sums[r // 2, 4 + zz] + sums[(r + 1) // 2, 8 + zz] + bias_wide
        )

    def logit_of(pre):
        hidden = (pre * sigmoid(pre)).astype(BF16).astype(F32)
        return jnp.sum(hidden * head_wide, axis=0, keepdims=True)

    def inner(k, carry):
        r = k + 5
        for zz in range(4):
            pre = line(r, zz)
            pre_out[k, zz] = pre
            logit = logit_of(pre)
            logit_out[pl.ds(4 * k + zz, 1), :] = logit
            if zz in (1, 2):
                row_logit[pl.ds(2 * (r - 1) + zz - 1, 1), :] = logit
        return carry

    lax.fori_loop(0, 8, inner, 0)

    def outer(k, carry):
        r = jnp.where(k < 4, k + 1, k + 9)
        for zz in (1, 2):
            row_logit[pl.ds(2 * (r - 1) + zz - 1, 1), :] = logit_of(line(r, zz))
        return carry

    lax.fori_loop(0, 8, outer, 0)
    speed = speed_low + speed_span * sigmoid(row_logit[...])
    for s in range(16):
        speed_out[s] = speed


def wave_kernel(
    place,
    source,
    pulses,
    left,
    right,
    density,
    wave_prev,
    wave_now,
    adj_next,
    adj_after,
    speeds,
    receivers,
    observed,
    send,
    buoy,
    faces,
    coef,
    speed,
    maps,
    u2,
    u3,
    u4,
    laps,
    lam4,
    lam3,
    grads,
):
    def windowed(ref, offset, first):
        def get(w):
            if w < 6:
                return left[offset + w - first]
            if w < 12:
                return ref[w - 6]
            return right[offset + w - 12]

        return get

    dens = windowed(density, 18, 0)
    u1 = windowed(wave_now.at[0], 0, 0)
    u0 = windowed(wave_prev.at[0], 6, 1)
    lam5 = windowed(adj_next.at[0], 11, 2)
    lam6 = windowed(adj_after.at[0], 15, 3)

    z_at = lax.broadcasted_iota(jnp.int32, (32, 128), 0)
    y_at = lax.broadcasted_iota(jnp.int32, (32, 128), 1)
    cell = z_at * 128 + y_at
    z_top, z_bottom, y_top, y_bottom = z_at < 31, z_at > 0, y_at < 127, y_at > 0

    def shifts(f):
        return (
            jnp.where(z_top, pltpu.roll(f, 31, 0), 0.0),
            jnp.where(z_bottom, pltpu.roll(f, 1, 0), 0.0),
            jnp.where(y_top, pltpu.roll(f, 127, 1), 0.0),
            jnp.where(y_bottom, pltpu.roll(f, 1, 1), 0.0),
        )

    tile = place[0]
    local = receivers[...] - (tile * 6 - 3) * 4096
    at_row = lax.broadcasted_iota(jnp.int32, (384, 128), 0) == (local >> 7)
    at_y = lax.broadcasted_iota(jnp.int32, (128, 128), 0) == (local & 127)
    picks = [jnp.where(at_y, 1.0, 0.0).astype(BF16)]
    for n in range(3):
        for piece in split(observed[0, n : n + 1, :], 3):
            picks.append(jnp.where(at_y, piece.astype(F32), 0.0).astype(BF16))
    maps[...] = lax.dot_general(
        jnp.where(at_row, 1.0, 0.0).astype(BF16),
        jnp.concatenate(picks, axis=0),
        NT,
        preferred_element_type=F32,
    )

    for w in range(18):
        d = dens(w)
        buoy[w] = jnp.where(d > 0.0, 1.0 / d, 0.0)
    for w in range(1, 17):
        centre = buoy[w]
        inside = jnp.where(centre > 0.0, 0.5, 0.0)
        for i, beside in enumerate((buoy[w + 1], buoy[w - 1]) + shifts(centre)):
            faces[i, w] = inside * (centre + beside)
        for j in range(2):
            speed[w, pl.ds(j, 16, 2), :] = speeds[pl.ds(2 * (w - 1) + j, 16, 32), :]
        v = speed[w]
        coef[w] = courant * v * v * dens(w)

    def laplace(f, w):
        centre = f(w)
        total = None
        for i, beside in enumerate((f(w + 1), f(w - 1)) + shifts(centre)):
            term = faces[i, w] * (beside - centre)
            total = term if total is None else total + term
        return total

    source_cell = source[0] - (tile * 6 - 6) * 4096

    def forward(f, before, n, rows, out):
        for w in rows:
            lap = laplace(f, w)
            if 5 <= w <= 12:
                laps[n, w - 5] = lap
            pulse = jnp.where(cell == source_cell - w * 4096, pulses[0, n], 0.0)
            out[w] = 2.0 * f(w) - before(w) + coef[w] * lap + pulse

    def row_of(ref):
        return lambda w: ref[w]

    forward(u1, u0, 0, range(1, 17), u2)
    forward(row_of(u2), u1, 1, range(2, 16), u3)
    forward(row_of(u3), row_of(u2), 2, range(3, 15), u4)

    def residual(u, n, w):
        at = slice(32 * (w - 3), 32 * (w - 2))
        count = maps[at, 0:128]
        records = [maps[at, 128 * i : 128 * i + 128] for i in range(1 + 3 * n, 4 + 3 * n)]
        return count * u[w] - (records[0] + records[1] + records[2])

    def backward(f, before, u, n, rows, out):
        for w in rows:
            lap = laplace(lambda v: coef[v] * f(v), w)
            out[w] = 2.0 * f(w) - before(w) + lap + residual(u, n, w)

    backward(lam5, lam6, u4, 2, range(3, 15), lam4)
    backward(row_of(lam4), lam5, u3, 1, range(4, 14), lam3)
    grads[...] = jnp.zeros_like(grads)
    for w in range(5, 13):
        lap4 = laplace(row_of(u4), w)
        lap = laplace(lambda v: coef[v] * lam3[v], w)
        lam2 = 2.0 * lam3[w] - lam4[w] + lap + residual(u2, 0, w)
        total = lam5(w) * lap4 + lam4[w] * laps[2, w - 5] + lam3[w] * laps[1, w - 5] + lam2 * laps[0, w - 5]
        grads[w - 5, 8:40, :] = total * (2.0 * courant * speed[w] * dens(w))
    for x in range(8):
        for zz in range(4):
            send[pl.ds(4 * x + zz, 16, 32), :] = grads[x, pl.ds(7 + zz, 16, 2), :]


def backward_kernel(
    received, logits, pre_act, lines, head, folded, latent_out, parts_out, low, low_wide, terms, logit_grads
):
    total = received[0]
    for s in range(1, 16):
        total = total + received[s]
    squash = sigmoid(logits[...])
    logit_grads[...] = total * speed_span * squash * (1.0 - squash)
    head_wide = jnp.broadcast_to(head[...], (64, 128))

    def grad_line(x, zz, sums):
        grad = logit_grads[pl.ds(4 * x + zz, 1), :]
        pre = pre_act[x, zz]
        gate = sigmoid(pre)
        pre_grad = grad * head_wide * (gate * (1.0 + pre * (1.0 - gate)))
        rounded = pre_grad.astype(BF16)
        low[x, zz] = rounded
        if sums is not None:
            px = (x - 1) % 2
            low_wide[2 * px + zz - 1, :, 64 * (x - 1 - px) : 64 * (x + 1 - px)] = rounded
            hidden = (pre * gate).astype(BF16).astype(F32)
            return sums[0] + hidden * grad, sums[1] + pre_grad
        return None

    def owned_rows(x, sums):
        grad_line(x, 0, None)
        grad_line(x, 3, None)
        for zz in (1, 2):
            sums = grad_line(x, zz, sums)
        return sums

    for zz in range(4):
        grad_line(0, zz, None)
        grad_line(7, zz, None)
    zero = jnp.zeros((64, 128), F32)
    sums = (zero, zero)
    for x in range(1, 7):
        sums = owned_rows(x, sums)
    head_sum, bias_sum = sums

    ones = jnp.ones((8, 128), BF16)
    row = None
    for piece in split(jnp.concatenate([head_sum, bias_sum], axis=0), 3):
        term = lax.dot_general(ones, piece, NT, preferred_element_type=F32)
        row = term if row is None else row + term
    parts_out[864:872, :] = row
    parts_out[872:896, :] = jnp.zeros((24, 128), F32)

    parities = {-1: (0,), 0: (0, 1), 1: (1,)}
    found = {}
    for dx in (-1, 0, 1):
        for dz in (-1, 0, 1):
            combos = [(px, pz) for px in parities[dx] for pz in parities[dz]]
            if len(combos) == 2 and dx == 0:
                grads = jnp.concatenate([low_wide[2 * px + pz] for px, pz in combos], axis=0)
            else:
                first = 2 * combos[0][0] + combos[0][1]
                grads = low_wide[first : first + len(combos)].reshape(64 * len(combos), 384)
            beside = lines[1 + dz, :, 128 * (1 + dx) : 128 * (4 + dx)]
            product = lax.dot_general(grads, beside, NT, preferred_element_type=F32)
            for i, (px, pz) in enumerate(combos):
                found[dx, px, dz, pz] = at = len(found)
                terms[at] = product[64 * i : 64 * i + 64]
    pairs = {-1: ((-1, 0), (0, 1)), 0: ((0, 0), (0, 1)), 1: ((0, 0), (1, 1))}
    for a in (-1, 0, 1):
        for b in (-1, 0, 1):
            tap = None
            for dx, px in pairs[a]:
                for dz, pz in pairs[b]:
                    term = terms[found[dx, px, dz, pz]]
                    tap = term if tap is None else tap + term
            at = 96 * (3 * (a + 1) + b + 1)
            parts_out[at : at + 64, :] = tap[:, :128]
            parts_out[at + 64 : at + 96, :] = jnp.concatenate([tap[:32, 128:], tap[32:, 128:]], axis=1)

    stacked = []
    for x in range(3):
        around = low[2 * x : 2 * x + 4].reshape(1024, 128)
        product = jnp.dot(folded[...], around, preferred_element_type=F32)
        both = product[:192] + product[192:]
        stacked.append(jnp.concatenate([both[64 * e : 64 * e + 64] for e in range(3)], axis=1))
    stacked = jnp.concatenate(stacked, axis=0)
    spread = spread_matrix()
    result = None
    for piece in split(stacked, 2):
        term = lax.dot_general(piece, spread, NT, preferred_element_type=F32)
        result = term if result is None else result + term
    for x in range(3):
        latent_out[x, 0] = result[64 * x : 64 * x + 64]


def sum_kernel(received, out):
    total = received[0]
    for s in range(1, 8):
        total = total + received[s]
    for s in range(8):
        out[s] = total


def unpack_kernel(rows, kernel_out, head_out, bias_out):
    for tap in range(9):
        at = 96 * tap
        pair = rows[at : at + 64, :]
        kernel_out[3 * tap] = pair[:, :64]
        kernel_out[3 * tap + 1] = pair[:, 64:]
        last = rows[at + 64 : at + 96, :]
        kernel_out[3 * tap + 2, 0:32] = last[:, :64]
        kernel_out[3 * tap + 2, 32:64] = last[:, 64:]
    row = rows[864:865, :]
    head_out[...] = row[:, :64]
    bias_out[...] = row[:, 64:]


def shape(dims, dtype=F32):
    return jax.ShapeDtypeStruct(dims, dtype)


VMEM = pl.BlockSpec(memory_space=pltpu.VMEM)
SMEM = pl.BlockSpec(memory_space=pltpu.SMEM)


def call(kernel, out_shape, in_specs, scratch=(), megabytes=8):
    outs = out_shape if isinstance(out_shape, tuple) else (out_shape,)
    specs = tuple(VMEM for _ in outs)
    return pl.pallas_call(
        kernel,
        out_shape=out_shape,
        in_specs=list(in_specs),
        out_specs=specs if isinstance(out_shape, tuple) else VMEM,
        scratch_shapes=list(scratch),
        compiler_params=pltpu.CompilerParams(vmem_limit_bytes=megabytes << 20),
    )


decode = call(
    decode_kernel,
    (
        shape((16, 32, 128)),
        shape((8, 4, 64, 128)),
        shape((32, 128)),
        shape((3, 192, 640), BF16),
    ),
    [VMEM] * 6,
    [
        pltpu.VMEM((9, 192, 384), BF16),
        pltpu.VMEM((9, 12, 64, 128), F32),
        pltpu.VMEM((32, 128), F32),
    ],
    32,
)
FIELD = pltpu.VMEM((18, 32, 128), F32)
waves = call(
    wave_kernel,
    shape((512, 128)),
    [SMEM] * 3 + [VMEM] * 10,
    [
        FIELD,
        pltpu.VMEM((6, 18, 32, 128), F32),
        FIELD,
        FIELD,
        pltpu.VMEM((384, 1280), F32),
        FIELD,
        FIELD,
        FIELD,
        pltpu.VMEM((3, 8, 32, 128), F32),
        FIELD,
        FIELD,
        pltpu.VMEM((8, 48, 128), F32),
    ],
    32,
)
backward = call(
    backward_kernel,
    (shape((3, 1, 64, 64)), shape((896, 128))),
    [VMEM] * 6,
    [
        pltpu.VMEM((8, 4, 64, 128), BF16),
        pltpu.VMEM((4, 64, 384), BF16),
        pltpu.VMEM((16, 64, 192), F32),
        pltpu.VMEM((32, 128), F32),
    ],
    32,
)


def shifted(block, axes, size):
    low = lax.ppermute(block[0], axes, [(i, i + 1) for i in range(size - 1)])
    high = lax.ppermute(block[1], axes, [(i + 1, i) for i in range(size - 1)])
    return low, high


def folded_taps(kernel):
    taps = kernel.astype(F32).reshape(3, 3, 3, 64, 64)
    taps = jnp.stack([taps[2], taps[1] + taps[2], taps[0] + taps[1], taps[0]])
    taps = jnp.stack([taps[:, 2], taps[:, 1] + taps[:, 2], taps[:, 0] + taps[:, 1], taps[:, 0]], axis=1)
    table = jnp.transpose(taps, (2, 4, 0, 1, 3)).reshape(192, 1024)
    high = lax.reduce_precision(table, 8, 7)
    return jnp.concatenate([high, table - high], axis=0).astype(BF16)


def per_device(
    latent,
    kernel,
    conv_bias,
    head_weight,
    density,
    wave_prev,
    wave_now,
    adjoint_next,
    adjoint_after,
    source_cell,
    wavelet,
    receiver_cells,
    observed,
):
    tile = lax.axis_index(TILE).astype(jnp.int32)
    coarse = latent.reshape(3, 64, 64)
    low, high = shifted((coarse, coarse), TILE, 32)
    nine = jnp.concatenate([low, coarse, high], axis=0)
    z_prev, z_next = shifted((nine, nine), SHOT, 16)
    to_next = jnp.concatenate(
        [wave_now[0], wave_prev[0, 1:], adjoint_next[0, 2:], adjoint_after[0, 3:], density], axis=0
    )
    to_prev = jnp.concatenate(
        [wave_now[0], wave_prev[0, :5], adjoint_next[0, :4], adjoint_after[0, :3], density], axis=0
    )
    left, right = shifted((to_next, to_prev), TILE, 32)

    wall = jnp.transpose(kernel.reshape(9, 3, 64, 64), (0, 2, 1, 3)).reshape(576, 192)
    folded = folded_taps(kernel)
    head = head_weight.astype(F32).reshape(64, 1)
    speed, pre_act, logits, lines = decode(z_prev, nine, z_next, wall, conv_bias.reshape(64, 1), head)
    speeds = lax.all_to_all(speed, SHOT, 0, 0, tiled=True)
    strips = waves(
        tile.reshape(1),
        source_cell,
        wavelet,
        left,
        right,
        density,
        wave_prev,
        wave_now,
        adjoint_next,
        adjoint_after,
        speeds.reshape(512, 128),
        receiver_cells,
        observed,
    )
    received = lax.all_to_all(strips.reshape(16, 32, 128), SHOT, 0, 0, tiled=True)
    latent_grad, parts = backward(received, logits, pre_act, lines, head, folded)

    add = call(sum_kernel, shape((8, ROWS, 128)), [VMEM], (), 8)
    chunks = parts.reshape(8, ROWS, 128)
    for axes in (NEAR, "y", "z"):
        chunks = add(lax.all_to_all(chunks, axes, 0, 0, tiled=True))
    whole = lax.all_to_all(chunks, NEAR, 0, 0, tiled=True)
    kernel_grad, head_grad, bias_grad = call(
        unpack_kernel,
        (shape((27, 64, 64)), shape((1, 64)), shape((1, 64))),
        [VMEM],
        (),
        8,
    )(whole.reshape(896, 128))
    return latent_grad, kernel_grad, head_grad.reshape(64), bias_grad.reshape(64)


def solution(mesh):
    fine_mesh = Mesh(mesh.devices.reshape(2, 8, 8, 2, 2), ("xlo", "z", "y", "xhi", "core"))
    return jax.shard_map(
        per_device,
        mesh=fine_mesh,
        in_specs=(
            P(TILE, SHOT, None, None),
            P(),
            P(),
            P(),
            P(TILE, None, None),
            P(SHOT, TILE, None, None),
            P(SHOT, TILE, None, None),
            P(SHOT, TILE, None, None),
            P(SHOT, TILE, None, None),
            P(SHOT),
            P(SHOT, None),
            P(SHOT, None),
            P(SHOT, None, None),
        ),
        out_specs=(P(TILE, SHOT, None, None), P(), P(), P()),
        check_vma=False,
    )
```

time: 592 us -> 155 us (0.26)
  waiting for transfers between devices: 299 us -> 9.9 us
  blocking collectives: 134 us -> 70.7 us
  starting transfers between devices: 94.6 us -> 35.8 us
  between operations: 18.9 us -> 1.57 us
  Pallas kernels: 0 us -> 13 us
  matrix products: 9.01 us -> 0 us
  local copies, waits for them, and re-layouts: 24.3 us -> 16.3 us
    psum x1 -> x0, waiting for transfers between devices: 154 us -> none  [per_device(): lax.psum((kernel_part, head_part, bias_part), ('shot', 'tile'))]
    unnamed x3 -> x0, waiting for transfers between devices: 136 us -> none
    psum x1 -> x0, blocking collectives: 101 us -> none  [per_device(): lax.psum((kernel_part, head_part, bias_part), ('shot', 'tile'))]
    ppermute x24 -> x6, starting transfers between devices: 94.5 us -> 20.5 us  [the longest x3 13.2 us: shifted(): low = lax.ppermute(block[0], axes, [(i, i + 1) for i in range(size - 1)])]
    all_to_all x0 -> x4, blocking collectives: none -> 70.7 us  [the longest x3 54.8 us: per_device(): chunks = add(lax.all_to_all(chunks, axes, 0, 0, tiled=True))]
    all_gather x1 -> x0, blocking collectives: 32.4 us -> none  [per_device(): tile_speed = lax.all_gather(velocity, 'shot', axis=1, tiled=True)]
    all_to_all x0 -> x2, starting transfers between devices: none -> 15.3 us  [the longest x1 11.1 us: per_device(): speeds = lax.all_to_all(speed, SHOT, 0, 0, tiled=True)]
    pallas_call x0 -> x7, Pallas kernels: none -> 13 us  [the longest x1 5.44 us: per_device(): decode(z_prev, nine, z_next, wall, conv_bias.reshape(64, 1), head)]
  transfers between devices with their start and end apart: 26 -> 8, of which waited for: 7 -> 3; matrix products, arithmetic and copies ran while one was open for 3% -> 15% of each run, Pallas kernels for 0% -> 4%
where the time goes in v1:
time: 155 us; the launch traced here: 154 us
  blocking collectives  70.7 us (46%)
  starting transfers between devices  35.8 us (23%)
  local copies, waits for them, and re-layouts  16.3 us (11%)
  Pallas kernels  13 us (8%)
  waiting for transfers between devices  9.9 us (6%)
  other arithmetic  6.92 us (4%)
  between operations  1.57 us (1%)
    all_to_all x3, blocking collectives, per_device(): chunks = add(lax.all_to_all(chunks, axes, 0, 0, tiled=True))  54.8 us
    all_to_all x1, blocking collectives, per_device(): whole = lax.all_to_all(chunks, NEAR, 0, 0, tiled=True)  15.9 us
    ppermute x3, starting transfers between devices, shifted(): low = lax.ppermute(block[0], axes, [(i, i + 1) for i in range(size - 1)])  13.2 us
    all_to_all x1, starting transfers between devices, per_device(): speeds = lax.all_to_all(speed, SHOT, 0, 0, tiled=True)  11.1 us
    unnamed x31, local copies, waits for them, and re-layouts  8.64 us
    ppermute x3, starting transfers between devices, shifted(): high = lax.ppermute(block[1], axes, [(i + 1, i) for i in range(size - 1)])  7.25 us
    pallas_call x1, Pallas kernels, per_device(): decode(z_prev, nine, z_next, wall, conv_bias.reshape(64, 1), head)  5.44 us
    ppermute x3, waiting for transfers between devices, shifted(): high = lax.ppermute(block[1], axes, [(i + 1, i) for i in range(size - 1)])  4.25 us
  transfers between devices with their start and end apart: 8, of which 3 were waited for; matrix products, arithmetic and copies ran while one was open for 15% of the time, Pallas kernels for 4%

profile of v1, /device:TPU:1, one launch (start us, length us, event | category | flops | bytes accessed | tf_op | source)
XLA Modules:
  0.0 154.1 jit_solution(1817668106222749493)
XLA Ops:
  0.7 6.2 %collective-permute-start.2 = (bf16[3,64,64]{2,1,0:T(8,128)(2,1)}, bf16[3,64,64]{2,1,0:T(8,128)(2,1)S(1)}, u32[]{:S(2)}, u32[]{:S(2)}) collective-permute-start(bf16[3,64,64]{2,1,0:T(8,128)(2,1)} %bitcast.46), channel_id=1, source_target_pairs={{0,1},{1,2},{2,3},{3,4},{4,5},{5,6},{6,7},{7,8},{8,9},{9,10},{10,1... | collective-permute-start | bytes 73736 | tf_op jit(solution)/shard_map/ppermute | solution.py:431
  6.8 4.0 %collective-permute-start.3 = (bf16[3,64,64]{2,1,0:T(8,128)(2,1)}, bf16[3,64,64]{2,1,0:T(8,128)(2,1)S(1)}, u32[]{:S(2)}, u32[]{:S(2)}) collective-permute-start(bf16[3,64,64]{2,1,0:T(8,128)(2,1)} %bitcast.47), channel_id=1, source_target_pairs={{1,0},{2,1},{3,2},{4,3},{5,4},{6,5},{7,6},{8,7},{9,8},{10,9},{11,1... | collective-permute-start | bytes 73736 | tf_op jit(solution)/shard_map/ppermute | solution.py:432
  10.9 1.5 %bitcast_dynamic-update-slice_fusion.1 = f32[24,32,128]{2,1,0:T(8,128)} fusion(f32[1,6,32,128]{3,2,1,0:T(8,128)} %wave_now.1), kind=kLoop, calls=%fused_computation.11 | loop fusion | bytes 196608
  12.4 1.8 %copy.48 = f32[24,32,128]{2,1,0:T(8,128)} copy(f32[24,32,128]{2,1,0:T(8,128)} %bitcast_dynamic-update-slice_fusion.1) | data formatting | bytes 786432
  14.2 1.5 bitcast_dynamic-update-slice_fusion.3
  15.7 1.5 bitcast_dynamic-update-slice_fusion.2
  17.3 1.6 %bitcast_dynamic-update-slice_fusion.4 = (f32[24,32,128]{2,1,0:T(8,128)}, f32[24,32,128]{2,1,0:T(8,128)}) fusion(f32[24,32,128]{2,1,0:T(8,128)} %bitcast_dynamic-update-slice_fusion.2, f32[1,6,32,128]{3,2,1,0:T(8,128)} %adj_next.1, f32[24,32,128]{2,1,0:T(8,128)} %bitcast_dynamic-update-slice_fusion.3), kind=kLoop, calls=%fused_computation.14 | loop fusion | bytes 262144
  18.8 0.6 bitcast_dynamic-update-slice_fusion.6
  19.5 0.7 constant_dynamic-update-slice_fusion.1
  20.2 3.0 %collective-permute-start = (f32[24,32,128]{2,1,0:T(8,128)}, f32[24,32,128]{2,1,0:T(8,128)S(1)}, u32[]{:S(2)}, u32[]{:S(2)}) collective-permute-start(f32[24,32,128]{2,1,0:T(8,128)} %get-tuple-element.34), channel_id=1, source_target_pairs={{0,1},{1,2},{2,3},{3,4},{4,5},{5,6},{6,7},{7,8},{8,9},{9,10},{10,1... | collective-permute-start | bytes 1179656 | tf_op jit(solution)/shard_map/ppermute | solution.py:431
  23.2 0.0 copy-start.10
  23.2 1.9 %collective-permute-start.1 = (f32[24,32,128]{2,1,0:T(8,128)}, f32[24,32,128]{2,1,0:T(8,128)}, u32[]{:S(2)}, u32[]{:S(2)}) collective-permute-start(f32[24,32,128]{2,1,0:T(8,128)} %get-tuple-element.33), channel_id=1, source_target_pairs={{1,0},{2,1},{3,2},{4,3},{5,4},{6,5},{7,6},{8,7},{9,8},{10,9},{11,1... | collective-permute-start | bytes 1179656 | tf_op jit(solution)/shard_map/ppermute | solution.py:432
  25.1 0.9 fusion.2
  26.1 0.0 collective-permute-done.2
  26.1 4.0 %collective-permute-start.4 = (bf16[9,64,64]{2,1,0:T(8,128)(2,1)S(1)}, bf16[9,64,64]{2,1,0:T(8,128)(2,1)S(1)}, u32[]{:S(2)}, u32[]{:S(2)}) collective-permute-start(bf16[9,64,64]{2,1,0:T(8,128)(2,1)S(1)} %pad_maximum_fusion.2.own), channel_id=1, source_target_pairs={{0,32},{32,64},{64,96},{96,128},{128,160},{160,192},{192,224},{224... | collective-permute-start | bytes 221192 | tf_op jit(solution)/shard_map/ppermute | solution.py:431
  30.1 1.3 collective-permute-start.5
  31.5 0.1 copy.41.head
  31.6 0.4 copy.46
  32.0 0.4 reshape.93.wall
  32.3 0.0 copy-start.9
  32.3 0.1 copy.40.bias
  32.4 4.2 %collective-permute-done.5.z_next = bf16[9,64,64]{2,1,0:T(8,128)(2,1)S(1)} collective-permute-done((bf16[9,64,64]{2,1,0:T(8,128)(2,1)S(1)}, bf16[9,64,64]{2,1,0:T(8,128)(2,1)S(1)}, u32[]{:S(2)}, u32[]{:S(2)}) %collective-permute-start.5) | collective-permute-done | bytes 73760 | tf_op jit(solution)/shard_map/ppermute | solution.py:432
  36.7 5.4 %shard_map.156 = (f32[16,32,128]{2,1,0:T(8,128)}, f32[8,4,64,128]{3,2,1,0:T(8,128)S(1)}, f32[32,128]{1,0:T(8,128)S(1)}, bf16[3,192,640]{2,1,0:T(8,128)(2,1)S(1)}) custom-call(bf16[9,64,64]{2,1,0:T(8,128)(2,1)S(1)} %collective-permute-done.4.z_prev, bf16[9,64,64]{2,1,0:T(8,128)(2,1)S(1)} %pad_maximum_fusion.2.own, ...), custom_call_target="tpu_custom_call" | custom-call | tf_op jit(solution)/shard_map/pallas_call | solution.py:476
  42.1 11.1 %all-to-all-start = ((f32[16,32,128]{2,1,0:T(8,128)}), f32[16,32,128]{2,1,0:T(8,128)S(1)}, u32[]{:S(2)}, u32[]{:S(2)}) async-start(f32[16,32,128]{2,1,0:T(8,128)} %get-tuple-element.13), calls=%async_computation | async-start | bytes 524288 | tf_op jit(solution)/shard_map/all_to_all | solution.py:477
  53.2 1.8 %fusion.3 = (f32[1,3,3,64,64]{4,3,2,1,0:T(8,128)S(1)}, f32[1,3,3,64,64]{4,3,2,1,0:T(8,128)}) fusion(f32[1,3,3,64,64]{4,3,2,1,0:T(8,128)} %bitcast.45, f32[1,3,3,64,64]{4,3,2,1,0:T(8,128)S(1)} %bitcast.40, f32[1,3,3,64,64]{4,3,2,1,0:T(8,128)} %bitcast.42), kind=kLoop, calls=%fused_computation.23 | loop fusion | flops 73728 | bytes 737280 | tf_op jit(solution)/shard_map/add | solution.py:438
  55.7 1.2 pad_maximum_fusion
  56.9 0.0 copy-start
  56.9 0.0 copy-start.1
  56.9 0.0 copy-start.2
  56.9 0.0 copy-start.5
  56.9 0.0 copy-start.6
  56.9 1.1 fusion.1
  58.1 0.0 collective-permute-done.1.right
  58.1 3.8 %all-to-all-done = f32[16,32,128]{2,1,0:T(8,128)S(1)} async-done(((f32[16,32,128]{2,1,0:T(8,128)}), f32[16,32,128]{2,1,0:T(8,128)S(1)}, u32[]{:S(2)}, u32[]{:S(2)}) %all-to-all-start) | async-done | bytes 262176 | tf_op jit(solution)/shard_map/all_to_all | solution.py:477
  61.9 3.8 %shard_map.157 = f32[512,128]{1,0:T(8,128)} custom-call(s32[1]{0:T(128)} %bitcast.place, s32[1]{0:T(128)S(6)} %copy.55.source, f32[1,3]{1,0:T(1,128)S(1)} %copy-done.5, f32[24,32,128]{2,1,0:T(8,128)S(1)} %collective-permute-done.left, f32[24,32,128]{2,1,0:T(8,128)} %collective-permute-done.1.right, f32[6,32,128]{2,1,0:T(8,128)S(1)} %copy-done.4, ...), custom_call_target="tpu_custom_call" | custom-call | tf_op jit(solution)/shard_map/pallas_call | solution.py:478
  65.7 4.2 %all-to-all-start.1 = ((f32[16,32,128]{2,1,0:T(8,128)}), f32[16,32,128]{2,1,0:T(8,128)S(1)}, u32[]{:S(2)}, u32[]{:S(2)}) async-start(f32[16,32,128]{2,1,0:T(8,128)} %bitcast.14), calls=%async_computation.1 | async-start | bytes 524288 | tf_op jit(solution)/shard_map/all_to_all | solution.py:493
  69.9 2.6 %maximum_bitcast_fusion = f32[3,64,4,4,64]{1,4,0,3,2:T(8,128)} fusion(f32[4,1,3,64,64]{4,3,2,1,0:T(8,128)} %get-tuple-element.24, f32[4,1,3,64,64]{4,3,2,1,0:T(8,128)} %get-tuple-element.23, f32[4,1,3,64,64]{4,3,2,1,0:T(8,128)} %get-tuple-element.25, f32[4,1,3,64,64]{4,3,2,1,0:T(8,128)S(1)} %get-tuple-element.22), kind=kLoop, calls=%fused_computation | loop fusion | flops 589824 | bytes 1572864 | tf_op jit(solution)/shard_map/transpose | solution.py:440
  72.5 2.6 %copy.43 = f32[3,64,4,4,64]{4,3,2,1,0:T(4,128)} copy(f32[3,64,4,4,64]{1,4,0,3,2:T(8,128)} %maximum_bitcast_fusion) | data formatting | bytes 1572864 | tf_op jit(solution)/shard_map/transpose | solution.py:440
  75.1 2.5 %reshape.99 = f32[192,1024]{1,0:T(8,128)S(1)} reshape(f32[3,64,4,4,64]{4,3,2,1,0:T(4,128)} %copy.43) | data formatting | bytes 1572864 | tf_op jit(solution)/shard_map/reshape | solution.py:440
  77.6 0.1 reduce-precision_convert_fusion
  77.7 0.1 pad_maximum_fusion.1.folded
  77.8 1.8 %all-to-all-done.1.received = f32[16,32,128]{2,1,0:T(8,128)S(1)} async-done(((f32[16,32,128]{2,1,0:T(8,128)}), f32[16,32,128]{2,1,0:T(8,128)S(1)}, u32[]{:S(2)}, u32[]{:S(2)}) %all-to-all-start.1) | async-done | bytes 262176 | tf_op jit(solution)/shard_map/all_to_all | solution.py:493
  79.6 2.5 %shard_map.158 = (f32[3,1,64,64]{3,2,1,0:T(8,128)}, f32[896,128]{1,0:T(8,128)S(1)}) custom-call(f32[16,32,128]{2,1,0:T(8,128)S(1)} %all-to-all-done.1.received, f32[32,128]{1,0:T(8,128)S(1)} %get-tuple-element.14.logits, f32[8,4,64,128]{3,2,1,0:T(8,128)S(1)} %get-tuple-element.15.pre_act, bf16[3,192,640]{2,1,0:T(8,128)(2,1)S(1)} %get-tuple-element.16.lines, ...), custom_call_target="tpu_custom_call" | custom-call | tf_op jit(solution)/shard_map/pallas_call | solution.py:494
  82.2 14.5 %all_to_all.30.received = f32[8,112,128]{2,1,0:T(8,128)S(1)} all-to-all(f32[8,112,128]{2,1,0:T(8,128)S(1)} %bitcast.38), channel_id=1, replica_groups=mesh['xlo'=2,'z'=8,'y'=8,'xhi'=2,'core'=2] {'xlo','xhi','core'}, dimensions={0} | all-to-all | bytes 917504 | tf_op jit(solution)/shard_map/all_to_all | solution.py:499
  96.7 22.4 %all_to_all.31.received = f32[8,112,128]{2,1,0:T(8,128)S(1)} all-to-all(f32[8,112,128]{2,1,0:T(8,128)S(1)} %shard_map.159), channel_id=1, replica_groups=mesh['xlo'=2,'z'=8,'y'=8,'xhi'=2,'core'=2] {'y'}, dimensions={0} | all-to-all | bytes 917504 | tf_op jit(solution)/shard_map/all_to_all | solution.py:499
  119.1 17.9 %all_to_all.32.received = f32[8,112,128]{2,1,0:T(8,128)S(1)} all-to-all(f32[8,112,128]{2,1,0:T(8,128)S(1)} %shard_map.160), channel_id=1, replica_groups=mesh['xlo'=2,'z'=8,'y'=8,'xhi'=2,'core'=2] {'z'}, dimensions={0} | all-to-all | bytes 917504 | tf_op jit(solution)/shard_map/all_to_all | solution.py:499
  137.1 15.9 %all_to_all.33 = f32[8,112,128]{2,1,0:T(8,128)S(1)} all-to-all(f32[8,112,128]{2,1,0:T(8,128)S(1)} %shard_map.161), channel_id=1, replica_groups=mesh['xlo'=2,'z'=8,'y'=8,'xhi'=2,'core'=2] {'xlo','xhi','core'}, dimensions={0} | all-to-all | bytes 917504 | tf_op jit(solution)/shard_map/all_to_all | solution.py:500
  153.0 1.1 shard_map.162
  (26 shorter events, 0.2 us)
Async XLA Ops:
  0.6 18.2 %copy-start.3 = (f32[1,6,32,128]{3,2,1,0:T(8,128)S(1)}, f32[1,6,32,128]{3,2,1,0:T(8,128)}, u32[]{:S(2)}) copy-start(f32[1,6,32,128]{3,2,1,0:T(8,128)} %adj_after.1) | copy-start | bytes 294916
  0.6 18.8 %copy-start.4 = (f32[6,32,128]{2,1,0:T(8,128)S(1)}, f32[6,32,128]{2,1,0:T(8,128)}, u32[]{:S(2)}) copy-start(f32[6,32,128]{2,1,0:T(8,128)} %density.1) | copy-start | bytes 294916
  0.7 24.5 %copy-start.7 = (bf16[27,64,64]{2,1,0:T(8,128)(2,1)S(1)}, bf16[27,64,64]{2,1,0:T(8,128)(2,1)}, u32[]{:S(2)}) copy-start(bf16[27,64,64]{2,1,0:T(8,128)(2,1)} %param.14) | copy-start | bytes 663556
  0.7 25.4 %collective-permute-start.2 = (bf16[3,64,64]{2,1,0:T(8,128)(2,1)}, bf16[3,64,64]{2,1,0:T(8,128)(2,1)S(1)}, u32[]{:S(2)}, u32[]{:S(2)}) collective-permute-start(bf16[3,64,64]{2,1,0:T(8,128)(2,1)} %bitcast.46), channel_id=1, source_target_pairs={{0,1},{1,2},{2,3},{3,4},{4,5},{5,6},{6,7},{7,8},{8,9},{9,10},{10,1... | collective-permute-start | bytes 73736 | tf_op jit(solution)/shard_map/ppermute | solution.py:431
  6.8 19.2 %collective-permute-start.3 = (bf16[3,64,64]{2,1,0:T(8,128)(2,1)}, bf16[3,64,64]{2,1,0:T(8,128)(2,1)S(1)}, u32[]{:S(2)}, u32[]{:S(2)}) collective-permute-start(bf16[3,64,64]{2,1,0:T(8,128)(2,1)} %bitcast.47), channel_id=1, source_target_pairs={{1,0},{2,1},{3,2},{4,3},{5,4},{6,5},{7,6},{8,7},{9,8},{10,9},{11,1... | collective-permute-start | bytes 73736 | tf_op jit(solution)/shard_map/ppermute | solution.py:432
  14.2 11.9 %copy-start.8 = (bf16[3,1,64,64]{3,2,1,0:T(8,128)(2,1)S(1)}, bf16[3,1,64,64]{3,2,1,0:T(8,128)(2,1)}, u32[]{:S(2)}) copy-start(bf16[3,1,64,64]{3,2,1,0:T(8,128)(2,1)} %param.13) | copy-start | bytes 73732
  14.2 17.2 %copy-start.11 = (bf16[64]{0:T(256)(128)(2,1)S(1)}, bf16[64]{0:T(256)(128)(2,1)}, u32[]{:S(2)}) copy-start(bf16[64]{0:T(256)(128)(2,1)} %param.16) | copy-start | bytes 388
  20.2 37.9 %collective-permute-start = (f32[24,32,128]{2,1,0:T(8,128)}, f32[24,32,128]{2,1,0:T(8,128)S(1)}, u32[]{:S(2)}, u32[]{:S(2)}) collective-permute-start(f32[24,32,128]{2,1,0:T(8,128)} %get-tuple-element.34), channel_id=1, source_target_pairs={{0,1},{1,2},{2,3},{3,4},{4,5},{5,6},{6,7},{7,8},{8,9},{9,10},{10,1... | collective-permute-start | bytes 1179656 | tf_op jit(solution)/shard_map/ppermute | solution.py:431
  23.2 9.1 %copy-start.10 = (f32[64]{0:T(128)S(1)}, f32[64]{0:T(128)}, u32[]{:S(2)}) copy-start(f32[64]{0:T(128)} %param.15) | copy-start | bytes 772
  23.2 34.9 %collective-permute-start.1 = (f32[24,32,128]{2,1,0:T(8,128)}, f32[24,32,128]{2,1,0:T(8,128)}, u32[]{:S(2)}, u32[]{:S(2)}) collective-permute-start(f32[24,32,128]{2,1,0:T(8,128)} %get-tuple-element.33), channel_id=1, source_target_pairs={{1,0},{2,1},{3,2},{4,3},{5,4},{6,5},{7,6},{8,7},{9,8},{10,9},{11,1... | collective-permute-start | bytes 1179656 | tf_op jit(solution)/shard_map/ppermute | solution.py:432
  26.1 6.3 %collective-permute-start.4 = (bf16[9,64,64]{2,1,0:T(8,128)(2,1)S(1)}, bf16[9,64,64]{2,1,0:T(8,128)(2,1)S(1)}, u32[]{:S(2)}, u32[]{:S(2)}) collective-permute-start(bf16[9,64,64]{2,1,0:T(8,128)(2,1)S(1)} %pad_maximum_fusion.2.own), channel_id=1, source_target_pairs={{0,32},{32,64},{64,96},{96,128},{128,160},{160,192},{192,224},{224... | collective-permute-start | bytes 221192 | tf_op jit(solution)/shard_map/ppermute | solution.py:431
  30.1 6.5 %collective-permute-start.5 = (bf16[9,64,64]{2,1,0:T(8,128)(2,1)S(1)}, bf16[9,64,64]{2,1,0:T(8,128)(2,1)S(1)}, u32[]{:S(2)}, u32[]{:S(2)}) collective-permute-start(bf16[9,64,64]{2,1,0:T(8,128)(2,1)S(1)} %pad_maximum_fusion.2.own), channel_id=1, source_target_pairs={{32,0},{64,32},{96,64},{128,96},{160,128},{192,160},{224,192},{256... | collective-permute-start | bytes 221192 | tf_op jit(solution)/shard_map/ppermute | solution.py:432
  32.3 22.8 %copy-start.9 = (f32[1,3,128]{2,0,1:T(1,128)S(1)}, f32[1,3,128]{2,0,1:T(1,128)}, u32[]{:S(2)}) copy-start(f32[1,3,128]{2,0,1:T(1,128)} %param.25) | copy-start | bytes 4612
  42.1 19.8 %all-to-all-start = ((f32[16,32,128]{2,1,0:T(8,128)}), f32[16,32,128]{2,1,0:T(8,128)S(1)}, u32[]{:S(2)}, u32[]{:S(2)}) async-start(f32[16,32,128]{2,1,0:T(8,128)} %get-tuple-element.13), calls=%async_computation | async-start | bytes 524288 | tf_op jit(solution)/shard_map/all_to_all | solution.py:477
  56.9 5.0 %copy-start = (f32[1,6,32,128]{3,2,1,0:T(8,128)S(1)}, f32[1,6,32,128]{3,2,1,0:T(8,128)}, u32[]{:S(2)}) copy-start(f32[1,6,32,128]{3,2,1,0:T(8,128)} %wave_prev.1) | copy-start | bytes 294916
  56.9 5.0 %copy-start.1 = (f32[1,6,32,128]{3,2,1,0:T(8,128)S(1)}, f32[1,6,32,128]{3,2,1,0:T(8,128)}, u32[]{:S(2)}) copy-start(f32[1,6,32,128]{3,2,1,0:T(8,128)} %adj_next.1) | copy-start | bytes 294916
  56.9 5.0 %copy-start.2 = (f32[1,6,32,128]{3,2,1,0:T(8,128)S(1)}, f32[1,6,32,128]{3,2,1,0:T(8,128)}, u32[]{:S(2)}) copy-start(f32[1,6,32,128]{3,2,1,0:T(8,128)} %wave_now.1) | copy-start | bytes 294916
  56.9 5.0 %copy-start.5 = (f32[1,3]{1,0:T(1,128)S(1)}, f32[1,3]{1,0:T(1,128)}, u32[]{:S(2)}) copy-start(f32[1,3]{1,0:T(1,128)} %pulses.1) | copy-start | bytes 40
  56.9 5.0 %copy-start.6 = (s32[1,128]{1,0:T(1,128)S(1)}, s32[1,128]{1,0:T(1,128)}, u32[]{:S(2)}) copy-start(s32[1,128]{1,0:T(1,128)} %receivers.1) | copy-start | bytes 1540
  65.7 13.9 %all-to-all-start.1 = ((f32[16,32,128]{2,1,0:T(8,128)}), f32[16,32,128]{2,1,0:T(8,128)S(1)}, u32[]{:S(2)}, u32[]{:S(2)}) async-start(f32[16,32,128]{2,1,0:T(8,128)} %bitcast.14), calls=%async_computation.1 | async-start | bytes 524288 | tf_op jit(solution)/shard_map/all_to_all | solution.py:493

commit v2 on v1

v2 whole, which is shorter than its diff:
```python
import jax
import jax.numpy as jnp
from jax import lax
from jax.experimental import pallas as pl
from jax.experimental.pallas import tpu as pltpu
from jax.sharding import Mesh
from jax.sharding import PartitionSpec as P

SHOT = ("xlo", "z")
TILE = ("y", "xhi", "core")
F32 = jnp.float32
BF16 = jnp.bfloat16
courant = 0.005
speed_low = 1.5
speed_span = 3.0
ROWS = 56
NT = (((1,), (1,)), ((), ()))


def sigmoid(v):
    return 1.0 / (1.0 + jnp.exp(-v))


def split(v, parts):
    out = []
    for _ in range(parts):
        piece = v.astype(BF16)
        out.append(piece)
        v = v - piece.astype(F32)
    return out


def spread_matrix():
    coarse = lax.broadcasted_iota(jnp.int32, (64, 384), 0)
    lane = lax.broadcasted_iota(jnp.int32, (64, 384), 1)
    fine = (lane & 127) + (lane >> 7) - 1
    return jnp.where((fine >> 1) == coarse, 1.0, 0.0).astype(BF16)


Z_LINE = ((0, 0, 1), (0, 1, 1), (1, 1, 2), (1, 2, 2))


def start_all(copies):
    for copy in copies:
        copy.start()
    return copies


def wait_all(copies):
    for copy in copies:
        copy.wait()


def prepare_kernel(
    wave_now,
    wave_prev,
    adj_next,
    adj_after,
    density,
    kernel_in,
    coarse,
    bias,
    head,
    to_next,
    to_prev,
    middle,
    wall,
    bias_wide,
    head_wide,
    kernel,
    sems,
):
    copies = [
        pltpu.make_async_copy(kernel_in, kernel, sems.at[10]),
        pltpu.make_async_copy(coarse, middle, sems.at[11]),
    ]
    fields = ((wave_now, 6), (wave_prev, 5), (adj_next, 4), (adj_after, 3), (density, 6))
    at = 0
    for i, (ref, rows) in enumerate(fields):
        field = ref if i == 4 else ref.at[0]
        here = pl.ds(at, rows)
        copies.append(pltpu.make_async_copy(field.at[pl.ds(6 - rows, rows)], to_next.at[here], sems.at[i]))
        copies.append(pltpu.make_async_copy(field.at[pl.ds(0, rows)], to_prev.at[here], sems.at[5 + i]))
        at += rows
    start_all(copies)
    bias_wide[...] = jnp.broadcast_to(bias[...], (128, 64)).T
    head_wide[...] = jnp.broadcast_to(head[...].astype(F32), (128, 64)).T
    copies[0].wait()
    for j in range(9):
        wall[64 * j : 64 * j + 64, :] = jnp.concatenate([kernel[3 * j + e] for e in range(3)], axis=1)
    wait_all(copies[1:])


def join_kernel(low, middle, high, out):
    for i, ref in enumerate((low, middle, high)):
        out[3 * i : 3 * i + 3] = ref[...]


def fold_taps(kernel, folded):
    reach = ((2,), (1, 2), (0, 1), (0,))
    for i in range(4):
        for j in range(0, 4, 2):
            blocks = []
            for jj in (j, j + 1):
                row = []
                for e in range(3):
                    total = None
                    for a in reach[i]:
                        for b in reach[jj]:
                            term = kernel[9 * a + 3 * b + e].astype(F32)
                            total = term if total is None else total + term
                    row.append(total)
                blocks.append(jnp.concatenate(row, axis=1))
            table = jnp.concatenate(blocks, axis=0).T
            high, low = split(table, 2)
            at = 64 * (4 * i + j)
            folded[0:192, at : at + 128] = high
            folded[192:384, at : at + 128] = low


def z_sums(product, rows, store):
    for a in range(3):
        for zz in rows:
            total = None
            for b in range(3):
                zi = Z_LINE[zz][b]
                term = product[64 * (3 * a + b) : 64 * (3 * a + b) + 64, 128 * zi : 128 * zi + 128]
                total = term if total is None else total + term
            store(a, zz, total)


def decode_kernel(
    z_prev, own, z_next, wall, bias, head, left, right, speed_out, lines_out, lines, sums, row_logit
):
    spread = spread_matrix()
    for zi, ref in enumerate((z_prev, own, z_next)):
        fine = jnp.dot(ref[...].reshape(576, 64), spread, preferred_element_type=F32).astype(BF16)
        for x in range(9):
            for e in range(3):
                piece = fine[64 * x : 64 * x + 64, 128 * e : 128 * e + 128]
                lines[x, 64 * e : 64 * e + 64, 128 * zi : 128 * zi + 128] = piece
                if 2 <= x <= 6:
                    lines_out[zi, 64 * e : 64 * e + 64, 128 * (x - 2) : 128 * (x - 1)] = piece

    def products(x, carry):
        product = jnp.dot(wall[...], lines[x], preferred_element_type=F32)

        def store(a, zz, total):
            sums[x, 2 * a + zz - 1] = total

        z_sums(product, (1, 2), store)
        return carry

    lax.fori_loop(0, 9, products, 0, unroll=3)

    def rows(k, carry):
        r = k + 1
        for j in range(2):
            pre = sums[(r - 1) // 2, j] + sums[r // 2, 2 + j] + sums[(r + 1) // 2, 4 + j] + bias[...]
            hidden = (pre * sigmoid(pre)).astype(BF16).astype(F32)
            row_logit[pl.ds(2 * k + j, 1), :] = jnp.sum(hidden * head[...], axis=0, keepdims=True)
        return carry

    lax.fori_loop(0, 16, rows, 0, unroll=2)
    speed = speed_low + speed_span * sigmoid(row_logit[...])
    for s in range(16):
        speed_out[s] = speed


def slopes_kernel(
    lines, wall_in, bias_in, head_in, kernel_in, after, slope_out, folded, wall, bias, head, kernel, sums, sems
):
    copies = start_all(
        [
            pltpu.make_async_copy(source, target, sems.at[i])
            for i, (source, target) in enumerate(
                ((wall_in, wall), (bias_in, bias), (head_in, head), (kernel_in, kernel))
            )
        ]
    )
    wait_all(copies)
    for x in range(5):
        columns = [lines[zi, :, 128 * x : 128 * x + 128] for zi in range(3)]
        product = jnp.dot(wall[...], jnp.concatenate(columns, axis=1), preferred_element_type=F32)

        def store(a, zz, total):
            sums[x, 4 * a + zz] = total

        z_sums(product, range(4), store)

    def rows(k, carry):
        r = k + 1
        for zz in range(4):
            pre = sums[(r - 1) // 2, zz] + sums[r // 2, 4 + zz] + sums[(r + 1) // 2, 8 + zz] + bias[...]
            gate = sigmoid(pre)
            hidden = (pre * gate).astype(BF16)
            slope_out[4 * k + zz] = head[...] * (gate * (1.0 + pre * (1.0 - gate)))
            hidden = hidden.astype(F32)
            if zz in (1, 2):
                slope_out[32 + 2 * k + zz - 1] = hidden
            logit = jnp.sum(hidden * head[...], axis=0, keepdims=True)
            slope_out[48, pl.ds(4 * k + zz, 1), :] = logit
        return carry

    lax.fori_loop(0, 8, rows, 0)
    slope_out[48, 0:32, :] = sigmoid(slope_out[48, 0:32, :])
    slope_out[48, 32:64, :] = jnp.zeros((32, 128), F32)
    fold_taps(kernel, folded)


def shifts(f):
    z_at = lax.broadcasted_iota(jnp.int32, (32, 128), 0)
    y_at = lax.broadcasted_iota(jnp.int32, (32, 128), 1)
    return (
        jnp.where(z_at < 31, pltpu.roll(f, 31, 0), 0.0),
        jnp.where(z_at > 0, pltpu.roll(f, 1, 0), 0.0),
        jnp.where(y_at < 127, pltpu.roll(f, 127, 1), 0.0),
        jnp.where(y_at > 0, pltpu.roll(f, 1, 1), 0.0),
    )


def windowed(left, own, right, field, offset, first):
    def get(w):
        if w < 6:
            return left[offset + w - first]
        if w < 12:
            return own[6 * field + w - 6]
        return right[offset + w - 12]

    return get


def records_kernel(place, receivers_in, observed_in, after, counts, receivers, observed, sems):
    wait_all(
        start_all(
            [
                pltpu.make_async_copy(receivers_in, receivers, sems.at[0]),
                pltpu.make_async_copy(observed_in, observed, sems.at[1]),
            ]
        )
    )
    local = receivers[...] - (place[0] * 6 - 3) * 4096
    at_row = lax.broadcasted_iota(jnp.int32, (384, 128), 0) == (local >> 7)
    at_y = lax.broadcasted_iota(jnp.int32, (128, 128), 0) == (local & 127)
    picks = [jnp.where(at_y, 1.0, 0.0).astype(BF16)]
    for n in range(3):
        for piece in split(observed[n], 3):
            picks.append(jnp.where(at_y, piece.astype(F32), 0.0).astype(BF16))
    maps = lax.dot_general(
        jnp.where(at_row, 1.0, 0.0).astype(BF16),
        jnp.concatenate(picks, axis=0),
        NT,
        preferred_element_type=F32,
    )
    counts[0] = maps[:, 0:128]
    for n in range(3):
        at = 128 + 384 * n
        counts[1 + n] = maps[:, at : at + 128] + maps[:, at + 128 : at + 256] + maps[:, at + 256 : at + 384]


def wave_kernel(
    place,
    source,
    pulses_in,
    left,
    right,
    wave_now,
    wave_prev,
    adj_next,
    adj_after,
    density,
    speeds,
    counts_in,
    send_out,
    own,
    counts,
    pulses,
    faces,
    buoy,
    coef,
    speed,
    u2,
    u3,
    u4,
    laps,
    lam4,
    lam3,
    grads,
    sems,
):
    fields = (wave_now.at[0], wave_prev.at[0], adj_next.at[0], adj_after.at[0], density)
    copies = start_all(
        [pltpu.make_async_copy(f, own.at[pl.ds(6 * i, 6)], sems.at[i]) for i, f in enumerate(fields)]
        + [
            pltpu.make_async_copy(pulses_in, pulses, sems.at[5]),
            pltpu.make_async_copy(counts_in, counts, sems.at[6]),
        ]
    )
    send = send_out.reshape(512, 128)
    u1 = windowed(left, own, right, 0, 0, 0)
    u0 = windowed(left, own, right, 1, 6, 1)
    lam5 = windowed(left, own, right, 2, 11, 2)
    lam6 = windowed(left, own, right, 3, 15, 3)
    dens = windowed(left, own, right, 4, 18, 0)
    cell = lax.broadcasted_iota(jnp.int32, (32, 128), 0) * 128 + lax.broadcasted_iota(
        jnp.int32, (32, 128), 1
    )

    for w in range(1, 17):
        for j in range(2):
            speed[w, pl.ds(j, 16, 2), :] = speeds[pl.ds(2 * (w - 1) + j, 16, 32), :]
    grads[...] = jnp.zeros_like(grads)
    wait_all(copies)
    for w in range(18):
        d = dens(w)
        buoy[w] = jnp.where(d > 0.0, 1.0 / d, 0.0)
    for w in range(1, 17):
        v = speed[w]
        coef[w] = courant * v * v * dens(w)
        centre = buoy[w]
        inside = jnp.where(centre > 0.0, 0.5, 0.0)
        for i, beside in enumerate((buoy[w + 1], buoy[w - 1]) + shifts(centre)):
            faces[i, w] = inside * (centre + beside)

    def laplace(f, w):
        centre = f(w)
        total = None
        for i, beside in enumerate((f(w + 1), f(w - 1)) + shifts(centre)):
            term = faces[i, w] * (beside - centre)
            total = term if total is None else total + term
        return total

    source_cell = source[0] - (place[0] * 6 - 6) * 4096

    def forward(f, before, n, rows, out):
        for w in rows:
            lap = laplace(f, w)
            if 5 <= w <= 12:
                laps[n, w - 5] = lap
            pulse = jnp.where(cell == source_cell - w * 4096, pulses[0, n], 0.0)
            out[w] = 2.0 * f(w) - before(w) + coef[w] * lap + pulse

    def row_of(ref):
        return lambda w: ref[w]

    forward(u1, u0, 0, range(1, 17), u2)
    forward(row_of(u2), u1, 1, range(2, 16), u3)
    forward(row_of(u3), row_of(u2), 2, range(3, 15), u4)

    def residual(u, n, w):
        at = slice(32 * (w - 3), 32 * (w - 2))
        return counts[0, at, :] * u[w] - counts[1 + n, at, :]

    def backward(f, before, u, n, rows, out):
        for w in rows:
            lap = laplace(lambda v: coef[v] * f(v), w)
            out[w] = 2.0 * f(w) - before(w) + lap + residual(u, n, w)

    backward(lam5, lam6, u4, 2, range(3, 15), lam4)
    backward(row_of(lam4), lam5, u3, 1, range(4, 14), lam3)
    for w in range(5, 13):
        lap4 = laplace(row_of(u4), w)
        lap = laplace(lambda v: coef[v] * lam3[v], w)
        lam2 = 2.0 * lam3[w] - lam4[w] + lap + residual(u2, 0, w)
        total = lam5(w) * lap4 + lam4[w] * laps[2, w - 5] + lam3[w] * laps[1, w - 5] + lam2 * laps[0, w - 5]
        grads[w - 5, 8:40, :] = total * (2.0 * courant * speed[w] * dens(w))
    for x in range(8):
        for zz in range(4):
            send[pl.ds(4 * x + zz, 16, 32), :] = grads[x, pl.ds(7 + zz, 16, 2), :]


def backward_kernel(
    received, slopes, lines, folded, latent_out, parts_out, low, low_wide, terms, logit_grads
):
    total = received[0]
    for s in range(1, 16):
        total = total + received[s]
    squash = slopes[48, 0:32, :]
    logit_grads[...] = total * speed_span * squash * (1.0 - squash)
    head_sum = jnp.zeros((64, 128), F32)
    bias_sum = jnp.zeros((64, 128), F32)
    for x in range(8):
        for zz in range(4):
            grad = logit_grads[4 * x + zz : 4 * x + zz + 1, :]
            pre_grad = grad * slopes[4 * x + zz]
            rounded = pre_grad.astype(BF16)
            low[x, zz] = rounded
            if 1 <= x <= 6 and 1 <= zz <= 2:
                px = (x - 1) % 2
                low_wide[2 * px + zz - 1, :, 64 * (x - 1 - px) : 64 * (x + 1 - px)] = rounded
                head_sum = head_sum + slopes[32 + 2 * x + zz - 1] * grad
                bias_sum = bias_sum + pre_grad

    ones = jnp.ones((8, 128), BF16)
    row = None
    for piece in split(jnp.concatenate([head_sum, bias_sum], axis=0), 3):
        term = lax.dot_general(ones, piece, NT, preferred_element_type=F32)
        row = term if row is None else row + term
    parts_out[864:872, :] = row
    parts_out[872:896, :] = jnp.zeros((24, 128), F32)

    parities = {-1: (0,), 0: (0, 1), 1: (1,)}
    found = {}
    for dx in (-1, 0, 1):
        for dz in (-1, 0, 1):
            combos = [(px, pz) for px in parities[dx] for pz in parities[dz]]
            if len(combos) == 2 and dx == 0:
                grads = jnp.concatenate([low_wide[2 * px + pz] for px, pz in combos], axis=0)
            else:
                first = 2 * combos[0][0] + combos[0][1]
                grads = low_wide[first : first + len(combos)].reshape(64 * len(combos), 384)
            beside = lines[1 + dz, :, 128 * (1 + dx) : 128 * (4 + dx)]
            product = lax.dot_general(grads, beside, NT, preferred_element_type=F32)
            for i, (px, pz) in enumerate(combos):
                found[dx, px, dz, pz] = at = len(found)
                terms[at] = product[64 * i : 64 * i + 64]
    pairs = {-1: ((-1, 0), (0, 1)), 0: ((0, 0), (0, 1)), 1: ((0, 0), (1, 1))}
    for a in (-1, 0, 1):
        for b in (-1, 0, 1):
            tap = None
            for dx, px in pairs[a]:
                for dz, pz in pairs[b]:
                    term = terms[found[dx, px, dz, pz]]
                    tap = term if tap is None else tap + term
            at = 96 * (3 * (a + 1) + b + 1)
            parts_out[at : at + 64, :] = tap[:, :128]
            parts_out[at + 64 : at + 96, :] = jnp.concatenate([tap[:32, 128:], tap[32:, 128:]], axis=1)

    stacked = []
    for x in range(3):
        around = low[2 * x : 2 * x + 4].reshape(1024, 128)
        product = jnp.dot(folded[...], around, preferred_element_type=F32)
        both = product[:192] + product[192:]
        stacked.append(jnp.concatenate([both[64 * e : 64 * e + 64] for e in range(3)], axis=1))
    stacked = jnp.concatenate(stacked, axis=0)
    spread = spread_matrix()
    result = None
    for piece in split(stacked, 2):
        term = lax.dot_general(piece, spread, NT, preferred_element_type=F32)
        result = term if result is None else result + term
    for x in range(3):
        latent_out[x, 0] = result[64 * x : 64 * x + 64]


def sum_kernel(received, out):
    total = received[0]
    for s in range(1, received.shape[0]):
        total = total + received[s]
    for s in range(out.shape[0]):
        out[s] = total


def unpack_kernel(rows, kernel_out, head_out, bias_out):
    for tap in range(9):
        at = 96 * tap
        pair = rows[at : at + 64, :]
        kernel_out[3 * tap] = pair[:, :64]
        kernel_out[3 * tap + 1] = pair[:, 64:]
        last = rows[at + 64 : at + 96, :]
        kernel_out[3 * tap + 2, 0:32] = last[:, :64]
        kernel_out[3 * tap + 2, 32:64] = last[:, 64:]
    row = rows[864:865, :]
    head_out[...] = row[:, :64]
    bias_out[...] = row[:, 64:]


def shape(dims, dtype=F32):
    return jax.ShapeDtypeStruct(dims, dtype)


VMEM = pl.BlockSpec(memory_space=pltpu.VMEM)
ANY = pl.BlockSpec(memory_space=pl.ANY)
HBM = pl.BlockSpec(memory_space=pltpu.HBM)
SMEM = pl.BlockSpec(memory_space=pltpu.SMEM)


def call(kernel, out_shape, in_specs, scratch=(), megabytes=8):
    outs = out_shape if isinstance(out_shape, tuple) else (out_shape,)
    specs = tuple(VMEM for _ in outs)
    return pl.pallas_call(
        kernel,
        out_shape=out_shape,
        in_specs=list(in_specs),
        out_specs=specs if isinstance(out_shape, tuple) else VMEM,
        scratch_shapes=list(scratch),
        compiler_params=pltpu.CompilerParams(vmem_limit_bytes=megabytes << 20),
    )


FIELD = pltpu.VMEM((18, 32, 128), F32)
prepare = call(
    prepare_kernel,
    (
        shape((24, 32, 128)),
        shape((24, 32, 128)),
        shape((3, 64, 64), BF16),
        shape((576, 192), BF16),
        shape((64, 128)),
        shape((64, 128)),
    ),
    [HBM] * 7 + [VMEM] * 2,
    [pltpu.VMEM((27, 64, 64), BF16), pltpu.SemaphoreType.DMA((12,))],
    6,
)
join = call(join_kernel, shape((9, 64, 64), BF16), [VMEM] * 3, (), 2)
decode = call(
    decode_kernel,
    (shape((16, 32, 128)), shape((3, 192, 640), BF16)),
    [VMEM] * 6 + [ANY] * 2,
    [
        pltpu.VMEM((9, 192, 384), BF16),
        pltpu.VMEM((9, 6, 64, 128), F32),
        pltpu.VMEM((32, 128), F32),
    ],
    14,
)
slopes = call(
    slopes_kernel,
    (shape((49, 64, 128)), shape((384, 1024), BF16)),
    [VMEM] + [HBM] * 4 + [ANY],
    [
        pltpu.VMEM((576, 192), BF16),
        pltpu.VMEM((64, 128), F32),
        pltpu.VMEM((64, 128), F32),
        pltpu.VMEM((27, 64, 64), BF16),
        pltpu.VMEM((5, 12, 64, 128), F32),
        pltpu.SemaphoreType.DMA((4,)),
    ],
    14,
)
records = call(
    records_kernel,
    shape((4, 384, 128)),
    [SMEM] + [HBM] * 2 + [ANY],
    [
        pltpu.VMEM((1, 128), jnp.int32),
        pltpu.VMEM((3, 1, 128), F32),
        pltpu.SemaphoreType.DMA((2,)),
    ],
    8,
)
waves = call(
    wave_kernel,
    shape((16, 32, 128)),
    [SMEM] * 2 + [HBM] + [VMEM] * 2 + [HBM] * 5 + [VMEM] + [HBM],
    [
        pltpu.VMEM((30, 32, 128), F32),
        pltpu.VMEM((4, 384, 128), F32),
        pltpu.SMEM((1, 3), F32),
        pltpu.VMEM((6, 18, 32, 128), F32),
        FIELD,
        FIELD,
        FIELD,
        FIELD,
        FIELD,
        FIELD,
        pltpu.VMEM((3, 8, 32, 128), F32),
        FIELD,
        FIELD,
        pltpu.VMEM((8, 48, 128), F32),
        pltpu.SemaphoreType.DMA((7,)),
    ],
    14,
)
backward = call(
    backward_kernel,
    (shape((3, 1, 64, 64)), shape((896, 128))),
    [VMEM] * 4,
    [
        pltpu.VMEM((8, 4, 64, 128), BF16),
        pltpu.VMEM((4, 64, 384), BF16),
        pltpu.VMEM((16, 64, 192), F32),
        pltpu.VMEM((32, 128), F32),
    ],
    14,
)


def in_hbm(x):
    return pltpu.with_memory_space_constraint(x, pltpu.HBM)


def shifted(block, axes, size):
    low = lax.ppermute(block[0], axes, [(i, i + 1) for i in range(size - 1)])
    high = lax.ppermute(block[1], axes, [(i + 1, i) for i in range(size - 1)])
    return low, high


def per_device(
    latent,
    kernel,
    conv_bias,
    head_weight,
    density,
    wave_prev,
    wave_now,
    adjoint_next,
    adjoint_after,
    source_cell,
    wavelet,
    receiver_cells,
    observed,
):
    place = lax.axis_index(TILE).astype(jnp.int32).reshape(1)
    coarse = latent.reshape(3, 64, 64)
    low, high = shifted((coarse, coarse), TILE, 32)
    fields = [in_hbm(f) for f in (wave_now, wave_prev, adjoint_next, adjoint_after, density)]
    taps = in_hbm(kernel)
    to_next, to_prev, middle, wall, bias, head = prepare(
        *fields, taps, in_hbm(coarse), conv_bias.reshape(1, 64), head_weight.reshape(1, 64)
    )
    low, high, to_next, to_prev = lax.optimization_barrier((low, high, to_next, to_prev))
    left, right = shifted((to_next, to_prev), TILE, 32)
    nine = join(low, middle, high)
    z_prev, z_next = shifted((nine, nine), SHOT, 16)

    speed, lines = decode(z_prev, nine, z_next, wall, bias, head, left, right)
    speeds = lax.all_to_all(speed, SHOT, 0, 0, tiled=True)
    counts = records(
        place, in_hbm(receiver_cells), in_hbm(jnp.transpose(observed, (1, 0, 2))), in_hbm(speed)
    )
    strips = waves(
        place,
        source_cell,
        in_hbm(wavelet),
        left,
        right,
        *fields,
        speeds.reshape(512, 128),
        in_hbm(counts),
    )
    received = lax.all_to_all(strips, SHOT, 0, 0, tiled=True)
    slope, folded = slopes(lines, in_hbm(wall), in_hbm(bias), in_hbm(head), taps, in_hbm(strips))
    latent_grad, parts = backward(received, slope, lines, folded)

    chunks = lax.all_to_all(parts.reshape(16, ROWS, 128), SHOT, 0, 0, tiled=True)
    for axes, copies in ((("xhi", "core"), 4), ("y", 8)):
        chunks = call(sum_kernel, shape((copies, ROWS, 128)), [VMEM])(chunks)
        chunks = lax.all_to_all(chunks, axes, 0, 0, tiled=True)
    chunks = call(sum_kernel, shape((16, ROWS, 128)), [VMEM])(chunks)
    whole = lax.all_to_all(chunks, SHOT, 0, 0, tiled=True)
    kernel_grad, head_grad, bias_grad = call(
        unpack_kernel, (shape((27, 64, 64)), shape((1, 64)), shape((1, 64))), [VMEM]
    )(whole.reshape(896, 128))
    head_grad = head_grad.reshape(64)
    bias_grad = bias_grad.reshape(64)
    return latent_grad, kernel_grad, head_grad, bias_grad


def solution(mesh):
    fine_mesh = Mesh(mesh.devices.reshape(2, 8, 8, 2, 2), ("xlo", "z", "y", "xhi", "core"))
    return jax.shard_map(
        per_device,
        mesh=fine_mesh,
        in_specs=(
            P(TILE, SHOT, None, None),
            P(),
            P(),
            P(),
            P(TILE, None, None),
            P(SHOT, TILE, None, None),
            P(SHOT, TILE, None, None),
            P(SHOT, TILE, None, None),
            P(SHOT, TILE, None, None),
            P(SHOT),
            P(SHOT, None),
            P(SHOT, None),
            P(SHOT, None, None),
        ),
        out_specs=(P(TILE, SHOT, None, None), P(), P(), P()),
        check_vma=False,
    )
```

time: 155 us -> 141 us (0.910)
  the two profiles are of different devices: /device:TPU:1 before, /device:TPU:2 now
where the time goes in v2:
time: 141 us; the launch traced here: 140 us
  blocking collectives  63.2 us (45%)
  starting transfers between devices  37.4 us (27%)
  waiting for transfers between devices  18.4 us (13%)
  Pallas kernels  17.4 us (12%)
  local copies, waits for them, and re-layouts  2.19 us (2%)
  between operations  1.46 us (1%)
    all_to_all x2, blocking collectives, per_device(): chunks = lax.all_to_all(chunks, axes, 0, 0, tiled=True)  28.8 us
    all_to_all x1, blocking collectives, per_device(): lax.all_to_all(parts.reshape(16, ROWS, 128), SHOT, 0, 0, tiled=True)  17.5 us
    all_to_all x1, blocking collectives, per_device(): whole = lax.all_to_all(chunks, SHOT, 0, 0, tiled=True)  16.9 us
    ppermute x3, starting transfers between devices, shifted(): low = lax.ppermute(block[0], axes, [(i, i + 1) for i in range(size - 1)])  12.2 us
    ppermute x3, starting transfers between devices, shifted(): high = lax.ppermute(block[1], axes, [(i + 1, i) for i in range(size - 1)])  12 us
    all_to_all x1, starting transfers between devices, per_device(): speeds = lax.all_to_all(speed, SHOT, 0, 0, tiled=True)  7.88 us
    all_to_all x1, waiting for transfers between devices, per_device(): speeds = lax.all_to_all(speed, SHOT, 0, 0, tiled=True)  7.04 us
    all_to_all x1, waiting for transfers between devices, per_device(): received = lax.all_to_all(strips, SHOT, 0, 0, tiled=True)  5.76 us
  transfers between devices with their start and end apart: 8, of which 5 were waited for; matrix products, arithmetic and copies ran while one was open for 0% of the time, Pallas kernels for 4%

profile of v2, /device:TPU:2, one launch (start us, length us, event | category | flops | bytes accessed | tf_op | source)
XLA Modules:
  0.0 140.1 jit_solution(12136850437071513328)
XLA Ops:
  0.6 1.7 %collective-permute-start = (bf16[3,64,64]{2,1,0:T(8,128)(2,1)}, bf16[3,64,64]{2,1,0:T(8,128)(2,1)S(1)}, u32[]{:S(2)}, u32[]{:S(2)}) collective-permute-start(bf16[3,64,64]{2,1,0:T(8,128)(2,1)} %bitcast.15), channel_id=1, source_target_pairs={{0,1},{1,2},{2,3},{3,4},{4,5},{5,6},{6,7},{7,8},{8,9},{9,10},{10,1... | collective-permute-start | bytes 73736 | tf_op jit(solution)/shard_map/ppermute | solution.py:584
  2.4 1.3 collective-permute-start.1
  3.7 0.0 copy-start.4
  3.7 0.6 copy-done.4
  4.3 0.0 copy-start.5
  4.3 0.7 copy-done.5
  5.0 1.4 shard_map.156
  6.4 0.0 copy-start.1
  6.4 0.0 copy-start.2
  6.4 0.0 copy-start.3
  6.4 0.0 collective-permute-done.low
  6.4 1.2 collective-permute-done.1.high
  7.6 6.2 %collective-permute-start.2 = (f32[24,32,128]{2,1,0:T(8,128)S(1)}, f32[24,32,128]{2,1,0:T(8,128)S(1)}, u32[]{:S(2)}, u32[]{:S(2)}) collective-permute-start(f32[24,32,128]{2,1,0:T(8,128)S(1)} %get-tuple-element.25), channel_id=1, source_target_pairs={{0,1},{1,2},{2,3},{3,4},{4,5},{5,6},{6,7},{7,8},{8,9},{9,10},{10,1... | collective-permute-start | bytes 1179656 | tf_op jit(solution)/shard_map/ppermute | solution.py:584
  13.8 1.3 collective-permute-start.3
  15.2 4.3 %collective-permute-start.4 = (bf16[9,64,64]{2,1,0:T(8,128)(2,1)S(1)}, bf16[9,64,64]{2,1,0:T(8,128)(2,1)S(1)}, u32[]{:S(2)}, u32[]{:S(2)}) collective-permute-start(bf16[9,64,64]{2,1,0:T(8,128)(2,1)S(1)} %shard_map.157.own), channel_id=1, source_target_pairs={{0,32},{32,64},{64,96},{96,128},{128,160},{160,192},{192,224},{224... | collective-permute-start | bytes 221192 | tf_op jit(solution)/shard_map/ppermute | solution.py:584
  19.5 9.5 %collective-permute-start.5 = (bf16[9,64,64]{2,1,0:T(8,128)(2,1)S(1)}, bf16[9,64,64]{2,1,0:T(8,128)(2,1)S(1)}, u32[]{:S(2)}, u32[]{:S(2)}) collective-permute-start(bf16[9,64,64]{2,1,0:T(8,128)(2,1)S(1)} %shard_map.157.own), channel_id=1, source_target_pairs={{32,0},{64,32},{96,64},{128,96},{160,128},{192,160},{224,192},{256... | collective-permute-start | bytes 221192 | tf_op jit(solution)/shard_map/ppermute | solution.py:585
  28.9 2.1 %collective-permute-done.4.z_prev = bf16[9,64,64]{2,1,0:T(8,128)(2,1)S(1)} collective-permute-done((bf16[9,64,64]{2,1,0:T(8,128)(2,1)S(1)}, bf16[9,64,64]{2,1,0:T(8,128)(2,1)S(1)}, u32[]{:S(2)}, u32[]{:S(2)}) %collective-permute-start.4) | collective-permute-done | bytes 73760 | tf_op jit(solution)/shard_map/ppermute | solution.py:584
  31.0 2.4 %collective-permute-done.5.z_next = bf16[9,64,64]{2,1,0:T(8,128)(2,1)S(1)} collective-permute-done((bf16[9,64,64]{2,1,0:T(8,128)(2,1)S(1)}, bf16[9,64,64]{2,1,0:T(8,128)(2,1)S(1)}, u32[]{:S(2)}, u32[]{:S(2)}) %collective-permute-start.5) | collective-permute-done | bytes 73760 | tf_op jit(solution)/shard_map/ppermute | solution.py:585
  33.4 0.0 collective-permute-done.2.left
  33.4 0.0 collective-permute-done.3.right
  33.4 3.8 %shard_map.158 = (f32[16,32,128]{2,1,0:T(8,128)}, bf16[3,192,640]{2,1,0:T(8,128)(2,1)S(1)}) custom-call(bf16[9,64,64]{2,1,0:T(8,128)(2,1)S(1)} %collective-permute-done.4.z_prev, bf16[9,64,64]{2,1,0:T(8,128)(2,1)S(1)} %shard_map.157.own, bf16[9,64,64]{2,1,0:T(8,128)(2,1)S(1)} %collective-permute-done.5.z_next, ...), custom_call_target="tpu_custom_call" | custom-call | tf_op jit(solution)/shard_map/pallas_call | solution.py:617
  37.2 7.9 %all-to-all-start = ((f32[16,32,128]{2,1,0:T(8,128)}), f32[16,32,128]{2,1,0:T(8,128)S(1)}, u32[]{:S(2)}, u32[]{:S(2)}) async-start(f32[16,32,128]{2,1,0:T(8,128)} %get-tuple-element.33.after), calls=%async_computation | async-start | bytes 524288 | tf_op jit(solution)/shard_map/all_to_all | solution.py:618
  45.7 1.1 shard_map.159.counts_in
  46.9 0.0 copy-done.1
  46.9 0.0 copy-done.2
  46.9 0.0 copy-done.3
  46.9 0.0 copy-start
  46.9 0.9 copy-done
  47.8 7.0 %all-to-all-done = f32[16,32,128]{2,1,0:T(8,128)S(1)} async-done(((f32[16,32,128]{2,1,0:T(8,128)}), f32[16,32,128]{2,1,0:T(8,128)S(1)}, u32[]{:S(2)}, u32[]{:S(2)}) %all-to-all-start) | async-done | bytes 262176 | tf_op jit(solution)/shard_map/all_to_all | solution.py:618
  54.8 3.9 %shard_map.160.after = f32[16,32,128]{2,1,0:T(8,128)} custom-call(s32[1]{0:T(128)} %bitcast.place, s32[1]{0:T(128)S(6)} %copy.17.source, f32[1,3]{1,0:T(1,128)} %pulses_in.1, f32[24,32,128]{2,1,0:T(8,128)S(1)} %collective-permute-done.2.left, f32[24,32,128]{2,1,0:T(8,128)S(1)} %collective-permute-done.3.right, f32[1,6,32,128]{3,2,1,0:T(8,128)} %wave_now.3, ...), custom_call_target="tpu_custom_call" | custom-call | tf_op jit(solution)/shard_map/pallas_call | solution.py:622
  58.7 5.2 %all-to-all-start.1 = ((f32[16,32,128]{2,1,0:T(8,128)}), f32[16,32,128]{2,1,0:T(8,128)S(1)}, u32[]{:S(2)}, u32[]{:S(2)}) async-start(f32[16,32,128]{2,1,0:T(8,128)} %shard_map.160.after), calls=%async_computation.1 | async-start | bytes 524288 | tf_op jit(solution)/shard_map/all_to_all | solution.py:632
  64.0 3.5 %shard_map.161 = (f32[49,64,128]{2,1,0:T(8,128)S(1)}, bf16[384,1024]{1,0:T(8,128)(2,1)S(1)}) custom-call(bf16[3,192,640]{2,1,0:T(8,128)(2,1)S(1)} %get-tuple-element.34.lines, bf16[576,192]{1,0:T(8,128)(2,1)} %copy-done.1, f32[64,128]{1,0:T(8,128)} %copy-done.2, f32[64,128]{1,0:T(8,128)} %copy-done.3, bf16[27,64,64]{2,1,0:T(8,128)(2,1)} %kernel_in.3, ...), custom_call_target="tpu_custom_call" | custom-call | tf_op jit(solution)/shard_map/pallas_call | solution.py:633
  67.5 5.8 %all-to-all-done.1.received = f32[16,32,128]{2,1,0:T(8,128)S(1)} async-done(((f32[16,32,128]{2,1,0:T(8,128)}), f32[16,32,128]{2,1,0:T(8,128)S(1)}, u32[]{:S(2)}, u32[]{:S(2)}) %all-to-all-start.1) | async-done | bytes 262176 | tf_op jit(solution)/shard_map/all_to_all | solution.py:632
  73.2 2.4 %shard_map.162 = (f32[3,1,64,64]{3,2,1,0:T(8,128)}, f32[896,128]{1,0:T(8,128)S(1)}) custom-call(f32[16,32,128]{2,1,0:T(8,128)S(1)} %all-to-all-done.1.received, f32[49,64,128]{2,1,0:T(8,128)S(1)} %get-tuple-element.35.slopes, bf16[3,192,640]{2,1,0:T(8,128)(2,1)S(1)} %get-tuple-element.34.lines, bf16[384,1024]{1,0:T(8,128)(2,1)S(1)} %get-tuple-element.36.folded), custom_call_target="tpu_custom_call" | custom-call | tf_op jit(solution)/shard_map/pallas_call | solution.py:634
  75.6 17.5 %all_to_all.30.received = f32[16,56,128]{2,1,0:T(8,128)S(1)} all-to-all(f32[16,56,128]{2,1,0:T(8,128)S(1)} %bitcast.12), channel_id=1, replica_groups=mesh['xlo'=2,'z'=8,'y'=8,'xhi'=2,'core'=2] {'xlo','z'}, dimensions={0} | all-to-all | bytes 917504 | tf_op jit(solution)/shard_map/all_to_all | solution.py:636
  93.2 10.1 %all_to_all.31.received = f32[4,56,128]{2,1,0:T(8,128)S(1)} all-to-all(f32[4,56,128]{2,1,0:T(8,128)S(1)} %shard_map.163), channel_id=1, replica_groups=mesh['xlo'=2,'z'=8,'y'=8,'xhi'=2,'core'=2] {'xhi','core'}, dimensions={0} | all-to-all | bytes 229376 | tf_op jit(solution)/shard_map/all_to_all | solution.py:639
  103.3 18.7 %all_to_all.32.received = f32[8,56,128]{2,1,0:T(8,128)S(1)} all-to-all(f32[8,56,128]{2,1,0:T(8,128)S(1)} %shard_map.164), channel_id=1, replica_groups=mesh['xlo'=2,'z'=8,'y'=8,'xhi'=2,'core'=2] {'y'}, dimensions={0} | all-to-all | bytes 458752 | tf_op jit(solution)/shard_map/all_to_all | solution.py:639
  122.0 16.9 %all_to_all.33 = f32[16,56,128]{2,1,0:T(8,128)S(1)} all-to-all(f32[16,56,128]{2,1,0:T(8,128)S(1)} %shard_map.165), channel_id=1, replica_groups=mesh['xlo'=2,'z'=8,'y'=8,'xhi'=2,'core'=2] {'xlo','z'}, dimensions={0} | all-to-all | bytes 917504 | tf_op jit(solution)/shard_map/all_to_all | solution.py:641
  138.9 1.1 shard_map.166
  (4 shorter events, 0.1 us)
Async XLA Ops:
  0.6 5.8 %collective-permute-start = (bf16[3,64,64]{2,1,0:T(8,128)(2,1)}, bf16[3,64,64]{2,1,0:T(8,128)(2,1)S(1)}, u32[]{:S(2)}, u32[]{:S(2)}) collective-permute-start(bf16[3,64,64]{2,1,0:T(8,128)(2,1)} %bitcast.15), channel_id=1, source_target_pairs={{0,1},{1,2},{2,3},{3,4},{4,5},{5,6},{6,7},{7,8},{8,9},{9,10},{10,1... | collective-permute-start | bytes 73736 | tf_op jit(solution)/shard_map/ppermute | solution.py:584
  2.4 5.2 %collective-permute-start.1 = (bf16[3,64,64]{2,1,0:T(8,128)(2,1)}, bf16[3,64,64]{2,1,0:T(8,128)(2,1)S(1)}, u32[]{:S(2)}, u32[]{:S(2)}) collective-permute-start(bf16[3,64,64]{2,1,0:T(8,128)(2,1)} %bitcast.16), channel_id=1, source_target_pairs={{1,0},{2,1},{3,2},{4,3},{5,4},{6,5},{7,6},{8,7},{9,8},{10,9},{11,1... | collective-permute-start | bytes 73736 | tf_op jit(solution)/shard_map/ppermute | solution.py:585
  3.7 0.7 copy-start.4
  4.3 0.7 copy-start.5
  6.4 40.5 %copy-start.1 = (bf16[576,192]{1,0:T(8,128)(2,1)}, bf16[576,192]{1,0:T(8,128)(2,1)S(1)}, u32[]{:S(2)}) copy-start(bf16[576,192]{1,0:T(8,128)(2,1)S(1)} %get-tuple-element.30.wall.wall_in) | copy-start | bytes 663556
  6.4 40.5 %copy-start.2 = (f32[64,128]{1,0:T(8,128)}, f32[64,128]{1,0:T(8,128)S(1)}, u32[]{:S(2)}) copy-start(f32[64,128]{1,0:T(8,128)S(1)} %get-tuple-element.31.bias.bias_in) | copy-start | bytes 98308
  6.4 40.5 %copy-start.3 = (f32[64,128]{1,0:T(8,128)}, f32[64,128]{1,0:T(8,128)S(1)}, u32[]{:S(2)}) copy-start(f32[64,128]{1,0:T(8,128)S(1)} %get-tuple-element.32.head.head_in) | copy-start | bytes 98308
  7.6 25.7 %collective-permute-start.2 = (f32[24,32,128]{2,1,0:T(8,128)S(1)}, f32[24,32,128]{2,1,0:T(8,128)S(1)}, u32[]{:S(2)}, u32[]{:S(2)}) collective-permute-start(f32[24,32,128]{2,1,0:T(8,128)S(1)} %get-tuple-element.25), channel_id=1, source_target_pairs={{0,1},{1,2},{2,3},{3,4},{4,5},{5,6},{6,7},{7,8},{8,9},{9,10},{10,1... | collective-permute-start | bytes 1179656 | tf_op jit(solution)/shard_map/ppermute | solution.py:584
  13.8 19.5 %collective-permute-start.3 = (f32[24,32,128]{2,1,0:T(8,128)S(1)}, f32[24,32,128]{2,1,0:T(8,128)S(1)}, u32[]{:S(2)}, u32[]{:S(2)}) collective-permute-start(f32[24,32,128]{2,1,0:T(8,128)S(1)} %get-tuple-element.26), channel_id=1, source_target_pairs={{1,0},{2,1},{3,2},{4,3},{5,4},{6,5},{7,6},{8,7},{9,8},{10,9},{11,1... | collective-permute-start | bytes 1179656 | tf_op jit(solution)/shard_map/ppermute | solution.py:585
  15.2 15.8 %collective-permute-start.4 = (bf16[9,64,64]{2,1,0:T(8,128)(2,1)S(1)}, bf16[9,64,64]{2,1,0:T(8,128)(2,1)S(1)}, u32[]{:S(2)}, u32[]{:S(2)}) collective-permute-start(bf16[9,64,64]{2,1,0:T(8,128)(2,1)S(1)} %shard_map.157.own), channel_id=1, source_target_pairs={{0,32},{32,64},{64,96},{96,128},{128,160},{160,192},{192,224},{224... | collective-permute-start | bytes 221192 | tf_op jit(solution)/shard_map/ppermute | solution.py:584
  19.5 13.9 %collective-permute-start.5 = (bf16[9,64,64]{2,1,0:T(8,128)(2,1)S(1)}, bf16[9,64,64]{2,1,0:T(8,128)(2,1)S(1)}, u32[]{:S(2)}, u32[]{:S(2)}) collective-permute-start(bf16[9,64,64]{2,1,0:T(8,128)(2,1)S(1)} %shard_map.157.own), channel_id=1, source_target_pairs={{32,0},{64,32},{96,64},{128,96},{160,128},{192,160},{224,192},{256... | collective-permute-start | bytes 221192 | tf_op jit(solution)/shard_map/ppermute | solution.py:585
  37.2 17.6 %all-to-all-start = ((f32[16,32,128]{2,1,0:T(8,128)}), f32[16,32,128]{2,1,0:T(8,128)S(1)}, u32[]{:S(2)}, u32[]{:S(2)}) async-start(f32[16,32,128]{2,1,0:T(8,128)} %get-tuple-element.33.after), calls=%async_computation | async-start | bytes 524288 | tf_op jit(solution)/shard_map/all_to_all | solution.py:618
  46.9 0.9 copy-start
  58.7 14.5 %all-to-all-start.1 = ((f32[16,32,128]{2,1,0:T(8,128)}), f32[16,32,128]{2,1,0:T(8,128)S(1)}, u32[]{:S(2)}, u32[]{:S(2)}) async-start(f32[16,32,128]{2,1,0:T(8,128)} %shard_map.160.after), calls=%async_computation.1 | async-start | bytes 524288 | tf_op jit(solution)/shard_map/all_to_all | solution.py:632

commit v3 on v2

--- a/solution.py
+++ b/solution.py
@@ -8,12 +8,13 @@
 
 SHOT = ("xlo", "z")
 TILE = ("y", "xhi", "core")
+NEAR = ("xlo", "xhi", "core")
+FAR = ("z", "y")
 F32 = jnp.float32
 BF16 = jnp.bfloat16
 courant = 0.005
 speed_low = 1.5
 speed_span = 3.0
-ROWS = 56
 NT = (((1,), (1,)), ((), ()))
 
 
@@ -51,29 +52,10 @@
         copy.wait()
 
 
-def prepare_kernel(
-    wave_now,
-    wave_prev,
-    adj_next,
-    adj_after,
-    density,
-    kernel_in,
-    coarse,
-    bias,
-    head,
-    to_next,
-    to_prev,
-    middle,
-    wall,
-    bias_wide,
-    head_wide,
-    kernel,
-    sems,
+def pack_kernel(
+    wave_now, wave_prev, adj_next, adj_after, density, latent, to_next, to_prev, coarse, sems
 ):
-    copies = [
-        pltpu.make_async_copy(kernel_in, kernel, sems.at[10]),
-        pltpu.make_async_copy(coarse, middle, sems.at[11]),
-    ]
+    copies = [pltpu.make_async_copy(latent, coarse, sems.at[10])]
     fields = ((wave_now, 6), (wave_prev, 5), (adj_next, 4), (adj_after, 3), (density, 6))
     at = 0
     for i, (ref, rows) in enumerate(fields):
@@ -83,17 +65,31 @@
         copies.append(pltpu.make_async_copy(field.at[pl.ds(0, rows)], to_prev.at[here], sems.at[5 + i]))
         at += rows
     start_all(copies)
+    copies[0].wait()
+    for x in range(3):
+        block = coarse[x].astype(F32)
+        packed = jnp.concatenate([block[0:32], block[32:64]], axis=1)
+        to_next[24 + x] = packed
+        to_prev[24 + x] = packed
+    wait_all(copies[1:])
+
+
+def join_kernel(left, coarse, right, out):
+    for i, ref in ((0, left), (2, right)):
+        for x in range(3):
+            packed = ref[24 + x]
+            out[3 * i + x] = jnp.concatenate([packed[:, :64], packed[:, 64:]], axis=0).astype(BF16)
+    out[3:6] = coarse[...]
+
+
+def taps_kernel(kernel_in, bias, head, wall, bias_wide, head_wide, kernel, sem):
+    copy = pltpu.make_async_copy(kernel_in, kernel, sem)
+    copy.start()
     bias_wide[...] = jnp.broadcast_to(bias[...], (128, 64)).T
     head_wide[...] = jnp.broadcast_to(head[...].astype(F32), (128, 64)).T
-    copies[0].wait()
+    copy.wait()
     for j in range(9):
         wall[64 * j : 64 * j + 64, :] = jnp.concatenate([kernel[3 * j + e] for e in range(3)], axis=1)
-    wait_all(copies[1:])
-
-
-def join_kernel(low, middle, high, out):
-    for i, ref in enumerate((low, middle, high)):
-        out[3 * i : 3 * i + 3] = ref[...]
 
 
 def fold_taps(kernel, folded):
@@ -130,7 +126,7 @@
 
 
 def decode_kernel(
-    z_prev, own, z_next, wall, bias, head, left, right, speed_out, lines_out, lines, sums, row_logit
+    z_prev, own, z_next, wall, bias, head, speed_out, lines_out, lines, sums, row_logit
 ):
     spread = spread_matrix()
     for zi, ref in enumerate((z_prev, own, z_next)):
@@ -188,23 +184,24 @@
 
         z_sums(product, range(4), store)
 
-    def rows(k, carry):
+    def rows(k, owned):
         r = k + 1
         for zz in range(4):
             pre = sums[(r - 1) // 2, zz] + sums[r // 2, 4 + zz] + sums[(r + 1) // 2, 8 + zz] + bias[...]
             gate = sigmoid(pre)
-            hidden = (pre * gate).astype(BF16)
+            hidden = (pre * gate).astype(BF16).astype(F32)
             slope_out[4 * k + zz] = head[...] * (gate * (1.0 + pre * (1.0 - gate)))
-            hidden = hidden.astype(F32)
-            if zz in (1, 2):
-                slope_out[32 + 2 * k + zz - 1] = hidden
+            if owned and zz in (1, 2):
+                slope_out[30 + 2 * k + zz - 1] = hidden
             logit = jnp.sum(hidden * head[...], axis=0, keepdims=True)
-            slope_out[48, pl.ds(4 * k + zz, 1), :] = logit
-        return carry
-
-    lax.fori_loop(0, 8, rows, 0)
-    slope_out[48, 0:32, :] = sigmoid(slope_out[48, 0:32, :])
-    slope_out[48, 32:64, :] = jnp.zeros((32, 128), F32)
+            slope_out[44, pl.ds(4 * k + zz, 1), :] = logit
+        return owned
+
+    rows(0, False)
+    lax.fori_loop(1, 7, lambda k, carry: rows(k, True), True)
+    rows(7, False)
+    slope_out[44, 0:32, :] = sigmoid(slope_out[44, 0:32, :])
+    slope_out[44, 32:64, :] = jnp.zeros((32, 128), F32)
     fold_taps(kernel, folded)
 
 
@@ -230,12 +227,30 @@
     return get
 
 
-def records_kernel(place, receivers_in, observed_in, after, counts, receivers, observed, sems):
+def medium_kernel(
+    place,
+    wave_now,
+    wave_prev,
+    adj_next,
+    adj_after,
+    density,
+    receivers_in,
+    observed_in,
+    after,
+    own,
+    counts_out,
+    counts,
+    receivers,
+    observed,
+    sems,
+):
+    fields = (wave_now.at[0], wave_prev.at[0], adj_next.at[0], adj_after.at[0], density)
     wait_all(
         start_all(
-            [
-                pltpu.make_async_copy(receivers_in, receivers, sems.at[0]),
-                pltpu.make_async_copy(observed_in, observed, sems.at[1]),
+            [pltpu.make_async_copy(f, own.at[pl.ds(6 * i, 6)], sems.at[i]) for i, f in enumerate(fields)]
+            + [
+                pltpu.make_async_copy(receivers_in, receivers, sems.at[5]),
+                pltpu.make_async_copy(observed_in, observed, sems.at[6]),
             ]
         )
     )
@@ -256,6 +271,7 @@
     for n in range(3):
         at = 128 + 384 * n
         counts[1 + n] = maps[:, at : at + 128] + maps[:, at + 128 : at + 256] + maps[:, at + 256 : at + 384]
+    wait_all(start_all([pltpu.make_async_copy(counts, counts_out, sems.at[7])]))
 
 
 def wave_kernel(
@@ -264,15 +280,10 @@
     pulses_in,
     left,
     right,
-    wave_now,
-    wave_prev,
-    adj_next,
-    adj_after,
-    density,
     speeds,
+    own,
     counts_in,
     send_out,
-    own,
     counts,
     pulses,
     faces,
@@ -288,12 +299,10 @@
     grads,
     sems,
 ):
-    fields = (wave_now.at[0], wave_prev.at[0], adj_next.at[0], adj_after.at[0], density)
     copies = start_all(
-        [pltpu.make_async_copy(f, own.at[pl.ds(6 * i, 6)], sems.at[i]) for i, f in enumerate(fields)]
-        + [
-            pltpu.make_async_copy(pulses_in, pulses, sems.at[5]),
-            pltpu.make_async_copy(counts_in, counts, sems.at[6]),
+        [
+            pltpu.make_async_copy(pulses_in, pulses, sems.at[0]),
+            pltpu.make_async_copy(counts_in, counts, sems.at[1]),
         ]
     )
     send = send_out.reshape(512, 128)
@@ -310,7 +319,6 @@
         for j in range(2):
             speed[w, pl.ds(j, 16, 2), :] = speeds[pl.ds(2 * (w - 1) + j, 16, 32), :]
     grads[...] = jnp.zeros_like(grads)
-    wait_all(copies)
     for w in range(18):
         d = dens(w)
         buoy[w] = jnp.where(d > 0.0, 1.0 / d, 0.0)
@@ -321,6 +329,7 @@
         inside = jnp.where(centre > 0.0, 0.5, 0.0)
         for i, beside in enumerate((buoy[w + 1], buoy[w - 1]) + shifts(centre)):
             faces[i, w] = inside * (centre + beside)
+    copies[0].wait()
 
     def laplace(f, w):
         centre = f(w)
@@ -356,6 +365,7 @@
             lap = laplace(lambda v: coef[v] * f(v), w)
             out[w] = 2.0 * f(w) - before(w) + lap + residual(u, n, w)
 
+    copies[1].wait()
     backward(lam5, lam6, u4, 2, range(3, 15), lam4)
     backward(row_of(lam4), lam5, u3, 1, range(4, 14), lam3)
     for w in range(5, 13):
@@ -375,7 +385,7 @@
     total = received[0]
     for s in range(1, 16):
         total = total + received[s]
-    squash = slopes[48, 0:32, :]
+    squash = slopes[44, 0:32, :]
     logit_grads[...] = total * speed_span * squash * (1.0 - squash)
     head_sum = jnp.zeros((64, 128), F32)
     bias_sum = jnp.zeros((64, 128), F32)
@@ -388,7 +398,7 @@
             if 1 <= x <= 6 and 1 <= zz <= 2:
                 px = (x - 1) % 2
                 low_wide[2 * px + zz - 1, :, 64 * (x - 1 - px) : 64 * (x + 1 - px)] = rounded
-                head_sum = head_sum + slopes[32 + 2 * x + zz - 1] * grad
+                head_sum = head_sum + slopes[30 + 2 * x + zz - 1] * grad
                 bias_sum = bias_sum + pre_grad
 
     ones = jnp.ones((8, 128), BF16)
@@ -397,7 +407,7 @@
         term = lax.dot_general(ones, piece, NT, preferred_element_type=F32)
         row = term if row is None else row + term
     parts_out[864:872, :] = row
-    parts_out[872:896, :] = jnp.zeros((24, 128), F32)
+    parts_out[872:1024, :] = jnp.zeros((152, 128), F32)
 
     parities = {-1: (0,), 0: (0, 1), 1: (1,)}
     found = {}
@@ -444,10 +454,24 @@
 
 def sum_kernel(received, out):
     total = received[0]
-    for s in range(1, received.shape[0]):
+    for s in range(1, 8):
         total = total + received[s]
-    for s in range(out.shape[0]):
-        out[s] = total
+    out[...] = total
+
+
+def sum_pairs_kernel(received, out):
+    total = received[0:8, :]
+    for s in range(1, 16):
+        total = total + received[8 * s : 8 * s + 8, :]
+    pair = total[0:2] + total[2:4] + total[4:6] + total[6:8]
+    pairs = jnp.concatenate([pair] * 4, axis=0)
+    for s in range(16):
+        out[8 * s : 8 * s + 8, :] = pairs
+
+
+def repeat_kernel(chunk, out):
+    for s in range(8):
+        out[s] = chunk[...]
 
 
 def unpack_kernel(rows, kernel_out, head_out, bias_out):
@@ -476,7 +500,7 @@
 
 def call(kernel, out_shape, in_specs, scratch=(), megabytes=8):
     outs = out_shape if isinstance(out_shape, tuple) else (out_shape,)
-    specs = tuple(VMEM for _ in outs)
+    specs = tuple(HBM if hasattr(out, "memory_space") else VMEM for out in outs)
     return pl.pallas_call(
         kernel,
         out_shape=out_shape,
@@ -488,25 +512,25 @@
 
 
 FIELD = pltpu.VMEM((18, 32, 128), F32)
-prepare = call(
-    prepare_kernel,
-    (
-        shape((24, 32, 128)),
-        shape((24, 32, 128)),
-        shape((3, 64, 64), BF16),
-        shape((576, 192), BF16),
-        shape((64, 128)),
-        shape((64, 128)),
-    ),
-    [HBM] * 7 + [VMEM] * 2,
-    [pltpu.VMEM((27, 64, 64), BF16), pltpu.SemaphoreType.DMA((12,))],
-    6,
+pack = call(
+    pack_kernel,
+    (shape((27, 32, 128)), shape((27, 32, 128)), shape((3, 64, 64), BF16)),
+    [HBM] * 6,
+    [pltpu.SemaphoreType.DMA((11,))],
+    4,
 )
-join = call(join_kernel, shape((9, 64, 64), BF16), [VMEM] * 3, (), 2)
+join = call(join_kernel, shape((9, 64, 64), BF16), [VMEM] * 3, (), 4)
+widen = call(
+    taps_kernel,
+    (shape((576, 192), BF16), shape((64, 128)), shape((64, 128))),
+    [HBM] + [VMEM] * 2,
+    [pltpu.VMEM((27, 64, 64), BF16), pltpu.SemaphoreType.DMA],
+    4,
+)
 decode = call(
     decode_kernel,
     (shape((16, 32, 128)), shape((3, 192, 640), BF16)),
-    [VMEM] * 6 + [ANY] * 2,
+    [VMEM] * 6,
     [
         pltpu.VMEM((9, 192, 384), BF16),
         pltpu.VMEM((9, 6, 64, 128), F32),
@@ -516,7 +540,7 @@
 )
 slopes = call(
     slopes_kernel,
-    (shape((49, 64, 128)), shape((384, 1024), BF16)),
+    (shape((45, 64, 128)), shape((384, 1024), BF16)),
     [VMEM] + [HBM] * 4 + [ANY],
     [
         pltpu.VMEM((576, 192), BF16),
@@ -528,23 +552,23 @@
     ],
     14,
 )
-records = call(
-    records_kernel,
-    shape((4, 384, 128)),
-    [SMEM] + [HBM] * 2 + [ANY],
+medium = call(
+    medium_kernel,
+    (shape((30, 32, 128)), pltpu.HBM((4, 384, 128), F32)),
+    [SMEM] + [HBM] * 7 + [ANY],
     [
+        pltpu.VMEM((4, 384, 128), F32),
         pltpu.VMEM((1, 128), jnp.int32),
         pltpu.VMEM((3, 1, 128), F32),
-        pltpu.SemaphoreType.DMA((2,)),
+        pltpu.SemaphoreType.DMA((8,)),
     ],
     8,
 )
 waves = call(
     wave_kernel,
     shape((16, 32, 128)),
-    [SMEM] * 2 + [HBM] + [VMEM] * 2 + [HBM] * 5 + [VMEM] + [HBM],
+    [SMEM] * 2 + [HBM] + [VMEM] * 4 + [HBM],
     [
-        pltpu.VMEM((30, 32, 128), F32),
         pltpu.VMEM((4, 384, 128), F32),
         pltpu.SMEM((1, 3), F32),
         pltpu.VMEM((6, 18, 32, 128), F32),
@@ -558,13 +582,13 @@
         FIELD,
         FIELD,
         pltpu.VMEM((8, 48, 128), F32),
-        pltpu.SemaphoreType.DMA((7,)),
+        pltpu.SemaphoreType.DMA((2,)),
     ],
     14,
 )
 backward = call(
     backward_kernel,
-    (shape((3, 1, 64, 64)), shape((896, 128))),
+    (shape((3, 1, 64, 64)), shape((1024, 128))),
     [VMEM] * 4,
     [
         pltpu.VMEM((8, 4, 64, 128), BF16),
@@ -602,46 +626,42 @@
     observed,
 ):
     place = lax.axis_index(TILE).astype(jnp.int32).reshape(1)
-    coarse = latent.reshape(3, 64, 64)
-    low, high = shifted((coarse, coarse), TILE, 32)
     fields = [in_hbm(f) for f in (wave_now, wave_prev, adjoint_next, adjoint_after, density)]
     taps = in_hbm(kernel)
-    to_next, to_prev, middle, wall, bias, head = prepare(
-        *fields, taps, in_hbm(coarse), conv_bias.reshape(1, 64), head_weight.reshape(1, 64)
-    )
-    low, high, to_next, to_prev = lax.optimization_barrier((low, high, to_next, to_prev))
+    to_next, to_prev, coarse = pack(*fields, in_hbm(latent.reshape(3, 64, 64)))
     left, right = shifted((to_next, to_prev), TILE, 32)
-    nine = join(low, middle, high)
+    wall, bias, head = widen(taps, conv_bias.reshape(1, 64), head_weight.reshape(1, 64))
+    nine = join(left, coarse, right)
     z_prev, z_next = shifted((nine, nine), SHOT, 16)
 
-    speed, lines = decode(z_prev, nine, z_next, wall, bias, head, left, right)
+    speed, lines = decode(z_prev, nine, z_next, wall, bias, head)
     speeds = lax.all_to_all(speed, SHOT, 0, 0, tiled=True)
-    counts = records(
-        place, in_hbm(receiver_cells), in_hbm(jnp.transpose(observed, (1, 0, 2))), in_hbm(speed)
-    )
+    records = jnp.transpose(observed, (1, 0, 2))
+    own, counts = medium(place, *fields, in_hbm(receiver_cells), in_hbm(records), in_hbm(speed))
     strips = waves(
         place,
         source_cell,
         in_hbm(wavelet),
         left,
         right,
-        *fields,
         speeds.reshape(512, 128),
+        own,
         in_hbm(counts),
     )
     received = lax.all_to_all(strips, SHOT, 0, 0, tiled=True)
     slope, folded = slopes(lines, in_hbm(wall), in_hbm(bias), in_hbm(head), taps, in_hbm(strips))
     latent_grad, parts = backward(received, slope, lines, folded)
 
-    chunks = lax.all_to_all(parts.reshape(16, ROWS, 128), SHOT, 0, 0, tiled=True)
-    for axes, copies in ((("xhi", "core"), 4), ("y", 8)):
-        chunks = call(sum_kernel, shape((copies, ROWS, 128)), [VMEM])(chunks)
-        chunks = lax.all_to_all(chunks, axes, 0, 0, tiled=True)
-    chunks = call(sum_kernel, shape((16, ROWS, 128)), [VMEM])(chunks)
-    whole = lax.all_to_all(chunks, SHOT, 0, 0, tiled=True)
+    chunks = lax.all_to_all(parts.reshape(8, 128, 128), NEAR, 0, 0, tiled=True)
+    chunk = call(sum_kernel, shape((128, 128)), [VMEM])(chunks)
+    pairs = lax.all_to_all(chunk.reshape(64, 2, 128), FAR, 0, 0, tiled=True)
+    pairs = call(sum_pairs_kernel, shape((128, 128)), [VMEM])(pairs.reshape(128, 128))
+    chunk = lax.all_to_all(pairs.reshape(64, 2, 128), FAR, 0, 0, tiled=True)
+    chunks = call(repeat_kernel, shape((8, 128, 128)), [VMEM])(chunk.reshape(128, 128))
+    whole = lax.all_to_all(chunks, NEAR, 0, 0, tiled=True)
     kernel_grad, head_grad, bias_grad = call(
         unpack_kernel, (shape((27, 64, 64)), shape((1, 64)), shape((1, 64))), [VMEM]
-    )(whole.reshape(896, 128))
+    )(whole.reshape(1024, 128))
     head_grad = head_grad.reshape(64)
     bias_grad = bias_grad.reshape(64)
     return latent_grad, kernel_grad, head_grad, bias_grad

time: 141 us -> 142 us (level)
  the two profiles are of different devices: /device:TPU:2 before, /device:TPU:1 now
where the time goes in v3:
time: 142 us; the launch traced here: 141 us
  blocking collectives  70.4 us (50%)
  starting transfers between devices  33.5 us (24%)
  Pallas kernels  18.6 us (13%)
  waiting for transfers between devices  17.2 us (12%)
  between operations  1.48 us (1%)
    all_to_all x1, blocking collectives, per_device(): pairs = lax.all_to_all(chunk.reshape(64, 2, 128), FAR, 0, 0, tiled=True)  22.3 us
    all_to_all x1, blocking collectives, per_device(): chunks = lax.all_to_all(parts.reshape(8, 128, 128), NEAR, 0, 0, tiled=True)  17.9 us
    all_to_all x1, blocking collectives, per_device(): whole = lax.all_to_all(chunks, NEAR, 0, 0, tiled=True)  15.3 us
    all_to_all x1, blocking collectives, per_device(): chunk = lax.all_to_all(pairs.reshape(64, 2, 128), FAR, 0, 0, tiled=True)  14.9 us
    all_to_all x1, starting transfers between devices, per_device(): speeds = lax.all_to_all(speed, SHOT, 0, 0, tiled=True)  13.5 us
    ppermute x2, starting transfers between devices, shifted(): low = lax.ppermute(block[0], axes, [(i, i + 1) for i in range(size - 1)])  10.7 us
    ppermute x2, waiting for transfers between devices, shifted(): high = lax.ppermute(block[1], axes, [(i + 1, i) for i in range(size - 1)])  5.9 us
    ppermute x2, starting transfers between devices, shifted(): high = lax.ppermute(block[1], axes, [(i + 1, i) for i in range(size - 1)])  5.35 us
  transfers between devices with their start and end apart: 6, of which 5 were waited for; matrix products, arithmetic and copies ran while one was open for 0% of the time, Pallas kernels for 5%

profile of v3, /device:TPU:1, one launch (start us, length us, event | category | flops | bytes accessed | tf_op | source)
XLA Modules:
  0.0 141.2 jit_solution(4530184616856948101)
XLA Ops:
  0.6 0.0 copy-start.4
  0.6 0.0 copy-start.3
  0.7 1.3 shard_map.156
  2.0 6.0 %collective-permute-start = (f32[27,32,128]{2,1,0:T(8,128)S(1)}, f32[27,32,128]{2,1,0:T(8,128)S(1)}, u32[]{:S(2)}, u32[]{:S(2)}) collective-permute-start(f32[27,32,128]{2,1,0:T(8,128)S(1)} %get-tuple-element.21), channel_id=1, source_target_pairs={{0,1},{1,2},{2,3},{3,4},{4,5},{5,6},{6,7},{7,8},{8,9},{9,10},{10,1... | collective-permute-start | bytes 1327112 | tf_op jit(solution)/shard_map/ppermute | solution.py:608
  8.0 4.1 %collective-permute-start.1 = (f32[27,32,128]{2,1,0:T(8,128)S(1)}, f32[27,32,128]{2,1,0:T(8,128)S(1)}, u32[]{:S(2)}, u32[]{:S(2)}) collective-permute-start(f32[27,32,128]{2,1,0:T(8,128)S(1)} %get-tuple-element.22), channel_id=1, source_target_pairs={{1,0},{2,1},{3,2},{4,3},{5,4},{6,5},{7,6},{8,7},{9,8},{10,9},{11,1... | collective-permute-start | bytes 1327112 | tf_op jit(solution)/shard_map/ppermute | solution.py:609
  12.1 1.2 collective-permute-done.left
  13.3 5.9 %collective-permute-done.1.right = f32[27,32,128]{2,1,0:T(8,128)S(1)} collective-permute-done((f32[27,32,128]{2,1,0:T(8,128)S(1)}, f32[27,32,128]{2,1,0:T(8,128)S(1)}, u32[]{:S(2)}, u32[]{:S(2)}) %collective-permute-start.1) | collective-permute-done | bytes 442400 | tf_op jit(solution)/shard_map/ppermute | solution.py:609
  19.2 0.1 shard_map.157.own
  19.2 1.3 collective-permute-start.3
  20.5 4.6 %collective-permute-start.2 = (bf16[9,64,64]{2,1,0:T(8,128)(2,1)S(1)}, bf16[9,64,64]{2,1,0:T(8,128)(2,1)S(1)}, u32[]{:S(2)}, u32[]{:S(2)}) collective-permute-start(bf16[9,64,64]{2,1,0:T(8,128)(2,1)S(1)} %shard_map.157.own), channel_id=1, source_target_pairs={{0,32},{32,64},{64,96},{96,128},{128,160},{160,192},{192,224},{224... | collective-permute-start | bytes 221192 | tf_op jit(solution)/shard_map/ppermute | solution.py:608
  25.2 0.0 copy-done.4
  25.2 0.0 copy-done.3
  25.2 1.1 shard_map.158
  26.3 0.0 copy-start
  26.4 0.0 copy-start.1
  26.4 0.0 copy-start.2
  26.4 0.0 collective-permute-done.3.z_next
  26.4 0.9 collective-permute-done.2.z_prev
  27.3 3.8 %shard_map.159 = (f32[16,32,128]{2,1,0:T(8,128)}, bf16[3,192,640]{2,1,0:T(8,128)(2,1)S(1)}) custom-call(bf16[9,64,64]{2,1,0:T(8,128)(2,1)S(1)} %collective-permute-done.2.z_prev, bf16[9,64,64]{2,1,0:T(8,128)(2,1)S(1)} %shard_map.157.own, bf16[9,64,64]{2,1,0:T(8,128)(2,1)S(1)} %collective-permute-done.3.z_next, ...), custom_call_target="tpu_custom_call" | custom-call | tf_op jit(solution)/shard_map/pallas_call | solution.py:637
  31.1 13.5 %all-to-all-start = ((f32[16,32,128]{2,1,0:T(8,128)}), f32[16,32,128]{2,1,0:T(8,128)S(1)}, u32[]{:S(2)}, u32[]{:S(2)}) async-start(f32[16,32,128]{2,1,0:T(8,128)} %get-tuple-element.27.after), calls=%async_computation | async-start | bytes 524288 | tf_op jit(solution)/shard_map/all_to_all | solution.py:638
  45.2 2.5 %shard_map.160 = (f32[30,32,128]{2,1,0:T(8,128)S(1)}, f32[4,384,128]{2,1,0:T(8,128)}) custom-call(s32[1]{0:T(128)} %bitcast.place, f32[1,6,32,128]{3,2,1,0:T(8,128)} %wave_now.3, f32[1,6,32,128]{3,2,1,0:T(8,128)} %wave_prev.3, f32[1,6,32,128]{3,2,1,0:T(8,128)} %adj_next.3, f32[1,6,32,128]{3,2,1,0:T(8,128)} %adj_after.3, f32[6,32,128]{2,1,0:T(8,128)} %density.3, ...), custom_call_target="tpu_custom_call" | custom-call | tf_op jit(solution)/shard_map/pallas_call | solution.py:640
  47.7 4.7 %all-to-all-done = f32[16,32,128]{2,1,0:T(8,128)S(1)} async-done(((f32[16,32,128]{2,1,0:T(8,128)}), f32[16,32,128]{2,1,0:T(8,128)S(1)}, u32[]{:S(2)}, u32[]{:S(2)}) %all-to-all-start) | async-done | bytes 262176 | tf_op jit(solution)/shard_map/all_to_all | solution.py:638
  52.4 2.9 %shard_map.161.after = f32[16,32,128]{2,1,0:T(8,128)} custom-call(s32[1]{0:T(128)} %bitcast.place, s32[1]{0:T(128)S(6)} %copy.17.source, f32[1,3]{1,0:T(1,128)} %pulses_in.1, f32[27,32,128]{2,1,0:T(8,128)S(1)} %collective-permute-done.left, f32[27,32,128]{2,1,0:T(8,128)S(1)} %collective-permute-done.1.right, f32[512,128]{1,0:T(8,128)S(1)} %bitcast.15, ...), custom_call_target="tpu_custom_call" | custom-call | tf_op jit(solution)/shard_map/pallas_call | solution.py:641
  55.3 0.0 copy-done
  55.4 0.0 copy-done.1
  55.4 0.0 copy-done.2
  55.4 4.0 %all-to-all-start.1 = ((f32[16,32,128]{2,1,0:T(8,128)}), f32[16,32,128]{2,1,0:T(8,128)S(1)}, u32[]{:S(2)}, u32[]{:S(2)}) async-start(f32[16,32,128]{2,1,0:T(8,128)} %shard_map.161.after), calls=%async_computation.1 | async-start | bytes 524288 | tf_op jit(solution)/shard_map/all_to_all | solution.py:651
  59.3 3.3 %shard_map.162 = (f32[45,64,128]{2,1,0:T(8,128)S(1)}, bf16[384,1024]{1,0:T(8,128)(2,1)S(1)}) custom-call(bf16[3,192,640]{2,1,0:T(8,128)(2,1)S(1)} %get-tuple-element.30.lines, bf16[576,192]{1,0:T(8,128)(2,1)} %copy-done, f32[64,128]{1,0:T(8,128)} %copy-done.1, f32[64,128]{1,0:T(8,128)} %copy-done.2, bf16[27,64,64]{2,1,0:T(8,128)(2,1)} %kernel_in.3, ...), custom_call_target="tpu_custom_call" | custom-call | tf_op jit(solution)/shard_map/pallas_call | solution.py:652
  62.7 4.5 %all-to-all-done.1.received = f32[16,32,128]{2,1,0:T(8,128)S(1)} async-done(((f32[16,32,128]{2,1,0:T(8,128)}), f32[16,32,128]{2,1,0:T(8,128)S(1)}, u32[]{:S(2)}, u32[]{:S(2)}) %all-to-all-start.1) | async-done | bytes 262176 | tf_op jit(solution)/shard_map/all_to_all | solution.py:651
  67.2 2.4 %shard_map.163 = (f32[3,1,64,64]{3,2,1,0:T(8,128)}, f32[1024,128]{1,0:T(8,128)S(1)}) custom-call(f32[16,32,128]{2,1,0:T(8,128)S(1)} %all-to-all-done.1.received, f32[45,64,128]{2,1,0:T(8,128)S(1)} %get-tuple-element.31.slopes, bf16[3,192,640]{2,1,0:T(8,128)(2,1)S(1)} %get-tuple-element.30.lines, bf16[384,1024]{1,0:T(8,128)(2,1)S(1)} %get-tuple-element.32.folded), custom_call_target="tpu_custom_call" | custom-call | tf_op jit(solution)/shard_map/pallas_call | solution.py:653
  69.6 17.9 %all_to_all.30.received = f32[8,128,128]{2,1,0:T(8,128)S(1)} all-to-all(f32[8,128,128]{2,1,0:T(8,128)S(1)} %bitcast.16), channel_id=1, replica_groups=mesh['xlo'=2,'z'=8,'y'=8,'xhi'=2,'core'=2] {'xlo','xhi','core'}, dimensions={0} | all-to-all | bytes 1048576 | tf_op jit(solution)/shard_map/all_to_all | solution.py:655
  87.5 22.3 %all_to_all.31 = f32[64,2,128]{2,1,0:T(2,128)S(1)} all-to-all(f32[64,2,128]{2,1,0:T(2,128)S(1)} %bitcast.17), channel_id=1, replica_groups=mesh['xlo'=2,'z'=8,'y'=8,'xhi'=2,'core'=2] {'z','y'}, dimensions={0} | all-to-all | bytes 131072 | tf_op jit(solution)/shard_map/all_to_all | solution.py:657
  109.9 14.9 %all_to_all.32 = f32[64,2,128]{2,1,0:T(2,128)S(1)} all-to-all(f32[64,2,128]{2,1,0:T(2,128)S(1)} %bitcast.20), channel_id=1, replica_groups=mesh['xlo'=2,'z'=8,'y'=8,'xhi'=2,'core'=2] {'z','y'}, dimensions={0} | all-to-all | bytes 131072 | tf_op jit(solution)/shard_map/all_to_all | solution.py:659
  124.8 15.3 %all_to_all.33 = f32[8,128,128]{2,1,0:T(8,128)S(1)} all-to-all(f32[8,128,128]{2,1,0:T(8,128)S(1)} %shard_map.166), channel_id=1, replica_groups=mesh['xlo'=2,'z'=8,'y'=8,'xhi'=2,'core'=2] {'xlo','xhi','core'}, dimensions={0} | all-to-all | bytes 1048576 | tf_op jit(solution)/shard_map/all_to_all | solution.py:661
  140.1 1.1 shard_map.167
  (3 shorter events, 0.1 us)
Async XLA Ops:
  0.6 24.6 %copy-start.4 = (bf16[64]{0:T(256)(128)(2,1)S(1)}, bf16[64]{0:T(256)(128)(2,1)}, u32[]{:S(2)}) copy-start(bf16[64]{0:T(256)(128)(2,1)} %param.16) | copy-start | bytes 388
  0.6 24.6 %copy-start.3 = (f32[64]{0:T(128)S(1)}, f32[64]{0:T(128)}, u32[]{:S(2)}) copy-start(f32[64]{0:T(128)} %param.15) | copy-start | bytes 772
  2.0 11.3 %collective-permute-start = (f32[27,32,128]{2,1,0:T(8,128)S(1)}, f32[27,32,128]{2,1,0:T(8,128)S(1)}, u32[]{:S(2)}, u32[]{:S(2)}) collective-permute-start(f32[27,32,128]{2,1,0:T(8,128)S(1)} %get-tuple-element.21), channel_id=1, source_target_pairs={{0,1},{1,2},{2,3},{3,4},{4,5},{5,6},{6,7},{7,8},{8,9},{9,10},{10,1... | collective-permute-start | bytes 1327112 | tf_op jit(solution)/shard_map/ppermute | solution.py:608
  8.0 11.1 %collective-permute-start.1 = (f32[27,32,128]{2,1,0:T(8,128)S(1)}, f32[27,32,128]{2,1,0:T(8,128)S(1)}, u32[]{:S(2)}, u32[]{:S(2)}) collective-permute-start(f32[27,32,128]{2,1,0:T(8,128)S(1)} %get-tuple-element.22), channel_id=1, source_target_pairs={{1,0},{2,1},{3,2},{4,3},{5,4},{6,5},{7,6},{8,7},{9,8},{10,9},{11,1... | collective-permute-start | bytes 1327112 | tf_op jit(solution)/shard_map/ppermute | solution.py:609
  19.2 7.1 %collective-permute-start.3 = (bf16[9,64,64]{2,1,0:T(8,128)(2,1)S(1)}, bf16[9,64,64]{2,1,0:T(8,128)(2,1)S(1)}, u32[]{:S(2)}, u32[]{:S(2)}) collective-permute-start(bf16[9,64,64]{2,1,0:T(8,128)(2,1)S(1)} %shard_map.157.own), channel_id=1, source_target_pairs={{32,0},{64,32},{96,64},{128,96},{160,128},{192,160},{224,192},{256... | collective-permute-start | bytes 221192 | tf_op jit(solution)/shard_map/ppermute | solution.py:609
  20.5 6.7 %collective-permute-start.2 = (bf16[9,64,64]{2,1,0:T(8,128)(2,1)S(1)}, bf16[9,64,64]{2,1,0:T(8,128)(2,1)S(1)}, u32[]{:S(2)}, u32[]{:S(2)}) collective-permute-start(bf16[9,64,64]{2,1,0:T(8,128)(2,1)S(1)} %shard_map.157.own), channel_id=1, source_target_pairs={{0,32},{32,64},{64,96},{96,128},{128,160},{160,192},{192,224},{224... | collective-permute-start | bytes 221192 | tf_op jit(solution)/shard_map/ppermute | solution.py:608
  26.3 29.0 %copy-start = (bf16[576,192]{1,0:T(8,128)(2,1)}, bf16[576,192]{1,0:T(8,128)(2,1)S(1)}, u32[]{:S(2)}) copy-start(bf16[576,192]{1,0:T(8,128)(2,1)S(1)} %get-tuple-element.24.wall.wall_in) | copy-start | bytes 663556
  26.4 29.0 %copy-start.1 = (f32[64,128]{1,0:T(8,128)}, f32[64,128]{1,0:T(8,128)S(1)}, u32[]{:S(2)}) copy-start(f32[64,128]{1,0:T(8,128)S(1)} %get-tuple-element.25.bias.bias_in) | copy-start | bytes 98308
  26.4 29.0 %copy-start.2 = (f32[64,128]{1,0:T(8,128)}, f32[64,128]{1,0:T(8,128)S(1)}, u32[]{:S(2)}) copy-start(f32[64,128]{1,0:T(8,128)S(1)} %get-tuple-element.26.head.head_in) | copy-start | bytes 98308
  31.1 21.4 %all-to-all-start = ((f32[16,32,128]{2,1,0:T(8,128)}), f32[16,32,128]{2,1,0:T(8,128)S(1)}, u32[]{:S(2)}, u32[]{:S(2)}) async-start(f32[16,32,128]{2,1,0:T(8,128)} %get-tuple-element.27.after), calls=%async_computation | async-start | bytes 524288 | tf_op jit(solution)/shard_map/all_to_all | solution.py:638
  55.4 11.8 %all-to-all-start.1 = ((f32[16,32,128]{2,1,0:T(8,128)}), f32[16,32,128]{2,1,0:T(8,128)S(1)}, u32[]{:S(2)}, u32[]{:S(2)}) async-start(f32[16,32,128]{2,1,0:T(8,128)} %shard_map.161.after), calls=%async_computation.1 | async-start | bytes 524288 | tf_op jit(solution)/shard_map/all_to_all | solution.py:651

commit v4 on v3

--- a/solution.py
+++ b/solution.py
@@ -8,8 +8,7 @@
 
 SHOT = ("xlo", "z")
 TILE = ("y", "xhi", "core")
-NEAR = ("xlo", "xhi", "core")
-FAR = ("z", "y")
+NEAR = ("xlo", "z", "xhi", "core")
 F32 = jnp.float32
 BF16 = jnp.bfloat16
 courant = 0.005
@@ -64,22 +63,13 @@
         copies.append(pltpu.make_async_copy(field.at[pl.ds(6 - rows, rows)], to_next.at[here], sems.at[i]))
         copies.append(pltpu.make_async_copy(field.at[pl.ds(0, rows)], to_prev.at[here], sems.at[5 + i]))
         at += rows
-    start_all(copies)
-    copies[0].wait()
-    for x in range(3):
-        block = coarse[x].astype(F32)
-        packed = jnp.concatenate([block[0:32], block[32:64]], axis=1)
-        to_next[24 + x] = packed
-        to_prev[24 + x] = packed
-    wait_all(copies[1:])
-
-
-def join_kernel(left, coarse, right, out):
-    for i, ref in ((0, left), (2, right)):
+    wait_all(start_all(copies))
+
+
+def join_kernel(low, middle, high, out):
+    for i, ref in enumerate((low, middle, high)):
         for x in range(3):
-            packed = ref[24 + x]
-            out[3 * i + x] = jnp.concatenate([packed[:, :64], packed[:, 64:]], axis=0).astype(BF16)
-    out[3:6] = coarse[...]
+            out[3 * i + x] = jnp.concatenate([ref[x, 0:32], ref[x, 32:64]], axis=1)
 
 
 def taps_kernel(kernel_in, bias, head, wall, bias_wide, head_wide, kernel, sem):
@@ -130,7 +120,9 @@
 ):
     spread = spread_matrix()
     for zi, ref in enumerate((z_prev, own, z_next)):
-        fine = jnp.dot(ref[...].reshape(576, 64), spread, preferred_element_type=F32).astype(BF16)
+        packed = [ref[x] for x in range(9)]
+        rows = jnp.concatenate([half for p in packed for half in (p[:, :64], p[:, 64:])], axis=0)
+        fine = jnp.dot(rows, spread, preferred_element_type=F32).astype(BF16)
         for x in range(9):
             for e in range(3):
                 piece = fine[64 * x : 64 * x + 64, 128 * e : 128 * e + 128]
@@ -237,6 +229,8 @@
     receivers_in,
     observed_in,
     after,
+    left,
+    right,
     own,
     counts_out,
     counts,
@@ -454,36 +448,23 @@
 
 def sum_kernel(received, out):
     total = received[0]
-    for s in range(1, 8):
+    for s in range(1, received.shape[0]):
         total = total + received[s]
-    out[...] = total
-
-
-def sum_pairs_kernel(received, out):
-    total = received[0:8, :]
-    for s in range(1, 16):
-        total = total + received[8 * s : 8 * s + 8, :]
-    pair = total[0:2] + total[2:4] + total[4:6] + total[6:8]
-    pairs = jnp.concatenate([pair] * 4, axis=0)
-    for s in range(16):
-        out[8 * s : 8 * s + 8, :] = pairs
-
-
-def repeat_kernel(chunk, out):
-    for s in range(8):
-        out[s] = chunk[...]
+    total = total.astype(out.dtype)
+    for s in range(out.shape[0]):
+        out[s] = total
 
 
 def unpack_kernel(rows, kernel_out, head_out, bias_out):
     for tap in range(9):
         at = 96 * tap
-        pair = rows[at : at + 64, :]
+        pair = rows[at : at + 64, :].astype(F32)
         kernel_out[3 * tap] = pair[:, :64]
         kernel_out[3 * tap + 1] = pair[:, 64:]
-        last = rows[at + 64 : at + 96, :]
+        last = rows[at + 64 : at + 96, :].astype(F32)
         kernel_out[3 * tap + 2, 0:32] = last[:, :64]
         kernel_out[3 * tap + 2, 32:64] = last[:, 64:]
-    row = rows[864:865, :]
+    row = rows[864:880, :].astype(F32)[0:1]
     head_out[...] = row[:, :64]
     bias_out[...] = row[:, 64:]
 
@@ -498,7 +479,7 @@
 SMEM = pl.BlockSpec(memory_space=pltpu.SMEM)
 
 
-def call(kernel, out_shape, in_specs, scratch=(), megabytes=8):
+def call(kernel, out_shape, in_specs, scratch=(), megabytes=8, flops=None):
     outs = out_shape if isinstance(out_shape, tuple) else (out_shape,)
     specs = tuple(HBM if hasattr(out, "memory_space") else VMEM for out in outs)
     return pl.pallas_call(
@@ -508,18 +489,19 @@
         out_specs=specs if isinstance(out_shape, tuple) else VMEM,
         scratch_shapes=list(scratch),
         compiler_params=pltpu.CompilerParams(vmem_limit_bytes=megabytes << 20),
+        cost_estimate=flops and pl.CostEstimate(flops=flops, bytes_accessed=0, transcendentals=0),
     )
 
 
 FIELD = pltpu.VMEM((18, 32, 128), F32)
 pack = call(
     pack_kernel,
-    (shape((27, 32, 128)), shape((27, 32, 128)), shape((3, 64, 64), BF16)),
+    (shape((24, 32, 128)), shape((24, 32, 128)), shape((3, 64, 64), BF16)),
     [HBM] * 6,
     [pltpu.SemaphoreType.DMA((11,))],
     4,
 )
-join = call(join_kernel, shape((9, 64, 64), BF16), [VMEM] * 3, (), 4)
+join = call(join_kernel, shape((9, 32, 128), BF16), [VMEM] * 3, (), 2)
 widen = call(
     taps_kernel,
     (shape((576, 192), BF16), shape((64, 128)), shape((64, 128))),
@@ -537,6 +519,7 @@
         pltpu.VMEM((32, 128), F32),
     ],
     14,
+    500_000_000,
 )
 slopes = call(
     slopes_kernel,
@@ -555,7 +538,7 @@
 medium = call(
     medium_kernel,
     (shape((30, 32, 128)), pltpu.HBM((4, 384, 128), F32)),
-    [SMEM] + [HBM] * 7 + [ANY],
+    [SMEM] + [HBM] * 7 + [ANY] * 3,
     [
         pltpu.VMEM((4, 384, 128), F32),
         pltpu.VMEM((1, 128), jnp.int32),
@@ -563,6 +546,7 @@
         pltpu.SemaphoreType.DMA((8,)),
     ],
     8,
+    2_000_000_000,
 )
 waves = call(
     wave_kernel,
@@ -628,16 +612,21 @@
     place = lax.axis_index(TILE).astype(jnp.int32).reshape(1)
     fields = [in_hbm(f) for f in (wave_now, wave_prev, adjoint_next, adjoint_after, density)]
     taps = in_hbm(kernel)
-    to_next, to_prev, coarse = pack(*fields, in_hbm(latent.reshape(3, 64, 64)))
+    coarse = latent.reshape(3, 64, 64)
+    low, high = shifted((coarse, coarse), TILE, 32)
+    to_next, to_prev, middle = pack(*fields, in_hbm(coarse))
+    wall, bias, head = widen(taps, conv_bias.reshape(1, 64), head_weight.reshape(1, 64))
+    nine = join(low, middle, high)
+    z_prev, z_next = shifted((nine, nine), SHOT, 16)
+    to_next, to_prev, nine = lax.optimization_barrier((to_next, to_prev, nine))
     left, right = shifted((to_next, to_prev), TILE, 32)
-    wall, bias, head = widen(taps, conv_bias.reshape(1, 64), head_weight.reshape(1, 64))
-    nine = join(left, coarse, right)
-    z_prev, z_next = shifted((nine, nine), SHOT, 16)
 
     speed, lines = decode(z_prev, nine, z_next, wall, bias, head)
     speeds = lax.all_to_all(speed, SHOT, 0, 0, tiled=True)
     records = jnp.transpose(observed, (1, 0, 2))
-    own, counts = medium(place, *fields, in_hbm(receiver_cells), in_hbm(records), in_hbm(speed))
+    own, counts = medium(
+        place, *fields, in_hbm(receiver_cells), in_hbm(records), in_hbm(speed), left, right
+    )
     strips = waves(
         place,
         source_cell,
@@ -652,13 +641,11 @@
     slope, folded = slopes(lines, in_hbm(wall), in_hbm(bias), in_hbm(head), taps, in_hbm(strips))
     latent_grad, parts = backward(received, slope, lines, folded)
 
-    chunks = lax.all_to_all(parts.reshape(8, 128, 128), NEAR, 0, 0, tiled=True)
-    chunk = call(sum_kernel, shape((128, 128)), [VMEM])(chunks)
-    pairs = lax.all_to_all(chunk.reshape(64, 2, 128), FAR, 0, 0, tiled=True)
-    pairs = call(sum_pairs_kernel, shape((128, 128)), [VMEM])(pairs.reshape(128, 128))
-    chunk = lax.all_to_all(pairs.reshape(64, 2, 128), FAR, 0, 0, tiled=True)
-    chunks = call(repeat_kernel, shape((8, 128, 128)), [VMEM])(chunk.reshape(128, 128))
-    whole = lax.all_to_all(chunks, NEAR, 0, 0, tiled=True)
+    pieces = lax.all_to_all(parts.reshape(64, 16, 128), NEAR, 0, 0, tiled=True)
+    pieces = call(sum_kernel, shape((8, 16, 128)), [VMEM])(pieces)
+    pieces = lax.all_to_all(pieces, "y", 0, 0, tiled=True)
+    pieces = call(sum_kernel, shape((64, 16, 128), BF16), [VMEM])(pieces)
+    whole = lax.all_to_all(pieces, NEAR, 0, 0, tiled=True)
     kernel_grad, head_grad, bias_grad = call(
         unpack_kernel, (shape((27, 64, 64)), shape((1, 64)), shape((1, 64))), [VMEM]
     )(whole.reshape(1024, 128))

time: 142 us -> 135 us (0.951)
  waiting for transfers between devices: 17.2 us -> 9.97 us
  blocking collectives: 70.4 us -> 65.4 us
  starting transfers between devices: 33.5 us -> 37.6 us
    ppermute x2 -> x3, starting transfers between devices: 5.35 us -> 12 us  [shifted(): high = lax.ppermute(block[1], axes, [(i + 1, i) for i in range(size - 1)])]
    ppermute x2 -> x3, waiting for transfers between devices: 5.9 us -> 0.01 us  [shifted(): high = lax.ppermute(block[1], axes, [(i + 1, i) for i in range(size - 1)])]
    all_to_all x4 -> x3, blocking collectives: 70.4 us -> 65.4 us  [the longest x1 30.9 us: per_device(): pieces = lax.all_to_all(parts.reshape(64, 16, 128), NEAR, 0, 0, tiled=True)]
    all_to_all x1, starting transfers between devices: 13.5 us -> 9.51 us  [per_device(): speeds = lax.all_to_all(speed, SHOT, 0, 0, tiled=True)]
    ppermute x2 -> x3, waiting for transfers between devices: 2.03 us -> 0.14 us  [shifted(): low = lax.ppermute(block[0], axes, [(i, i + 1) for i in range(size - 1)])]
    ppermute x2 -> x3, starting transfers between devices: 10.7 us -> 12.1 us  [shifted(): low = lax.ppermute(block[0], axes, [(i, i + 1) for i in range(size - 1)])]
  transfers between devices with their start and end apart: 6 -> 8, of which waited for: 5 -> 3; matrix products, arithmetic and copies ran while one was open for 0% -> 0% of each run, Pallas kernels for 5% -> 9%
where the time goes in v4:
time: 135 us; the launch traced here: 134 us
  blocking collectives  65.4 us (48%)
  starting transfers between devices  37.6 us (28%)
  Pallas kernels  18.6 us (14%)
  waiting for transfers between devices  9.97 us (7%)
  between operations  1.49 us (1%)
    all_to_all x1, blocking collectives, per_device(): pieces = lax.all_to_all(parts.reshape(64, 16, 128), NEAR, 0, 0, tiled=True)  30.9 us
    all_to_all x1, blocking collectives, per_device(): whole = lax.all_to_all(pieces, NEAR, 0, 0, tiled=True)  20.6 us
    all_to_all x1, blocking collectives, per_device(): pieces = lax.all_to_all(pieces, 'y', 0, 0, tiled=True)  13.9 us
    ppermute x3, starting transfers between devices, shifted(): low = lax.ppermute(block[0], axes, [(i, i + 1) for i in range(size - 1)])  12.1 us
    ppermute x3, starting transfers between devices, shifted(): high = lax.ppermute(block[1], axes, [(i + 1, i) for i in range(size - 1)])  12 us
    all_to_all x1, starting transfers between devices, per_device(): speeds = lax.all_to_all(speed, SHOT, 0, 0, tiled=True)  9.51 us
    all_to_all x1, waiting for transfers between devices, per_device(): received = lax.all_to_all(strips, SHOT, 0, 0, tiled=True)  5.12 us
    all_to_all x1, waiting for transfers between devices, per_device(): speeds = lax.all_to_all(speed, SHOT, 0, 0, tiled=True)  4.7 us
  transfers between devices with their start and end apart: 8, of which 3 were waited for; matrix products, arithmetic and copies ran while one was open for 0% of the time, Pallas kernels for 9%

profile of v4, /device:TPU:1, one launch (start us, length us, event | category | flops | bytes accessed | tf_op | source)
XLA Modules:
  0.0 134.3 jit_solution(4367726034831779393)
XLA Ops:
  0.6 8.8 %collective-permute-start.1 = (bf16[3,64,64]{2,1,0:T(8,128)(2,1)}, bf16[3,64,64]{2,1,0:T(8,128)(2,1)S(1)}, u32[]{:S(2)}, u32[]{:S(2)}) collective-permute-start(bf16[3,64,64]{2,1,0:T(8,128)(2,1)} %bitcast.15), channel_id=1, source_target_pairs={{1,0},{2,1},{3,2},{4,3},{5,4},{6,5},{7,6},{8,7},{9,8},{10,9},{11,1... | collective-permute-start | bytes 73736 | tf_op jit(solution)/shard_map/ppermute | solution.py:593
  9.4 1.9 %collective-permute-start = (bf16[3,64,64]{2,1,0:T(8,128)(2,1)}, bf16[3,64,64]{2,1,0:T(8,128)(2,1)S(1)}, u32[]{:S(2)}, u32[]{:S(2)}) collective-permute-start(bf16[3,64,64]{2,1,0:T(8,128)(2,1)} %bitcast.16), channel_id=1, source_target_pairs={{0,1},{1,2},{2,3},{3,4},{4,5},{5,6},{6,7},{7,8},{8,9},{9,10},{10,1... | collective-permute-start | bytes 73736 | tf_op jit(solution)/shard_map/ppermute | solution.py:592
  11.4 1.3 shard_map.156
  12.7 0.0 collective-permute-done.1.high
  12.7 0.1 collective-permute-done.low
  12.8 0.1 shard_map.157.own
  12.9 1.3 collective-permute-start.5
  14.2 4.0 %collective-permute-start.4 = (bf16[9,32,128]{2,1,0:T(8,128)(2,1)S(1)}, bf16[9,32,128]{2,1,0:T(8,128)(2,1)S(1)}, u32[]{:S(2)}, u32[]{:S(2)}) collective-permute-start(bf16[9,32,128]{2,1,0:T(8,128)(2,1)S(1)} %shard_map.157.own), channel_id=1, source_target_pairs={{0,32},{32,64},{64,96},{96,128},{128,160},{160,192},{192,224},{224... | collective-permute-start | bytes 221192 | tf_op jit(solution)/shard_map/ppermute | solution.py:592
  18.2 6.2 %collective-permute-start.2 = (f32[24,32,128]{2,1,0:T(8,128)S(1)}, f32[24,32,128]{2,1,0:T(8,128)S(1)}, u32[]{:S(2)}, u32[]{:S(2)}) collective-permute-start(f32[24,32,128]{2,1,0:T(8,128)S(1)} %get-tuple-element.27), channel_id=1, source_target_pairs={{0,1},{1,2},{2,3},{3,4},{4,5},{5,6},{6,7},{7,8},{8,9},{9,10},{10,1... | collective-permute-start | bytes 1179656 | tf_op jit(solution)/shard_map/ppermute | solution.py:592
  24.4 1.9 %collective-permute-start.3 = (f32[24,32,128]{2,1,0:T(8,128)S(1)}, f32[24,32,128]{2,1,0:T(8,128)S(1)}, u32[]{:S(2)}, u32[]{:S(2)}) collective-permute-start(f32[24,32,128]{2,1,0:T(8,128)S(1)} %get-tuple-element.28), channel_id=1, source_target_pairs={{1,0},{2,1},{3,2},{4,3},{5,4},{6,5},{7,6},{8,7},{9,8},{10,9},{11,1... | collective-permute-start | bytes 1179656 | tf_op jit(solution)/shard_map/ppermute | solution.py:593
  26.4 0.0 copy-start.3
  26.4 0.6 copy-done.3
  27.0 0.0 copy-start.4
  27.0 0.7 copy-done.4
  27.7 1.1 shard_map.158
  28.8 0.0 copy-start.1
  28.8 0.0 copy-start.2
  28.8 0.0 copy-start
  28.8 0.0 collective-permute-done.5.z_next
  28.8 0.0 collective-permute-done.4.z_prev
  28.9 3.8 %shard_map.159 = (f32[16,32,128]{2,1,0:T(8,128)}, bf16[3,192,640]{2,1,0:T(8,128)(2,1)S(1)}) custom-call(bf16[9,32,128]{2,1,0:T(8,128)(2,1)S(1)} %collective-permute-done.4.z_prev, bf16[9,32,128]{2,1,0:T(8,128)(2,1)S(1)} %shard_map.157.own, bf16[9,32,128]{2,1,0:T(8,128)(2,1)S(1)} %collective-permute-done.5.z_next, ...), custom_call_target="tpu_custom_call" | custom-call | flops 500000000 | tf_op jit(solution)/shard_map/pallas_call | solution.py:624
  32.7 0.0 copy-done.1
  32.7 0.0 copy-done.2
  32.7 9.5 %all-to-all-start = ((f32[16,32,128]{2,1,0:T(8,128)}), f32[16,32,128]{2,1,0:T(8,128)S(1)}, u32[]{:S(2)}, u32[]{:S(2)}) async-start(f32[16,32,128]{2,1,0:T(8,128)} %get-tuple-element.33.after), calls=%async_computation | async-start | bytes 524288 | tf_op jit(solution)/shard_map/all_to_all | solution.py:625
  42.9 0.0 collective-permute-done.2.left
  42.9 0.0 collective-permute-done.3.right
  42.9 2.5 %shard_map.160 = (f32[30,32,128]{2,1,0:T(8,128)S(1)}, f32[4,384,128]{2,1,0:T(8,128)}) custom-call(s32[1]{0:T(128)} %bitcast.place, f32[1,6,32,128]{3,2,1,0:T(8,128)} %wave_now.3, f32[1,6,32,128]{3,2,1,0:T(8,128)} %wave_prev.3, f32[1,6,32,128]{3,2,1,0:T(8,128)} %adj_next.3, f32[1,6,32,128]{3,2,1,0:T(8,128)} %adj_after.3, f32[6,32,128]{2,1,0:T(8,128)} %density.3, ...), custom_call_target="tpu_custom_call" | custom-call | flops 2000000000 | tf_op jit(solution)/shard_map/pallas_call | solution.py:627
  45.4 0.0 copy-done
  45.4 4.7 %all-to-all-done = f32[16,32,128]{2,1,0:T(8,128)S(1)} async-done(((f32[16,32,128]{2,1,0:T(8,128)}), f32[16,32,128]{2,1,0:T(8,128)S(1)}, u32[]{:S(2)}, u32[]{:S(2)}) %all-to-all-start) | async-done | bytes 262176 | tf_op jit(solution)/shard_map/all_to_all | solution.py:625
  50.1 2.9 %shard_map.161.after = f32[16,32,128]{2,1,0:T(8,128)} custom-call(s32[1]{0:T(128)} %bitcast.place, s32[1]{0:T(128)S(6)} %copy.17.source, f32[1,3]{1,0:T(1,128)} %pulses_in.1, f32[24,32,128]{2,1,0:T(8,128)S(1)} %collective-permute-done.2.left, f32[24,32,128]{2,1,0:T(8,128)S(1)} %collective-permute-done.3.right, f32[512,128]{1,0:T(8,128)S(1)} %bitcast.11, ...), custom_call_target="tpu_custom_call" | custom-call | tf_op jit(solution)/shard_map/pallas_call | solution.py:630
  53.0 4.0 %all-to-all-start.1 = ((f32[16,32,128]{2,1,0:T(8,128)}), f32[16,32,128]{2,1,0:T(8,128)S(1)}, u32[]{:S(2)}, u32[]{:S(2)}) async-start(f32[16,32,128]{2,1,0:T(8,128)} %shard_map.161.after), calls=%async_computation.1 | async-start | bytes 524288 | tf_op jit(solution)/shard_map/all_to_all | solution.py:640
  57.0 3.3 %shard_map.162 = (f32[45,64,128]{2,1,0:T(8,128)S(1)}, bf16[384,1024]{1,0:T(8,128)(2,1)S(1)}) custom-call(bf16[3,192,640]{2,1,0:T(8,128)(2,1)S(1)} %get-tuple-element.36.lines, bf16[576,192]{1,0:T(8,128)(2,1)} %copy-done, f32[64,128]{1,0:T(8,128)} %copy-done.1, f32[64,128]{1,0:T(8,128)} %copy-done.2, bf16[27,64,64]{2,1,0:T(8,128)(2,1)} %kernel_in.3, ...), custom_call_target="tpu_custom_call" | custom-call | tf_op jit(solution)/shard_map/pallas_call | solution.py:641
  60.3 5.1 %all-to-all-done.1.received = f32[16,32,128]{2,1,0:T(8,128)S(1)} async-done(((f32[16,32,128]{2,1,0:T(8,128)}), f32[16,32,128]{2,1,0:T(8,128)S(1)}, u32[]{:S(2)}, u32[]{:S(2)}) %all-to-all-start.1) | async-done | bytes 262176 | tf_op jit(solution)/shard_map/all_to_all | solution.py:640
  65.4 2.4 %shard_map.163 = (f32[3,1,64,64]{3,2,1,0:T(8,128)}, f32[1024,128]{1,0:T(8,128)S(1)}) custom-call(f32[16,32,128]{2,1,0:T(8,128)S(1)} %all-to-all-done.1.received, f32[45,64,128]{2,1,0:T(8,128)S(1)} %get-tuple-element.37.slopes, bf16[3,192,640]{2,1,0:T(8,128)(2,1)S(1)} %get-tuple-element.36.lines, bf16[384,1024]{1,0:T(8,128)(2,1)S(1)} %get-tuple-element.38.folded), custom_call_target="tpu_custom_call" | custom-call | tf_op jit(solution)/shard_map/pallas_call | solution.py:642
  67.8 30.9 %all_to_all.25.received = f32[64,16,128]{2,1,0:T(8,128)S(1)} all-to-all(f32[64,16,128]{2,1,0:T(8,128)S(1)} %bitcast.12), channel_id=1, replica_groups=mesh['xlo'=2,'z'=8,'y'=8,'xhi'=2,'core'=2] {'xlo','z','xhi','core'}, dimensions={0} | all-to-all | bytes 1048576 | tf_op jit(solution)/shard_map/all_to_all | solution.py:644
  98.8 0.1 shard_map.164
  98.8 13.9 %all_to_all.26.received = f32[8,16,128]{2,1,0:T(8,128)S(1)} all-to-all(f32[8,16,128]{2,1,0:T(8,128)S(1)} %shard_map.164), channel_id=1, replica_groups=mesh['xlo'=2,'z'=8,'y'=8,'xhi'=2,'core'=2] {'y'}, dimensions={0} | all-to-all | bytes 131072 | tf_op jit(solution)/shard_map/all_to_all | solution.py:646
  112.7 20.6 %all_to_all.27 = bf16[64,16,128]{2,1,0:T(8,128)(2,1)S(1)} all-to-all(bf16[64,16,128]{2,1,0:T(8,128)(2,1)S(1)} %shard_map.165), channel_id=1, replica_groups=mesh['xlo'=2,'z'=8,'y'=8,'xhi'=2,'core'=2] {'xlo','z','xhi','core'}, dimensions={0} | all-to-all | bytes 524288 | tf_op jit(solution)/shard_map/all_to_all | solution.py:648
  133.3 1.0 shard_map.166
  (1 shorter events, 0.0 us)
Async XLA Ops:
  0.6 12.0 %collective-permute-start.1 = (bf16[3,64,64]{2,1,0:T(8,128)(2,1)}, bf16[3,64,64]{2,1,0:T(8,128)(2,1)S(1)}, u32[]{:S(2)}, u32[]{:S(2)}) collective-permute-start(bf16[3,64,64]{2,1,0:T(8,128)(2,1)} %bitcast.15), channel_id=1, source_target_pairs={{1,0},{2,1},{3,2},{4,3},{5,4},{6,5},{7,6},{8,7},{9,8},{10,9},{11,1... | collective-permute-start | bytes 73736 | tf_op jit(solution)/shard_map/ppermute | solution.py:593
  9.4 3.4 %collective-permute-start = (bf16[3,64,64]{2,1,0:T(8,128)(2,1)}, bf16[3,64,64]{2,1,0:T(8,128)(2,1)S(1)}, u32[]{:S(2)}, u32[]{:S(2)}) collective-permute-start(bf16[3,64,64]{2,1,0:T(8,128)(2,1)} %bitcast.16), channel_id=1, source_target_pairs={{0,1},{1,2},{2,3},{3,4},{4,5},{5,6},{6,7},{7,8},{8,9},{9,10},{10,1... | collective-permute-start | bytes 73736 | tf_op jit(solution)/shard_map/ppermute | solution.py:592
  12.9 15.9 %collective-permute-start.5 = (bf16[9,32,128]{2,1,0:T(8,128)(2,1)S(1)}, bf16[9,32,128]{2,1,0:T(8,128)(2,1)S(1)}, u32[]{:S(2)}, u32[]{:S(2)}) collective-permute-start(bf16[9,32,128]{2,1,0:T(8,128)(2,1)S(1)} %shard_map.157.own), channel_id=1, source_target_pairs={{32,0},{64,32},{96,64},{128,96},{160,128},{192,160},{224,192},{256... | collective-permute-start | bytes 221192 | tf_op jit(solution)/shard_map/ppermute | solution.py:593
  14.2 14.6 %collective-permute-start.4 = (bf16[9,32,128]{2,1,0:T(8,128)(2,1)S(1)}, bf16[9,32,128]{2,1,0:T(8,128)(2,1)S(1)}, u32[]{:S(2)}, u32[]{:S(2)}) collective-permute-start(bf16[9,32,128]{2,1,0:T(8,128)(2,1)S(1)} %shard_map.157.own), channel_id=1, source_target_pairs={{0,32},{32,64},{64,96},{96,128},{128,160},{160,192},{192,224},{224... | collective-permute-start | bytes 221192 | tf_op jit(solution)/shard_map/ppermute | solution.py:592
  18.2 24.7 %collective-permute-start.2 = (f32[24,32,128]{2,1,0:T(8,128)S(1)}, f32[24,32,128]{2,1,0:T(8,128)S(1)}, u32[]{:S(2)}, u32[]{:S(2)}) collective-permute-start(f32[24,32,128]{2,1,0:T(8,128)S(1)} %get-tuple-element.27), channel_id=1, source_target_pairs={{0,1},{1,2},{2,3},{3,4},{4,5},{5,6},{6,7},{7,8},{8,9},{9,10},{10,1... | collective-permute-start | bytes 1179656 | tf_op jit(solution)/shard_map/ppermute | solution.py:592
  24.4 18.5 %collective-permute-start.3 = (f32[24,32,128]{2,1,0:T(8,128)S(1)}, f32[24,32,128]{2,1,0:T(8,128)S(1)}, u32[]{:S(2)}, u32[]{:S(2)}) collective-permute-start(f32[24,32,128]{2,1,0:T(8,128)S(1)} %get-tuple-element.28), channel_id=1, source_target_pairs={{1,0},{2,1},{3,2},{4,3},{5,4},{6,5},{7,6},{8,7},{9,8},{10,9},{11,1... | collective-permute-start | bytes 1179656 | tf_op jit(solution)/shard_map/ppermute | solution.py:593
  26.4 0.7 copy-start.3
  27.0 0.7 copy-start.4
  28.8 3.9 %copy-start.1 = (f32[64,128]{1,0:T(8,128)}, f32[64,128]{1,0:T(8,128)S(1)}, u32[]{:S(2)}) copy-start(f32[64,128]{1,0:T(8,128)S(1)} %get-tuple-element.31.bias.bias_in) | copy-start | bytes 98308
  28.8 3.9 %copy-start.2 = (f32[64,128]{1,0:T(8,128)}, f32[64,128]{1,0:T(8,128)S(1)}, u32[]{:S(2)}) copy-start(f32[64,128]{1,0:T(8,128)S(1)} %get-tuple-element.32.head.head_in) | copy-start | bytes 98308
  28.8 16.6 %copy-start = (bf16[576,192]{1,0:T(8,128)(2,1)}, bf16[576,192]{1,0:T(8,128)(2,1)S(1)}, u32[]{:S(2)}) copy-start(bf16[576,192]{1,0:T(8,128)(2,1)S(1)} %get-tuple-element.30.wall.wall_in) | copy-start | bytes 663556
  32.7 17.4 %all-to-all-start = ((f32[16,32,128]{2,1,0:T(8,128)}), f32[16,32,128]{2,1,0:T(8,128)S(1)}, u32[]{:S(2)}, u32[]{:S(2)}) async-start(f32[16,32,128]{2,1,0:T(8,128)} %get-tuple-element.33.after), calls=%async_computation | async-start | bytes 524288 | tf_op jit(solution)/shard_map/all_to_all | solution.py:625
  53.0 12.4 %all-to-all-start.1 = ((f32[16,32,128]{2,1,0:T(8,128)}), f32[16,32,128]{2,1,0:T(8,128)S(1)}, u32[]{:S(2)}, u32[]{:S(2)}) async-start(f32[16,32,128]{2,1,0:T(8,128)} %shard_map.161.after), calls=%async_computation.1 | async-start | bytes 524288 | tf_op jit(solution)/shard_map/all_to_all | solution.py:640

commit v5 on v4

--- a/solution.py
+++ b/solution.py
@@ -52,9 +52,28 @@
 
 
 def pack_kernel(
-    wave_now, wave_prev, adj_next, adj_after, density, latent, to_next, to_prev, coarse, sems
+    wave_now,
+    wave_prev,
+    adj_next,
+    adj_after,
+    density,
+    latent,
+    kernel_in,
+    bias,
+    head,
+    to_next,
+    to_prev,
+    coarse,
+    wall,
+    bias_wide,
+    head_wide,
+    kernel,
+    sems,
 ):
-    copies = [pltpu.make_async_copy(latent, coarse, sems.at[10])]
+    copies = [
+        pltpu.make_async_copy(kernel_in, kernel, sems.at[11]),
+        pltpu.make_async_copy(latent, coarse, sems.at[10]),
+    ]
     fields = ((wave_now, 6), (wave_prev, 5), (adj_next, 4), (adj_after, 3), (density, 6))
     at = 0
     for i, (ref, rows) in enumerate(fields):
@@ -63,23 +82,22 @@
         copies.append(pltpu.make_async_copy(field.at[pl.ds(6 - rows, rows)], to_next.at[here], sems.at[i]))
         copies.append(pltpu.make_async_copy(field.at[pl.ds(0, rows)], to_prev.at[here], sems.at[5 + i]))
         at += rows
-    wait_all(start_all(copies))
+    start_all(copies)
+    bias_wide[...] = jnp.broadcast_to(bias[...], (128, 64)).T
+    head_wide[...] = jnp.broadcast_to(head[...].astype(F32), (128, 64)).T
+    copies[0].wait()
+    for a in range(3):
+        for b in range(3):
+            at = 64 * (3 * b + a)
+            taps = [kernel[9 * a + 3 * b + e] for e in range(3)]
+            wall[at : at + 64, :] = jnp.concatenate(taps, axis=1)
+    wait_all(copies[1:])
 
 
 def join_kernel(low, middle, high, out):
     for i, ref in enumerate((low, middle, high)):
         for x in range(3):
             out[3 * i + x] = jnp.concatenate([ref[x, 0:32], ref[x, 32:64]], axis=1)
-
-
-def taps_kernel(kernel_in, bias, head, wall, bias_wide, head_wide, kernel, sem):
-    copy = pltpu.make_async_copy(kernel_in, kernel, sem)
-    copy.start()
-    bias_wide[...] = jnp.broadcast_to(bias[...], (128, 64)).T
-    head_wide[...] = jnp.broadcast_to(head[...].astype(F32), (128, 64)).T
-    copy.wait()
-    for j in range(9):
-        wall[64 * j : 64 * j + 64, :] = jnp.concatenate([kernel[3 * j + e] for e in range(3)], axis=1)
 
 
 def fold_taps(kernel, folded):
@@ -110,14 +128,12 @@
             total = None
             for b in range(3):
                 zi = Z_LINE[zz][b]
-                term = product[64 * (3 * a + b) : 64 * (3 * a + b) + 64, 128 * zi : 128 * zi + 128]
+                term = product[64 * (3 * b + a) : 64 * (3 * b + a) + 64, 128 * zi : 128 * zi + 128]
                 total = term if total is None else total + term
             store(a, zz, total)
 
 
-def decode_kernel(
-    z_prev, own, z_next, wall, bias, head, speed_out, lines_out, lines, sums, row_logit
-):
+def decode_kernel(z_prev, own, z_next, wall, bias, head, speed_out, lines_out, lines, sums, row_logit):
     spread = spread_matrix()
     for zi, ref in enumerate((z_prev, own, z_next)):
         packed = [ref[x] for x in range(9)]
@@ -126,20 +142,22 @@
         for x in range(9):
             for e in range(3):
                 piece = fine[64 * x : 64 * x + 64, 128 * e : 128 * e + 128]
-                lines[x, 64 * e : 64 * e + 64, 128 * zi : 128 * zi + 128] = piece
+                lines[zi, 64 * e : 64 * e + 64, 128 * x : 128 * x + 128] = piece
                 if 2 <= x <= 6:
                     lines_out[zi, 64 * e : 64 * e + 64, 128 * (x - 2) : 128 * (x - 1)] = piece
 
-    def products(x, carry):
-        product = jnp.dot(wall[...], lines[x], preferred_element_type=F32)
-
-        def store(a, zz, total):
-            sums[x, 2 * a + zz - 1] = total
-
-        z_sums(product, (1, 2), store)
-        return carry
-
-    lax.fori_loop(0, 9, products, 0, unroll=3)
+    for first, count in ((0, 2), (2, 2), (4, 2), (6, 3)):
+        at = slice(128 * first, 128 * (first + count))
+        before = jnp.dot(wall[0:192, :], lines[0, :, at], preferred_element_type=F32)
+        middle = jnp.dot(wall[...], lines[1, :, at], preferred_element_type=F32)
+        after = jnp.dot(wall[384:576, :], lines[2, :, at], preferred_element_type=F32)
+        for i in range(count):
+            col = slice(128 * i, 128 * i + 128)
+            for a in range(3):
+                low, centre, high = [middle[64 * (3 * b + a) : 64 * (3 * b + a) + 64, col] for b in range(3)]
+                block = slice(64 * a, 64 * a + 64)
+                sums[first + i, 2 * a] = before[block, col] + (centre + high)
+                sums[first + i, 2 * a + 1] = (low + centre) + after[block, col]
 
     def rows(k, carry):
         r = k + 1
@@ -373,6 +391,12 @@
             send[pl.ds(4 * x + zz, 16, 32), :] = grads[x, pl.ds(7 + zz, 16, 2), :]
 
 
+def in_pairs(block):
+    at = lax.broadcasted_iota(jnp.int32, (16, 128), 0)
+    rest = block - block.astype(BF16).astype(F32)
+    return jnp.where(at == 0, block, jnp.where(at == 1, rest, 0.0))
+
+
 def backward_kernel(
     received, slopes, lines, folded, latent_out, parts_out, low, low_wide, terms, logit_grads
 ):
@@ -400,8 +424,8 @@
     for piece in split(jnp.concatenate([head_sum, bias_sum], axis=0), 3):
         term = lax.dot_general(ones, piece, NT, preferred_element_type=F32)
         row = term if row is None else row + term
-    parts_out[864:872, :] = row
-    parts_out[872:1024, :] = jnp.zeros((152, 128), F32)
+    parts_out[864:880, :] = in_pairs(jnp.concatenate([row, row], axis=0)).astype(BF16)
+    parts_out[880:1024, :] = jnp.zeros((144, 128), BF16)
 
     parities = {-1: (0,), 0: (0, 1), 1: (1,)}
     found = {}
@@ -427,8 +451,9 @@
                     term = terms[found[dx, px, dz, pz]]
                     tap = term if tap is None else tap + term
             at = 96 * (3 * (a + 1) + b + 1)
-            parts_out[at : at + 64, :] = tap[:, :128]
-            parts_out[at + 64 : at + 96, :] = jnp.concatenate([tap[:32, 128:], tap[32:, 128:]], axis=1)
+            parts_out[at : at + 64, :] = tap[:, :128].astype(BF16)
+            both = jnp.concatenate([tap[:32, 128:], tap[32:, 128:]], axis=1)
+            parts_out[at + 64 : at + 96, :] = both.astype(BF16)
 
     stacked = []
     for x in range(3):
@@ -446,10 +471,13 @@
         latent_out[x, 0] = result[64 * x : 64 * x + 64]
 
 
-def sum_kernel(received, out):
-    total = received[0]
+def sum_kernel(place, received, out):
+    total = received[0].astype(F32)
     for s in range(1, received.shape[0]):
-        total = total + received[s]
+        total = total + received[s].astype(F32)
+    if out.dtype == BF16:
+        pair = jnp.broadcast_to(total[0:1] + total[1:2], (16, 128))
+        total = jnp.where(place[0] == 54, in_pairs(pair), total)
     total = total.astype(out.dtype)
     for s in range(out.shape[0]):
         out[s] = total
@@ -464,7 +492,8 @@
         last = rows[at + 64 : at + 96, :].astype(F32)
         kernel_out[3 * tap + 2, 0:32] = last[:, :64]
         kernel_out[3 * tap + 2, 32:64] = last[:, 64:]
-    row = rows[864:880, :].astype(F32)[0:1]
+    row = rows[864:880, :].astype(F32)
+    row = row[0:1] + row[1:2]
     head_out[...] = row[:, :64]
     bias_out[...] = row[:, 64:]
 
@@ -496,25 +525,25 @@
 FIELD = pltpu.VMEM((18, 32, 128), F32)
 pack = call(
     pack_kernel,
-    (shape((24, 32, 128)), shape((24, 32, 128)), shape((3, 64, 64), BF16)),
-    [HBM] * 6,
-    [pltpu.SemaphoreType.DMA((11,))],
-    4,
+    (
+        shape((24, 32, 128)),
+        shape((24, 32, 128)),
+        shape((3, 64, 64), BF16),
+        shape((576, 192), BF16),
+        shape((64, 128)),
+        shape((64, 128)),
+    ),
+    [HBM] * 7 + [VMEM] * 2,
+    [pltpu.VMEM((27, 64, 64), BF16), pltpu.SemaphoreType.DMA((12,))],
+    6,
 )
 join = call(join_kernel, shape((9, 32, 128), BF16), [VMEM] * 3, (), 2)
-widen = call(
-    taps_kernel,
-    (shape((576, 192), BF16), shape((64, 128)), shape((64, 128))),
-    [HBM] + [VMEM] * 2,
-    [pltpu.VMEM((27, 64, 64), BF16), pltpu.SemaphoreType.DMA],
-    4,
-)
 decode = call(
     decode_kernel,
     (shape((16, 32, 128)), shape((3, 192, 640), BF16)),
     [VMEM] * 6,
     [
-        pltpu.VMEM((9, 192, 384), BF16),
+        pltpu.VMEM((3, 192, 1152), BF16),
         pltpu.VMEM((9, 6, 64, 128), F32),
         pltpu.VMEM((32, 128), F32),
     ],
@@ -572,7 +601,7 @@
 )
 backward = call(
     backward_kernel,
-    (shape((3, 1, 64, 64)), shape((1024, 128))),
+    (shape((3, 1, 64, 64)), shape((1024, 128), BF16)),
     [VMEM] * 4,
     [
         pltpu.VMEM((8, 4, 64, 128), BF16),
@@ -614,8 +643,9 @@
     taps = in_hbm(kernel)
     coarse = latent.reshape(3, 64, 64)
     low, high = shifted((coarse, coarse), TILE, 32)
-    to_next, to_prev, middle = pack(*fields, in_hbm(coarse))
-    wall, bias, head = widen(taps, conv_bias.reshape(1, 64), head_weight.reshape(1, 64))
+    to_next, to_prev, middle, wall, bias, head = pack(
+        *fields, in_hbm(coarse), taps, conv_bias.reshape(1, 64), head_weight.reshape(1, 64)
+    )
     nine = join(low, middle, high)
     z_prev, z_next = shifted((nine, nine), SHOT, 16)
     to_next, to_prev, nine = lax.optimization_barrier((to_next, to_prev, nine))
@@ -642,9 +672,10 @@
     latent_grad, parts = backward(received, slope, lines, folded)
 
     pieces = lax.all_to_all(parts.reshape(64, 16, 128), NEAR, 0, 0, tiled=True)
-    pieces = call(sum_kernel, shape((8, 16, 128)), [VMEM])(pieces)
+    piece = lax.axis_index(NEAR).astype(jnp.int32).reshape(1)
+    pieces = call(sum_kernel, shape((8, 16, 128)), [SMEM, VMEM])(piece, pieces)
     pieces = lax.all_to_all(pieces, "y", 0, 0, tiled=True)
-    pieces = call(sum_kernel, shape((64, 16, 128), BF16), [VMEM])(pieces)
+    pieces = call(sum_kernel, shape((64, 16, 128), BF16), [SMEM, VMEM])(piece, pieces)
     whole = lax.all_to_all(pieces, NEAR, 0, 0, tiled=True)
     kernel_grad, head_grad, bias_grad = call(
         unpack_kernel, (shape((27, 64, 64)), shape((1, 64)), shape((1, 64))), [VMEM]

time: 135 us -> 126 us (0.933)
  blocking collectives: 65.4 us -> 33.7 us
  waiting for transfers between devices: 9.97 us -> 25 us
  starting transfers between devices: 37.6 us -> 47 us
  Pallas kernels: 18.6 us -> 16.6 us
    all_to_all x1 -> x0, blocking collectives: 30.9 us -> none  [per_device(): pieces = lax.all_to_all(parts.reshape(64, 16, 128), NEAR, 0, 0, tiled=True)]
    all_to_all x0 -> x1, waiting for transfers between devices: none -> 12.6 us  [per_device(): pieces = lax.all_to_all(parts.reshape(64, 16, 128), NEAR, 0, 0, tiled=True)]
    all_to_all x0 -> x1, starting transfers between devices: none -> 10.7 us  [per_device(): pieces = lax.all_to_all(parts.reshape(64, 16, 128), NEAR, 0, 0, tiled=True)]
    ppermute x3, starting transfers between devices: 12 us -> 7.25 us  [shifted(): high = lax.ppermute(block[1], axes, [(i + 1, i) for i in range(size - 1)])]
    all_to_all x1, starting transfers between devices: 9.51 us -> 11.6 us  [per_device(): speeds = lax.all_to_all(speed, SHOT, 0, 0, tiled=True)]
    all_to_all x1, waiting for transfers between devices: 4.7 us -> 6.4 us  [per_device(): speeds = lax.all_to_all(speed, SHOT, 0, 0, tiled=True)]
  transfers between devices with their start and end apart: 8 -> 9, of which waited for: 3 -> 4; matrix products, arithmetic and copies ran while one was open for 0% -> 0% of each run, Pallas kernels for 9% -> 8%
where the time goes in v5:
time: 126 us; the launch traced here: 125 us
  starting transfers between devices  47 us (37%)
  blocking collectives  33.7 us (27%)
  waiting for transfers between devices  25 us (20%)
  Pallas kernels  16.6 us (13%)
  between operations  1.5 us (1%)
  local copies, waits for them, and re-layouts  1.32 us (1%)
    all_to_all x1, blocking collectives, per_device(): whole = lax.all_to_all(pieces, NEAR, 0, 0, tiled=True)  19.3 us
    all_to_all x1, blocking collectives, per_device(): pieces = lax.all_to_all(pieces, 'y', 0, 0, tiled=True)  14.4 us
    ppermute x3, starting transfers between devices, shifted(): low = lax.ppermute(block[0], axes, [(i, i + 1) for i in range(size - 1)])  13 us
    all_to_all x1, waiting for transfers between devices, per_device(): pieces = lax.all_to_all(parts.reshape(64, 16, 128), NEAR, 0, 0, tiled=True)  12.6 us
    all_to_all x1, starting transfers between devices, per_device(): speeds = lax.all_to_all(speed, SHOT, 0, 0, tiled=True)  11.6 us
    all_to_all x1, starting transfers between devices, per_device(): pieces = lax.all_to_all(parts.reshape(64, 16, 128), NEAR, 0, 0, tiled=True)  10.7 us
    ppermute x3, starting transfers between devices, shifted(): high = lax.ppermute(block[1], axes, [(i + 1, i) for i in range(size - 1)])  7.25 us
    all_to_all x1, waiting for transfers between devices, per_device(): speeds = lax.all_to_all(speed, SHOT, 0, 0, tiled=True)  6.4 us
  transfers between devices with their start and end apart: 9, of which 4 were waited for; matrix products, arithmetic and copies ran while one was open for 0% of the time, Pallas kernels for 8%

profile of v5, /device:TPU:1, one launch (start us, length us, event | category | flops | bytes accessed | tf_op | source)
XLA Modules:
  0.0 125.1 jit_solution(10011500108269416097)
XLA Ops:
  0.6 6.0 %collective-permute-start = (bf16[3,64,64]{2,1,0:T(8,128)(2,1)}, bf16[3,64,64]{2,1,0:T(8,128)(2,1)S(1)}, u32[]{:S(2)}, u32[]{:S(2)}) collective-permute-start(bf16[3,64,64]{2,1,0:T(8,128)(2,1)} %bitcast.15), channel_id=1, source_target_pairs={{0,1},{1,2},{2,3},{3,4},{4,5},{5,6},{6,7},{7,8},{8,9},{9,10},{10,1... | collective-permute-start | bytes 73736 | tf_op jit(solution)/shard_map/ppermute | solution.py:621
  6.7 4.0 %collective-permute-start.1 = (bf16[3,64,64]{2,1,0:T(8,128)(2,1)}, bf16[3,64,64]{2,1,0:T(8,128)(2,1)S(1)}, u32[]{:S(2)}, u32[]{:S(2)}) collective-permute-start(bf16[3,64,64]{2,1,0:T(8,128)(2,1)} %bitcast.16), channel_id=1, source_target_pairs={{1,0},{2,1},{3,2},{4,3},{5,4},{6,5},{7,6},{8,7},{9,8},{10,9},{11,1... | collective-permute-start | bytes 73736 | tf_op jit(solution)/shard_map/ppermute | solution.py:622
  10.7 0.0 copy-start.3
  10.7 0.6 copy-done.3
  11.4 0.0 copy-start.4
  11.4 0.7 copy-done.4
  12.0 1.4 %shard_map.156 = (f32[24,32,128]{2,1,0:T(8,128)S(1)}, f32[24,32,128]{2,1,0:T(8,128)S(1)}, bf16[3,64,64]{2,1,0:T(8,128)(2,1)S(1)}, bf16[576,192]{1,0:T(8,128)(2,1...) custom-call(f32[1,6,32,128]{3,2,1,0:T(8,128)} %wave_now.3, f32[1,6,32,128]{3,2,1,0:T(8,128)} %wave_prev.3, ...), custom_call_target="tpu_custom_call" | custom-call | tf_op jit(solution)/shard_map/pallas_call | solution.py:646
  13.4 0.0 copy-start.1
  13.4 0.0 copy-start.2
  13.4 0.0 copy-start
  13.5 0.0 collective-permute-done.low
  13.5 0.3 collective-permute-done.1.high
  13.8 0.1 shard_map.157.own
  13.9 4.0 %collective-permute-start.4 = (bf16[9,32,128]{2,1,0:T(8,128)(2,1)S(1)}, bf16[9,32,128]{2,1,0:T(8,128)(2,1)S(1)}, u32[]{:S(2)}, u32[]{:S(2)}) collective-permute-start(bf16[9,32,128]{2,1,0:T(8,128)(2,1)S(1)} %shard_map.157.own), channel_id=1, source_target_pairs={{0,32},{32,64},{64,96},{96,128},{128,160},{160,192},{192,224},{224... | collective-permute-start | bytes 221192 | tf_op jit(solution)/shard_map/ppermute | solution.py:621
  17.9 1.3 %collective-permute-start.5 = (bf16[9,32,128]{2,1,0:T(8,128)(2,1)S(1)}, bf16[9,32,128]{2,1,0:T(8,128)(2,1)S(1)}, u32[]{:S(2)}, u32[]{:S(2)}) collective-permute-start(bf16[9,32,128]{2,1,0:T(8,128)(2,1)S(1)} %shard_map.157.own), channel_id=1, source_target_pairs={{32,0},{64,32},{96,64},{128,96},{160,128},{192,160},{224,192},{256... | collective-permute-start | bytes 221192 | tf_op jit(solution)/shard_map/ppermute | solution.py:622
  19.2 3.0 %collective-permute-start.2 = (f32[24,32,128]{2,1,0:T(8,128)S(1)}, f32[24,32,128]{2,1,0:T(8,128)S(1)}, u32[]{:S(2)}, u32[]{:S(2)}) collective-permute-start(f32[24,32,128]{2,1,0:T(8,128)S(1)} %get-tuple-element.27), channel_id=1, source_target_pairs={{0,1},{1,2},{2,3},{3,4},{4,5},{5,6},{6,7},{7,8},{8,9},{9,10},{10,1... | collective-permute-start | bytes 1179656 | tf_op jit(solution)/shard_map/ppermute | solution.py:621
  22.2 1.9 %collective-permute-start.3 = (f32[24,32,128]{2,1,0:T(8,128)S(1)}, f32[24,32,128]{2,1,0:T(8,128)S(1)}, u32[]{:S(2)}, u32[]{:S(2)}) collective-permute-start(f32[24,32,128]{2,1,0:T(8,128)S(1)} %get-tuple-element.28), channel_id=1, source_target_pairs={{1,0},{2,1},{3,2},{4,3},{5,4},{6,5},{7,6},{8,7},{9,8},{10,9},{11,1... | collective-permute-start | bytes 1179656 | tf_op jit(solution)/shard_map/ppermute | solution.py:622
  24.1 0.0 collective-permute-done.4.z_prev
  24.1 0.0 collective-permute-done.5.z_next
  24.1 2.8 %shard_map.158 = (f32[16,32,128]{2,1,0:T(8,128)}, bf16[3,192,640]{2,1,0:T(8,128)(2,1)S(1)}) custom-call(bf16[9,32,128]{2,1,0:T(8,128)(2,1)S(1)} %collective-permute-done.4.z_prev, bf16[9,32,128]{2,1,0:T(8,128)(2,1)S(1)} %shard_map.157.own, bf16[9,32,128]{2,1,0:T(8,128)(2,1)S(1)} %collective-permute-done.5.z_next, ...), custom_call_target="tpu_custom_call" | custom-call | flops 500000000 | tf_op jit(solution)/shard_map/pallas_call | solution.py:654
  27.0 0.0 copy-done.1
  27.0 0.0 copy-done.2
  27.0 11.6 %all-to-all-start = ((f32[16,32,128]{2,1,0:T(8,128)}), f32[16,32,128]{2,1,0:T(8,128)S(1)}, u32[]{:S(2)}, u32[]{:S(2)}) async-start(f32[16,32,128]{2,1,0:T(8,128)} %get-tuple-element.33.after), calls=%async_computation | async-start | bytes 524288 | tf_op jit(solution)/shard_map/all_to_all | solution.py:655
  39.3 0.0 collective-permute-done.2.left
  39.3 0.0 collective-permute-done.3.right
  39.3 2.5 %shard_map.159 = (f32[30,32,128]{2,1,0:T(8,128)S(1)}, f32[4,384,128]{2,1,0:T(8,128)}) custom-call(s32[1]{0:T(128)} %bitcast.place, f32[1,6,32,128]{3,2,1,0:T(8,128)} %wave_now.3, f32[1,6,32,128]{3,2,1,0:T(8,128)} %wave_prev.3, f32[1,6,32,128]{3,2,1,0:T(8,128)} %adj_next.3, f32[1,6,32,128]{3,2,1,0:T(8,128)} %adj_after.3, f32[6,32,128]{2,1,0:T(8,128)} %density.3, ...), custom_call_target="tpu_custom_call" | custom-call | flops 2000000000 | tf_op jit(solution)/shard_map/pallas_call | solution.py:657
  41.8 0.0 copy-done
  41.8 6.4 %all-to-all-done = f32[16,32,128]{2,1,0:T(8,128)S(1)} async-done(((f32[16,32,128]{2,1,0:T(8,128)}), f32[16,32,128]{2,1,0:T(8,128)S(1)}, u32[]{:S(2)}, u32[]{:S(2)}) %all-to-all-start) | async-done | bytes 262176 | tf_op jit(solution)/shard_map/all_to_all | solution.py:655
  48.2 2.9 %shard_map.160.after = f32[16,32,128]{2,1,0:T(8,128)} custom-call(s32[1]{0:T(128)} %bitcast.place, s32[1]{0:T(128)S(6)} %copy.17.source, f32[1,3]{1,0:T(1,128)} %pulses_in.1, f32[24,32,128]{2,1,0:T(8,128)S(1)} %collective-permute-done.2.left, f32[24,32,128]{2,1,0:T(8,128)S(1)} %collective-permute-done.3.right, f32[512,128]{1,0:T(8,128)S(1)} %bitcast.12, ...), custom_call_target="tpu_custom_call" | custom-call | tf_op jit(solution)/shard_map/pallas_call | solution.py:660
  51.1 4.5 %all-to-all-start.1 = ((f32[16,32,128]{2,1,0:T(8,128)}), f32[16,32,128]{2,1,0:T(8,128)S(1)}, u32[]{:S(2)}, u32[]{:S(2)}) async-start(f32[16,32,128]{2,1,0:T(8,128)} %shard_map.160.after), calls=%async_computation.1 | async-start | bytes 524288 | tf_op jit(solution)/shard_map/all_to_all | solution.py:670
  55.6 3.3 %shard_map.161 = (f32[45,64,128]{2,1,0:T(8,128)S(1)}, bf16[384,1024]{1,0:T(8,128)(2,1)S(1)}) custom-call(bf16[3,192,640]{2,1,0:T(8,128)(2,1)S(1)} %get-tuple-element.36.lines, bf16[576,192]{1,0:T(8,128)(2,1)} %copy-done, f32[64,128]{1,0:T(8,128)} %copy-done.1, f32[64,128]{1,0:T(8,128)} %copy-done.2, bf16[27,64,64]{2,1,0:T(8,128)(2,1)} %kernel_in.3, ...), custom_call_target="tpu_custom_call" | custom-call | tf_op jit(solution)/shard_map/pallas_call | solution.py:671
  58.9 5.6 %all-to-all-done.1.received = f32[16,32,128]{2,1,0:T(8,128)S(1)} async-done(((f32[16,32,128]{2,1,0:T(8,128)}), f32[16,32,128]{2,1,0:T(8,128)S(1)}, u32[]{:S(2)}, u32[]{:S(2)}) %all-to-all-start.1) | async-done | bytes 262176 | tf_op jit(solution)/shard_map/all_to_all | solution.py:670
  64.5 2.4 %shard_map.162 = (f32[3,1,64,64]{3,2,1,0:T(8,128)}, bf16[1024,128]{1,0:T(8,128)(2,1)}) custom-call(f32[16,32,128]{2,1,0:T(8,128)S(1)} %all-to-all-done.1.received, f32[45,64,128]{2,1,0:T(8,128)S(1)} %get-tuple-element.37.slopes, bf16[3,192,640]{2,1,0:T(8,128)(2,1)S(1)} %get-tuple-element.36.lines, bf16[384,1024]{1,0:T(8,128)(2,1)S(1)} %get-tuple-element.38.folded), custom_call_target="tpu_custom_call" | custom-call | tf_op jit(solution)/shard_map/pallas_call | solution.py:672
  66.9 10.7 %all-to-all-start.2 = ((bf16[64,16,128]{2,1,0:T(8,128)(2,1)}), bf16[64,16,128]{2,1,0:T(8,128)(2,1)S(1)}, u32[]{:S(2)}, u32[]{:S(2)}) async-start(bf16[64,16,128]{2,1,0:T(8,128)(2,1)} %bitcast.7), calls=%async_computation.2 | async-start | bytes 524288 | tf_op jit(solution)/shard_map/all_to_all | solution.py:674
  77.6 12.6 %all-to-all-done.2.received = bf16[64,16,128]{2,1,0:T(8,128)(2,1)S(1)} async-done(((bf16[64,16,128]{2,1,0:T(8,128)(2,1)}), bf16[64,16,128]{2,1,0:T(8,128)(2,1)S(1)}, u32[]{:S(2)}, u32[]{:S(2)}) %all-to-all-start.2) | async-done | bytes 262176 | tf_op jit(solution)/shard_map/all_to_all | solution.py:674
  90.2 0.1 shard_map.163
  90.3 14.4 %all_to_all.25.received = f32[8,16,128]{2,1,0:T(8,128)S(1)} all-to-all(f32[8,16,128]{2,1,0:T(8,128)S(1)} %shard_map.163), channel_id=1, replica_groups=mesh['xlo'=2,'z'=8,'y'=8,'xhi'=2,'core'=2] {'y'}, dimensions={0} | all-to-all | bytes 131072 | tf_op jit(solution)/shard_map/all_to_all | solution.py:677
  104.7 19.3 %all_to_all.26 = bf16[64,16,128]{2,1,0:T(8,128)(2,1)S(1)} all-to-all(bf16[64,16,128]{2,1,0:T(8,128)(2,1)S(1)} %shard_map.164), channel_id=1, replica_groups=mesh['xlo'=2,'z'=8,'y'=8,'xhi'=2,'core'=2] {'xlo','z','xhi','core'}, dimensions={0} | all-to-all | bytes 524288 | tf_op jit(solution)/shard_map/all_to_all | solution.py:679
  124.0 1.0 shard_map.165
  (1 shorter events, 0.0 us)
Async XLA Ops:
  0.6 12.8 %collective-permute-start = (bf16[3,64,64]{2,1,0:T(8,128)(2,1)}, bf16[3,64,64]{2,1,0:T(8,128)(2,1)S(1)}, u32[]{:S(2)}, u32[]{:S(2)}) collective-permute-start(bf16[3,64,64]{2,1,0:T(8,128)(2,1)} %bitcast.15), channel_id=1, source_target_pairs={{0,1},{1,2},{2,3},{3,4},{4,5},{5,6},{6,7},{7,8},{8,9},{9,10},{10,1... | collective-permute-start | bytes 73736 | tf_op jit(solution)/shard_map/ppermute | solution.py:621
  6.7 7.1 %collective-permute-start.1 = (bf16[3,64,64]{2,1,0:T(8,128)(2,1)}, bf16[3,64,64]{2,1,0:T(8,128)(2,1)S(1)}, u32[]{:S(2)}, u32[]{:S(2)}) collective-permute-start(bf16[3,64,64]{2,1,0:T(8,128)(2,1)} %bitcast.16), channel_id=1, source_target_pairs={{1,0},{2,1},{3,2},{4,3},{5,4},{6,5},{7,6},{8,7},{9,8},{10,9},{11,1... | collective-permute-start | bytes 73736 | tf_op jit(solution)/shard_map/ppermute | solution.py:622
  10.7 0.7 copy-start.3
  11.4 0.7 copy-start.4
  13.4 13.5 %copy-start.1 = (f32[64,128]{1,0:T(8,128)}, f32[64,128]{1,0:T(8,128)S(1)}, u32[]{:S(2)}) copy-start(f32[64,128]{1,0:T(8,128)S(1)} %get-tuple-element.31.bias.bias_in) | copy-start | bytes 98308
  13.4 13.5 %copy-start.2 = (f32[64,128]{1,0:T(8,128)}, f32[64,128]{1,0:T(8,128)S(1)}, u32[]{:S(2)}) copy-start(f32[64,128]{1,0:T(8,128)S(1)} %get-tuple-element.32.head.head_in) | copy-start | bytes 98308
  13.4 28.3 %copy-start = (bf16[576,192]{1,0:T(8,128)(2,1)}, bf16[576,192]{1,0:T(8,128)(2,1)S(1)}, u32[]{:S(2)}) copy-start(bf16[576,192]{1,0:T(8,128)(2,1)S(1)} %get-tuple-element.30.wall.wall_in) | copy-start | bytes 663556
  13.9 10.2 %collective-permute-start.4 = (bf16[9,32,128]{2,1,0:T(8,128)(2,1)S(1)}, bf16[9,32,128]{2,1,0:T(8,128)(2,1)S(1)}, u32[]{:S(2)}, u32[]{:S(2)}) collective-permute-start(bf16[9,32,128]{2,1,0:T(8,128)(2,1)S(1)} %shard_map.157.own), channel_id=1, source_target_pairs={{0,32},{32,64},{64,96},{96,128},{128,160},{160,192},{192,224},{224... | collective-permute-start | bytes 221192 | tf_op jit(solution)/shard_map/ppermute | solution.py:621
  17.9 6.2 %collective-permute-start.5 = (bf16[9,32,128]{2,1,0:T(8,128)(2,1)S(1)}, bf16[9,32,128]{2,1,0:T(8,128)(2,1)S(1)}, u32[]{:S(2)}, u32[]{:S(2)}) collective-permute-start(bf16[9,32,128]{2,1,0:T(8,128)(2,1)S(1)} %shard_map.157.own), channel_id=1, source_target_pairs={{32,0},{64,32},{96,64},{128,96},{160,128},{192,160},{224,192},{256... | collective-permute-start | bytes 221192 | tf_op jit(solution)/shard_map/ppermute | solution.py:622
  19.2 20.1 %collective-permute-start.2 = (f32[24,32,128]{2,1,0:T(8,128)S(1)}, f32[24,32,128]{2,1,0:T(8,128)S(1)}, u32[]{:S(2)}, u32[]{:S(2)}) collective-permute-start(f32[24,32,128]{2,1,0:T(8,128)S(1)} %get-tuple-element.27), channel_id=1, source_target_pairs={{0,1},{1,2},{2,3},{3,4},{4,5},{5,6},{6,7},{7,8},{8,9},{9,10},{10,1... | collective-permute-start | bytes 1179656 | tf_op jit(solution)/shard_map/ppermute | solution.py:621
  22.2 17.1 %collective-permute-start.3 = (f32[24,32,128]{2,1,0:T(8,128)S(1)}, f32[24,32,128]{2,1,0:T(8,128)S(1)}, u32[]{:S(2)}, u32[]{:S(2)}) collective-permute-start(f32[24,32,128]{2,1,0:T(8,128)S(1)} %get-tuple-element.28), channel_id=1, source_target_pairs={{1,0},{2,1},{3,2},{4,3},{5,4},{6,5},{7,6},{8,7},{9,8},{10,9},{11,1... | collective-permute-start | bytes 1179656 | tf_op jit(solution)/shard_map/ppermute | solution.py:622
  27.0 21.2 %all-to-all-start = ((f32[16,32,128]{2,1,0:T(8,128)}), f32[16,32,128]{2,1,0:T(8,128)S(1)}, u32[]{:S(2)}, u32[]{:S(2)}) async-start(f32[16,32,128]{2,1,0:T(8,128)} %get-tuple-element.33.after), calls=%async_computation | async-start | bytes 524288 | tf_op jit(solution)/shard_map/all_to_all | solution.py:655
  51.1 13.4 %all-to-all-start.1 = ((f32[16,32,128]{2,1,0:T(8,128)}), f32[16,32,128]{2,1,0:T(8,128)S(1)}, u32[]{:S(2)}, u32[]{:S(2)}) async-start(f32[16,32,128]{2,1,0:T(8,128)} %shard_map.160.after), calls=%async_computation.1 | async-start | bytes 524288 | tf_op jit(solution)/shard_map/all_to_all | solution.py:670
  66.9 23.3 %all-to-all-start.2 = ((bf16[64,16,128]{2,1,0:T(8,128)(2,1)}), bf16[64,16,128]{2,1,0:T(8,128)(2,1)S(1)}, u32[]{:S(2)}, u32[]{:S(2)}) async-start(bf16[64,16,128]{2,1,0:T(8,128)(2,1)} %bitcast.7), calls=%async_computation.2 | async-start | bytes 524288 | tf_op jit(solution)/shard_map/all_to_all | solution.py:674

commit v6 on v5

--- a/solution.py
+++ b/solution.py
@@ -398,7 +398,7 @@
 
 
 def backward_kernel(
-    received, slopes, lines, folded, latent_out, parts_out, low, low_wide, terms, logit_grads
+    received, slopes, lines, low_out, parts_out, low, low_wide, terms, logit_grads, sem
 ):
     total = received[0]
     for s in range(1, 16):
@@ -418,6 +418,9 @@
                 low_wide[2 * px + zz - 1, :, 64 * (x - 1 - px) : 64 * (x + 1 - px)] = rounded
                 head_sum = head_sum + slopes[30 + 2 * x + zz - 1] * grad
                 bias_sum = bias_sum + pre_grad
+
+    copy = pltpu.make_async_copy(low, low_out, sem)
+    copy.start()
 
     ones = jnp.ones((8, 128), BF16)
     row = None
@@ -454,7 +457,13 @@
             parts_out[at : at + 64, :] = tap[:, :128].astype(BF16)
             both = jnp.concatenate([tap[:32, 128:], tap[32:, 128:]], axis=1)
             parts_out[at + 64 : at + 96, :] = both.astype(BF16)
-
+    copy.wait()
+
+
+def latent_kernel(low_in, folded, after, latent_out, low, sem):
+    copy = pltpu.make_async_copy(low_in, low, sem)
+    copy.start()
+    copy.wait()
     stacked = []
     for x in range(3):
         around = low[2 * x : 2 * x + 4].reshape(1024, 128)
@@ -601,14 +610,22 @@
 )
 backward = call(
     backward_kernel,
-    (shape((3, 1, 64, 64)), shape((1024, 128), BF16)),
-    [VMEM] * 4,
+    (pltpu.HBM((8, 4, 64, 128), BF16), shape((1024, 128), BF16)),
+    [VMEM] * 3,
     [
         pltpu.VMEM((8, 4, 64, 128), BF16),
         pltpu.VMEM((4, 64, 384), BF16),
         pltpu.VMEM((16, 64, 192), F32),
         pltpu.VMEM((32, 128), F32),
+        pltpu.SemaphoreType.DMA,
     ],
+    14,
+)
+latent_part = call(
+    latent_kernel,
+    shape((3, 1, 64, 64)),
+    [HBM, VMEM, ANY],
+    [pltpu.VMEM((8, 4, 64, 128), BF16), pltpu.SemaphoreType.DMA],
     14,
 )
 
@@ -669,7 +686,8 @@
     )
     received = lax.all_to_all(strips, SHOT, 0, 0, tiled=True)
     slope, folded = slopes(lines, in_hbm(wall), in_hbm(bias), in_hbm(head), taps, in_hbm(strips))
-    latent_grad, parts = backward(received, slope, lines, folded)
+    low, parts = backward(received, slope, lines)
+    latent_grad = latent_part(in_hbm(low), folded, parts)
 
     pieces = lax.all_to_all(parts.reshape(64, 16, 128), NEAR, 0, 0, tiled=True)
     piece = lax.axis_index(NEAR).astype(jnp.int32).reshape(1)

time: 126 us -> 127 us (level)
  blocking collectives: 33.7 us -> 13.8 us
  waiting for transfers between devices: 25 us -> 34.7 us
  starting transfers between devices: 47 us -> 55.1 us
  Pallas kernels: 16.6 us -> 19.8 us
    all_to_all x1 -> x0, blocking collectives: 19.3 us -> none  [per_device(): whole = lax.all_to_all(pieces, NEAR, 0, 0, tiled=True)]
    all_to_all x0 -> x1, waiting for transfers between devices: none -> 9.87 us  [per_device(): whole = lax.all_to_all(pieces, NEAR, 0, 0, tiled=True)]
    all_to_all x0 -> x1, starting transfers between devices: none -> 6.87 us  [per_device(): whole = lax.all_to_all(pieces, NEAR, 0, 0, tiled=True)]
    ppermute x3, starting transfers between devices: 7.25 us -> 12 us  [shifted(): high = lax.ppermute(block[1], axes, [(i + 1, i) for i in range(size - 1)])]
    pallas_call x1 -> x2, Pallas kernels: 2.42 us -> 4.95 us  [the longest x1 2.76 us: per_device(): latent_grad = latent_part(in_hbm(low), folded, parts)]
    ppermute x3, starting transfers between devices: 13 us -> 10.8 us  [shifted(): low = lax.ppermute(block[0], axes, [(i, i + 1) for i in range(size - 1)])]
    all_to_all x1, starting transfers between devices: 11.6 us -> 9.51 us  [per_device(): speeds = lax.all_to_all(speed, SHOT, 0, 0, tiled=True)]
    all_to_all x1, waiting for transfers between devices: 5.59 us -> 7.08 us  [per_device(): received = lax.all_to_all(strips, SHOT, 0, 0, tiled=True)]
  transfers between devices with their start and end apart: 9 -> 10, of which waited for: 4 -> 4; matrix products, arithmetic and copies ran while one was open for 0% -> 0% of each run, Pallas kernels for 8% -> 10%
where the time goes in v6:
time: 127 us; the launch traced here: 126 us
  starting transfers between devices  55.1 us (43%)
  waiting for transfers between devices  34.7 us (27%)
  Pallas kernels  19.8 us (16%)
  blocking collectives  13.8 us (11%)
  between operations  1.53 us (1%)
  local copies, waits for them, and re-layouts  1.32 us (1%)
    all_to_all x1, blocking collectives, per_device(): pieces = lax.all_to_all(pieces, 'y', 0, 0, tiled=True)  13.8 us
    all_to_all x1, waiting for transfers between devices, per_device(): pieces = lax.all_to_all(parts.reshape(64, 16, 128), NEAR, 0, 0, tiled=True)  12.6 us
    ppermute x3, starting transfers between devices, shifted(): high = lax.ppermute(block[1], axes, [(i + 1, i) for i in range(size - 1)])  12 us
    all_to_all x1, starting transfers between devices, per_device(): pieces = lax.all_to_all(parts.reshape(64, 16, 128), NEAR, 0, 0, tiled=True)  11.8 us
    ppermute x3, starting transfers between devices, shifted(): low = lax.ppermute(block[0], axes, [(i, i + 1) for i in range(size - 1)])  10.8 us
    all_to_all x1, waiting for transfers between devices, per_device(): whole = lax.all_to_all(pieces, NEAR, 0, 0, tiled=True)  9.87 us
    all_to_all x1, starting transfers between devices, per_device(): speeds = lax.all_to_all(speed, SHOT, 0, 0, tiled=True)  9.51 us
    all_to_all x1, waiting for transfers between devices, per_device(): received = lax.all_to_all(strips, SHOT, 0, 0, tiled=True)  7.08 us
  transfers between devices with their start and end apart: 10, of which 4 were waited for; matrix products, arithmetic and copies ran while one was open for 0% of the time, Pallas kernels for 10%

profile of v6, /device:TPU:1, one launch (start us, length us, event | category | flops | bytes accessed | tf_op | source)
XLA Modules:
  0.0 126.1 jit_solution(15679242995666296483)
XLA Ops:
  0.6 8.8 %collective-permute-start.1 = (bf16[3,64,64]{2,1,0:T(8,128)(2,1)}, bf16[3,64,64]{2,1,0:T(8,128)(2,1)S(1)}, u32[]{:S(2)}, u32[]{:S(2)}) collective-permute-start(bf16[3,64,64]{2,1,0:T(8,128)(2,1)} %bitcast.15), channel_id=1, source_target_pairs={{1,0},{2,1},{3,2},{4,3},{5,4},{6,5},{7,6},{8,7},{9,8},{10,9},{11,1... | collective-permute-start | bytes 73736 | tf_op jit(solution)/shard_map/ppermute | solution.py:639
  9.4 1.9 %collective-permute-start = (bf16[3,64,64]{2,1,0:T(8,128)(2,1)}, bf16[3,64,64]{2,1,0:T(8,128)(2,1)S(1)}, u32[]{:S(2)}, u32[]{:S(2)}) collective-permute-start(bf16[3,64,64]{2,1,0:T(8,128)(2,1)} %bitcast.16), channel_id=1, source_target_pairs={{0,1},{1,2},{2,3},{3,4},{4,5},{5,6},{6,7},{7,8},{8,9},{9,10},{10,1... | collective-permute-start | bytes 73736 | tf_op jit(solution)/shard_map/ppermute | solution.py:638
  11.4 0.0 copy-start.3
  11.4 0.6 copy-done.3
  12.0 0.0 copy-start.4
  12.0 0.7 copy-done.4
  12.7 1.4 %shard_map.156 = (f32[24,32,128]{2,1,0:T(8,128)S(1)}, f32[24,32,128]{2,1,0:T(8,128)S(1)}, bf16[3,64,64]{2,1,0:T(8,128)(2,1)S(1)}, bf16[576,192]{1,0:T(8,128)(2,1...) custom-call(f32[1,6,32,128]{3,2,1,0:T(8,128)} %wave_now.3, f32[1,6,32,128]{3,2,1,0:T(8,128)} %wave_prev.3, ...), custom_call_target="tpu_custom_call" | custom-call | tf_op jit(solution)/shard_map/pallas_call | solution.py:663
  14.1 0.0 copy-start.1
  14.1 0.0 copy-start.2
  14.1 0.0 copy-start
  14.1 0.0 collective-permute-done.1.high
  14.1 0.0 collective-permute-done.low
  14.1 0.1 shard_map.157.own
  14.2 1.3 %collective-permute-start.5 = (bf16[9,32,128]{2,1,0:T(8,128)(2,1)S(1)}, bf16[9,32,128]{2,1,0:T(8,128)(2,1)S(1)}, u32[]{:S(2)}, u32[]{:S(2)}) collective-permute-start(bf16[9,32,128]{2,1,0:T(8,128)(2,1)S(1)} %shard_map.157.own), channel_id=1, source_target_pairs={{32,0},{64,32},{96,64},{128,96},{160,128},{192,160},{224,192},{256... | collective-permute-start | bytes 221192 | tf_op jit(solution)/shard_map/ppermute | solution.py:639
  15.5 4.0 %collective-permute-start.4 = (bf16[9,32,128]{2,1,0:T(8,128)(2,1)S(1)}, bf16[9,32,128]{2,1,0:T(8,128)(2,1)S(1)}, u32[]{:S(2)}, u32[]{:S(2)}) collective-permute-start(bf16[9,32,128]{2,1,0:T(8,128)(2,1)S(1)} %shard_map.157.own), channel_id=1, source_target_pairs={{0,32},{32,64},{64,96},{96,128},{128,160},{160,192},{192,224},{224... | collective-permute-start | bytes 221192 | tf_op jit(solution)/shard_map/ppermute | solution.py:638
  19.5 4.9 %collective-permute-start.2 = (f32[24,32,128]{2,1,0:T(8,128)S(1)}, f32[24,32,128]{2,1,0:T(8,128)S(1)}, u32[]{:S(2)}, u32[]{:S(2)}) collective-permute-start(f32[24,32,128]{2,1,0:T(8,128)S(1)} %get-tuple-element.27), channel_id=1, source_target_pairs={{0,1},{1,2},{2,3},{3,4},{4,5},{5,6},{6,7},{7,8},{8,9},{9,10},{10,1... | collective-permute-start | bytes 1179656 | tf_op jit(solution)/shard_map/ppermute | solution.py:638
  24.4 1.9 %collective-permute-start.3 = (f32[24,32,128]{2,1,0:T(8,128)S(1)}, f32[24,32,128]{2,1,0:T(8,128)S(1)}, u32[]{:S(2)}, u32[]{:S(2)}) collective-permute-start(f32[24,32,128]{2,1,0:T(8,128)S(1)} %get-tuple-element.28), channel_id=1, source_target_pairs={{1,0},{2,1},{3,2},{4,3},{5,4},{6,5},{7,6},{8,7},{9,8},{10,9},{11,1... | collective-permute-start | bytes 1179656 | tf_op jit(solution)/shard_map/ppermute | solution.py:639
  26.4 0.0 collective-permute-done.5.z_next
  26.4 0.0 collective-permute-done.4.z_prev
  26.4 2.8 %shard_map.158 = (f32[16,32,128]{2,1,0:T(8,128)}, bf16[3,192,640]{2,1,0:T(8,128)(2,1)S(1)}) custom-call(bf16[9,32,128]{2,1,0:T(8,128)(2,1)S(1)} %collective-permute-done.4.z_prev, bf16[9,32,128]{2,1,0:T(8,128)(2,1)S(1)} %shard_map.157.own, bf16[9,32,128]{2,1,0:T(8,128)(2,1)S(1)} %collective-permute-done.5.z_next, ...), custom_call_target="tpu_custom_call" | custom-call | flops 500000000 | tf_op jit(solution)/shard_map/pallas_call | solution.py:671
  29.2 0.0 copy-done.1
  29.2 0.0 copy-done.2
  29.2 9.5 %all-to-all-start = ((f32[16,32,128]{2,1,0:T(8,128)}), f32[16,32,128]{2,1,0:T(8,128)S(1)}, u32[]{:S(2)}, u32[]{:S(2)}) async-start(f32[16,32,128]{2,1,0:T(8,128)} %get-tuple-element.33.after), calls=%async_computation | async-start | bytes 524288 | tf_op jit(solution)/shard_map/all_to_all | solution.py:672
  39.4 0.0 collective-permute-done.2.left
  39.4 0.0 collective-permute-done.3.right
  39.4 2.5 %shard_map.159 = (f32[30,32,128]{2,1,0:T(8,128)S(1)}, f32[4,384,128]{2,1,0:T(8,128)}) custom-call(s32[1]{0:T(128)} %bitcast.place, f32[1,6,32,128]{3,2,1,0:T(8,128)} %wave_now.3, f32[1,6,32,128]{3,2,1,0:T(8,128)} %wave_prev.3, f32[1,6,32,128]{3,2,1,0:T(8,128)} %adj_next.3, f32[1,6,32,128]{3,2,1,0:T(8,128)} %adj_after.3, f32[6,32,128]{2,1,0:T(8,128)} %density.3, ...), custom_call_target="tpu_custom_call" | custom-call | flops 2000000000 | tf_op jit(solution)/shard_map/pallas_call | solution.py:674
  41.9 0.0 copy-done
  41.9 5.1 %all-to-all-done = f32[16,32,128]{2,1,0:T(8,128)S(1)} async-done(((f32[16,32,128]{2,1,0:T(8,128)}), f32[16,32,128]{2,1,0:T(8,128)S(1)}, u32[]{:S(2)}, u32[]{:S(2)}) %all-to-all-start) | async-done | bytes 262176 | tf_op jit(solution)/shard_map/all_to_all | solution.py:672
  46.9 2.9 %shard_map.160.after = f32[16,32,128]{2,1,0:T(8,128)} custom-call(s32[1]{0:T(128)} %bitcast.place, s32[1]{0:T(128)S(6)} %copy.17.source, f32[1,3]{1,0:T(1,128)} %pulses_in.1, f32[24,32,128]{2,1,0:T(8,128)S(1)} %collective-permute-done.2.left, f32[24,32,128]{2,1,0:T(8,128)S(1)} %collective-permute-done.3.right, f32[512,128]{1,0:T(8,128)S(1)} %bitcast.12, ...), custom_call_target="tpu_custom_call" | custom-call | tf_op jit(solution)/shard_map/pallas_call | solution.py:677
  49.9 4.0 %all-to-all-start.1 = ((f32[16,32,128]{2,1,0:T(8,128)}), f32[16,32,128]{2,1,0:T(8,128)S(1)}, u32[]{:S(2)}, u32[]{:S(2)}) async-start(f32[16,32,128]{2,1,0:T(8,128)} %shard_map.160.after), calls=%async_computation.1 | async-start | bytes 524288 | tf_op jit(solution)/shard_map/all_to_all | solution.py:687
  53.9 3.3 %shard_map.161 = (f32[45,64,128]{2,1,0:T(8,128)S(1)}, bf16[384,1024]{1,0:T(8,128)(2,1)S(1)}) custom-call(bf16[3,192,640]{2,1,0:T(8,128)(2,1)S(1)} %get-tuple-element.36.lines, bf16[576,192]{1,0:T(8,128)(2,1)} %copy-done, f32[64,128]{1,0:T(8,128)} %copy-done.1, f32[64,128]{1,0:T(8,128)} %copy-done.2, bf16[27,64,64]{2,1,0:T(8,128)(2,1)} %kernel_in.3, ...), custom_call_target="tpu_custom_call" | custom-call | tf_op jit(solution)/shard_map/pallas_call | solution.py:688
  57.2 7.1 %all-to-all-done.1.received = f32[16,32,128]{2,1,0:T(8,128)S(1)} async-done(((f32[16,32,128]{2,1,0:T(8,128)}), f32[16,32,128]{2,1,0:T(8,128)S(1)}, u32[]{:S(2)}, u32[]{:S(2)}) %all-to-all-start.1) | async-done | bytes 262176 | tf_op jit(solution)/shard_map/all_to_all | solution.py:687
  64.3 2.2 %shard_map.162 = (bf16[8,4,64,128]{3,2,1,0:T(8,128)(2,1)}, bf16[1024,128]{1,0:T(8,128)(2,1)}) custom-call(f32[16,32,128]{2,1,0:T(8,128)S(1)} %all-to-all-done.1.received, f32[45,64,128]{2,1,0:T(8,128)S(1)} %get-tuple-element.37.slopes, bf16[3,192,640]{2,1,0:T(8,128)(2,1)S(1)} %get-tuple-element.36.lines), custom_call_target="tpu_custom_call" | custom-call | tf_op jit(solution)/shard_map/pallas_call | solution.py:689
  66.5 11.8 %all-to-all-start.2 = ((bf16[64,16,128]{2,1,0:T(8,128)(2,1)}), bf16[64,16,128]{2,1,0:T(8,128)(2,1)S(1)}, u32[]{:S(2)}, u32[]{:S(2)}) async-start(bf16[64,16,128]{2,1,0:T(8,128)(2,1)} %bitcast.7), calls=%async_computation.2 | async-start | bytes 524288 | tf_op jit(solution)/shard_map/all_to_all | solution.py:692
  78.3 12.6 %all-to-all-done.2.received = bf16[64,16,128]{2,1,0:T(8,128)(2,1)S(1)} async-done(((bf16[64,16,128]{2,1,0:T(8,128)(2,1)}), bf16[64,16,128]{2,1,0:T(8,128)(2,1)S(1)}, u32[]{:S(2)}, u32[]{:S(2)}) %all-to-all-start.2) | async-done | bytes 262176 | tf_op jit(solution)/shard_map/all_to_all | solution.py:692
  91.0 0.1 shard_map.164
  91.0 13.8 %all_to_all.25.received = f32[8,16,128]{2,1,0:T(8,128)S(1)} all-to-all(f32[8,16,128]{2,1,0:T(8,128)S(1)} %shard_map.164), channel_id=1, replica_groups=mesh['xlo'=2,'z'=8,'y'=8,'xhi'=2,'core'=2] {'y'}, dimensions={0} | all-to-all | bytes 131072 | tf_op jit(solution)/shard_map/all_to_all | solution.py:695
  104.8 0.7 shard_map.165
  105.5 6.9 %all-to-all-start.4 = ((bf16[64,16,128]{2,1,0:T(8,128)(2,1)}), bf16[64,16,128]{2,1,0:T(8,128)(2,1)S(1)}, u32[]{:S(2)}, u32[]{:S(2)}) async-start(bf16[64,16,128]{2,1,0:T(8,128)(2,1)} %shard_map.165), calls=%async_computation.4 | async-start | bytes 524288 | tf_op jit(solution)/shard_map/all_to_all | solution.py:697
  112.4 2.8 %shard_map.163 = f32[3,1,64,64]{3,2,1,0:T(8,128)} custom-call(bf16[8,4,64,128]{3,2,1,0:T(8,128)(2,1)} %get-tuple-element.38.low_in, bf16[384,1024]{1,0:T(8,128)(2,1)S(1)} %get-tuple-element.39.folded, bf16[1024,128]{1,0:T(8,128)(2,1)} %get-tuple-element.40.after), custom_call_target="tpu_custom_call" | custom-call | tf_op jit(solution)/shard_map/pallas_call | solution.py:690
  115.2 9.9 %all-to-all-done.4 = bf16[64,16,128]{2,1,0:T(8,128)(2,1)S(1)} async-done(((bf16[64,16,128]{2,1,0:T(8,128)(2,1)}), bf16[64,16,128]{2,1,0:T(8,128)(2,1)S(1)}, u32[]{:S(2)}, u32[]{:S(2)}) %all-to-all-start.4) | async-done | bytes 262176 | tf_op jit(solution)/shard_map/all_to_all | solution.py:697
  125.1 1.0 shard_map.166
Async XLA Ops:
  0.6 13.5 %collective-permute-start.1 = (bf16[3,64,64]{2,1,0:T(8,128)(2,1)}, bf16[3,64,64]{2,1,0:T(8,128)(2,1)S(1)}, u32[]{:S(2)}, u32[]{:S(2)}) collective-permute-start(bf16[3,64,64]{2,1,0:T(8,128)(2,1)} %bitcast.15), channel_id=1, source_target_pairs={{1,0},{2,1},{3,2},{4,3},{5,4},{6,5},{7,6},{8,7},{9,8},{10,9},{11,1... | collective-permute-start | bytes 73736 | tf_op jit(solution)/shard_map/ppermute | solution.py:639
  9.4 4.7 %collective-permute-start = (bf16[3,64,64]{2,1,0:T(8,128)(2,1)}, bf16[3,64,64]{2,1,0:T(8,128)(2,1)S(1)}, u32[]{:S(2)}, u32[]{:S(2)}) collective-permute-start(bf16[3,64,64]{2,1,0:T(8,128)(2,1)} %bitcast.16), channel_id=1, source_target_pairs={{0,1},{1,2},{2,3},{3,4},{4,5},{5,6},{6,7},{7,8},{8,9},{9,10},{10,1... | collective-permute-start | bytes 73736 | tf_op jit(solution)/shard_map/ppermute | solution.py:638
  11.4 0.7 copy-start.3
  12.0 0.7 copy-start.4
  14.1 15.1 %copy-start.1 = (f32[64,128]{1,0:T(8,128)}, f32[64,128]{1,0:T(8,128)S(1)}, u32[]{:S(2)}) copy-start(f32[64,128]{1,0:T(8,128)S(1)} %get-tuple-element.31.bias.bias_in) | copy-start | bytes 98308
  14.1 15.1 %copy-start.2 = (f32[64,128]{1,0:T(8,128)}, f32[64,128]{1,0:T(8,128)S(1)}, u32[]{:S(2)}) copy-start(f32[64,128]{1,0:T(8,128)S(1)} %get-tuple-element.32.head.head_in) | copy-start | bytes 98308
  14.1 27.8 %copy-start = (bf16[576,192]{1,0:T(8,128)(2,1)}, bf16[576,192]{1,0:T(8,128)(2,1)S(1)}, u32[]{:S(2)}) copy-start(bf16[576,192]{1,0:T(8,128)(2,1)S(1)} %get-tuple-element.30.wall.wall_in) | copy-start | bytes 663556
  14.2 12.2 %collective-permute-start.5 = (bf16[9,32,128]{2,1,0:T(8,128)(2,1)S(1)}, bf16[9,32,128]{2,1,0:T(8,128)(2,1)S(1)}, u32[]{:S(2)}, u32[]{:S(2)}) collective-permute-start(bf16[9,32,128]{2,1,0:T(8,128)(2,1)S(1)} %shard_map.157.own), channel_id=1, source_target_pairs={{32,0},{64,32},{96,64},{128,96},{160,128},{192,160},{224,192},{256... | collective-permute-start | bytes 221192 | tf_op jit(solution)/shard_map/ppermute | solution.py:639
  15.5 10.9 %collective-permute-start.4 = (bf16[9,32,128]{2,1,0:T(8,128)(2,1)S(1)}, bf16[9,32,128]{2,1,0:T(8,128)(2,1)S(1)}, u32[]{:S(2)}, u32[]{:S(2)}) collective-permute-start(bf16[9,32,128]{2,1,0:T(8,128)(2,1)S(1)} %shard_map.157.own), channel_id=1, source_target_pairs={{0,32},{32,64},{64,96},{96,128},{128,160},{160,192},{192,224},{224... | collective-permute-start | bytes 221192 | tf_op jit(solution)/shard_map/ppermute | solution.py:638
  19.5 19.9 %collective-permute-start.2 = (f32[24,32,128]{2,1,0:T(8,128)S(1)}, f32[24,32,128]{2,1,0:T(8,128)S(1)}, u32[]{:S(2)}, u32[]{:S(2)}) collective-permute-start(f32[24,32,128]{2,1,0:T(8,128)S(1)} %get-tuple-element.27), channel_id=1, source_target_pairs={{0,1},{1,2},{2,3},{3,4},{4,5},{5,6},{6,7},{7,8},{8,9},{9,10},{10,1... | collective-permute-start | bytes 1179656 | tf_op jit(solution)/shard_map/ppermute | solution.py:638
  24.4 14.9 %collective-permute-start.3 = (f32[24,32,128]{2,1,0:T(8,128)S(1)}, f32[24,32,128]{2,1,0:T(8,128)S(1)}, u32[]{:S(2)}, u32[]{:S(2)}) collective-permute-start(f32[24,32,128]{2,1,0:T(8,128)S(1)} %get-tuple-element.28), channel_id=1, source_target_pairs={{1,0},{2,1},{3,2},{4,3},{5,4},{6,5},{7,6},{8,7},{9,8},{10,9},{11,1... | collective-permute-start | bytes 1179656 | tf_op jit(solution)/shard_map/ppermute | solution.py:639
  29.2 17.8 %all-to-all-start = ((f32[16,32,128]{2,1,0:T(8,128)}), f32[16,32,128]{2,1,0:T(8,128)S(1)}, u32[]{:S(2)}, u32[]{:S(2)}) async-start(f32[16,32,128]{2,1,0:T(8,128)} %get-tuple-element.33.after), calls=%async_computation | async-start | bytes 524288 | tf_op jit(solution)/shard_map/all_to_all | solution.py:672
  49.9 14.4 %all-to-all-start.1 = ((f32[16,32,128]{2,1,0:T(8,128)}), f32[16,32,128]{2,1,0:T(8,128)S(1)}, u32[]{:S(2)}, u32[]{:S(2)}) async-start(f32[16,32,128]{2,1,0:T(8,128)} %shard_map.160.after), calls=%async_computation.1 | async-start | bytes 524288 | tf_op jit(solution)/shard_map/all_to_all | solution.py:687
  66.5 24.5 %all-to-all-start.2 = ((bf16[64,16,128]{2,1,0:T(8,128)(2,1)}), bf16[64,16,128]{2,1,0:T(8,128)(2,1)S(1)}, u32[]{:S(2)}, u32[]{:S(2)}) async-start(bf16[64,16,128]{2,1,0:T(8,128)(2,1)} %bitcast.7), calls=%async_computation.2 | async-start | bytes 524288 | tf_op jit(solution)/shard_map/all_to_all | solution.py:692
  105.5 19.5 %all-to-all-start.4 = ((bf16[64,16,128]{2,1,0:T(8,128)(2,1)}), bf16[64,16,128]{2,1,0:T(8,128)(2,1)S(1)}, u32[]{:S(2)}, u32[]{:S(2)}) async-start(bf16[64,16,128]{2,1,0:T(8,128)(2,1)} %shard_map.165), calls=%async_computation.4 | async-start | bytes 524288 | tf_op jit(solution)/shard_map/all_to_all | solution.py:697

commit v7 on v6

--- a/solution.py
+++ b/solution.py
@@ -59,7 +59,7 @@
     density,
     latent,
     kernel_in,
-    bias,
+    bias_in,
     head,
     to_next,
     to_prev,
@@ -68,10 +68,12 @@
     bias_wide,
     head_wide,
     kernel,
+    bias,
     sems,
 ):
     copies = [
         pltpu.make_async_copy(kernel_in, kernel, sems.at[11]),
+        pltpu.make_async_copy(bias_in, bias, sems.at[12]),
         pltpu.make_async_copy(latent, coarse, sems.at[10]),
     ]
     fields = ((wave_now, 6), (wave_prev, 5), (adj_next, 4), (adj_after, 3), (density, 6))
@@ -83,18 +85,18 @@
         copies.append(pltpu.make_async_copy(field.at[pl.ds(0, rows)], to_prev.at[here], sems.at[5 + i]))
         at += rows
     start_all(copies)
+    head_wide[...] = jnp.broadcast_to(head[...].astype(F32), (128, 64)).T
+    wait_all(copies[:2])
     bias_wide[...] = jnp.broadcast_to(bias[...], (128, 64)).T
-    head_wide[...] = jnp.broadcast_to(head[...].astype(F32), (128, 64)).T
-    copies[0].wait()
     for a in range(3):
         for b in range(3):
             at = 64 * (3 * b + a)
             taps = [kernel[9 * a + 3 * b + e] for e in range(3)]
             wall[at : at + 64, :] = jnp.concatenate(taps, axis=1)
-    wait_all(copies[1:])
-
-
-def join_kernel(low, middle, high, out):
+    wait_all(copies[2:])
+
+
+def join_kernel(high, middle, low, out):
     for i, ref in enumerate((low, middle, high)):
         for x in range(3):
             out[3 * i + x] = jnp.concatenate([ref[x, 0:32], ref[x, 32:64]], axis=1)
@@ -133,7 +135,7 @@
             store(a, zz, total)
 
 
-def decode_kernel(z_prev, own, z_next, wall, bias, head, speed_out, lines_out, lines, sums, row_logit):
+def decode_kernel(z_next, own, z_prev, wall, bias, head, speed_out, lines_out, lines, sums, row_logit):
     spread = spread_matrix()
     for zi, ref in enumerate((z_prev, own, z_next)):
         packed = [ref[x] for x in range(9)]
@@ -542,8 +544,8 @@
         shape((64, 128)),
         shape((64, 128)),
     ),
-    [HBM] * 7 + [VMEM] * 2,
-    [pltpu.VMEM((27, 64, 64), BF16), pltpu.SemaphoreType.DMA((12,))],
+    [HBM] * 8 + [VMEM],
+    [pltpu.VMEM((27, 64, 64), BF16), pltpu.VMEM((1, 64), F32), pltpu.SemaphoreType.DMA((13,))],
     6,
 )
 join = call(join_kernel, shape((9, 32, 128), BF16), [VMEM] * 3, (), 2)
@@ -661,14 +663,14 @@
     coarse = latent.reshape(3, 64, 64)
     low, high = shifted((coarse, coarse), TILE, 32)
     to_next, to_prev, middle, wall, bias, head = pack(
-        *fields, in_hbm(coarse), taps, conv_bias.reshape(1, 64), head_weight.reshape(1, 64)
-    )
-    nine = join(low, middle, high)
+        *fields, in_hbm(coarse), taps, in_hbm(conv_bias.reshape(1, 64)), head_weight.reshape(1, 64)
+    )
+    nine = join(high, middle, low)
     z_prev, z_next = shifted((nine, nine), SHOT, 16)
     to_next, to_prev, nine = lax.optimization_barrier((to_next, to_prev, nine))
     left, right = shifted((to_next, to_prev), TILE, 32)
 
-    speed, lines = decode(z_prev, nine, z_next, wall, bias, head)
+    speed, lines = decode(z_next, nine, z_prev, wall, bias, head)
     speeds = lax.all_to_all(speed, SHOT, 0, 0, tiled=True)
     records = jnp.transpose(observed, (1, 0, 2))
     own, counts = medium(

time: 127 us -> 126 us (level)
  starting transfers between devices: 55.1 us -> 52.4 us
  waiting for transfers between devices: 34.7 us -> 36.4 us
    ppermute x3, starting transfers between devices: 12 us -> 7.32 us  [shifted(): high = lax.ppermute(block[1], axes, [(i + 1, i) for i in range(size - 1)])]
    all_to_all x1, waiting for transfers between devices: 5.08 us -> 7.26 us  [per_device(): speeds = lax.all_to_all(speed, SHOT, 0, 0, tiled=True)]
    all_to_all x1, starting transfers between devices: 9.51 us -> 11.5 us  [per_device(): speeds = lax.all_to_all(speed, SHOT, 0, 0, tiled=True)]
    all_to_all x1, starting transfers between devices: 11.8 us -> 9.89 us  [per_device(): pieces = lax.all_to_all(parts.reshape(64, 16, 128), NEAR, 0, 0, tiled=True)]
    ppermute x3, starting transfers between devices: 10.8 us -> 12.4 us  [shifted(): low = lax.ppermute(block[0], axes, [(i, i + 1) for i in range(size - 1)])]
    all_to_all x1, waiting for transfers between devices: 7.08 us -> 5.59 us  [per_device(): received = lax.all_to_all(strips, SHOT, 0, 0, tiled=True)]
  transfers between devices with their start and end apart: 10 -> 10, of which waited for: 4 -> 6; matrix products, arithmetic and copies ran while one was open for 0% -> 0% of each run, Pallas kernels for 10% -> 10%
where the time goes in v7:
time: 126 us; the launch traced here: 125 us
  starting transfers between devices  52.4 us (42%)
  waiting for transfers between devices  36.4 us (29%)
  Pallas kernels  19.8 us (16%)
  blocking collectives  14.4 us (11%)
  between operations  1.52 us (1%)
    all_to_all x1, blocking collectives, per_device(): pieces = lax.all_to_all(pieces, 'y', 0, 0, tiled=True)  14.4 us
    all_to_all x1, waiting for transfers between devices, per_device(): pieces = lax.all_to_all(parts.reshape(64, 16, 128), NEAR, 0, 0, tiled=True)  12.6 us
    ppermute x3, starting transfers between devices, shifted(): low = lax.ppermute(block[0], axes, [(i, i + 1) for i in range(size - 1)])  12.4 us
    all_to_all x1, starting transfers between devices, per_device(): speeds = lax.all_to_all(speed, SHOT, 0, 0, tiled=True)  11.5 us
    all_to_all x1, starting transfers between devices, per_device(): pieces = lax.all_to_all(parts.reshape(64, 16, 128), NEAR, 0, 0, tiled=True)  9.89 us
    all_to_all x1, waiting for transfers between devices, per_device(): whole = lax.all_to_all(pieces, NEAR, 0, 0, tiled=True)  9.87 us
    ppermute x3, starting transfers between devices, shifted(): high = lax.ppermute(block[1], axes, [(i + 1, i) for i in range(size - 1)])  7.32 us
    all_to_all x1, waiting for transfers between devices, per_device(): speeds = lax.all_to_all(speed, SHOT, 0, 0, tiled=True)  7.26 us
  transfers between devices with their start and end apart: 10, of which 6 were waited for; matrix products, arithmetic and copies ran while one was open for 0% of the time, Pallas kernels for 10%

profile of v7, /device:TPU:1, one launch (start us, length us, event | category | flops | bytes accessed | tf_op | source)
XLA Modules:
  0.0 125.1 jit_solution(9401776903245886620)
XLA Ops:
  0.6 6.0 %collective-permute-start.1 = (bf16[3,64,64]{2,1,0:T(8,128)(2,1)}, bf16[3,64,64]{2,1,0:T(8,128)(2,1)S(1)}, u32[]{:S(2)}, u32[]{:S(2)}) collective-permute-start(bf16[3,64,64]{2,1,0:T(8,128)(2,1)} %bitcast.14), channel_id=1, source_target_pairs={{0,1},{1,2},{2,3},{3,4},{4,5},{5,6},{6,7},{7,8},{8,9},{9,10},{10,1... | collective-permute-start | bytes 73736 | tf_op jit(solution)/shard_map/ppermute | solution.py:640
  6.7 4.0 %collective-permute-start = (bf16[3,64,64]{2,1,0:T(8,128)(2,1)}, bf16[3,64,64]{2,1,0:T(8,128)(2,1)S(1)}, u32[]{:S(2)}, u32[]{:S(2)}) collective-permute-start(bf16[3,64,64]{2,1,0:T(8,128)(2,1)} %bitcast.15), channel_id=1, source_target_pairs={{1,0},{2,1},{3,2},{4,3},{5,4},{6,5},{7,6},{8,7},{9,8},{10,9},{11,1... | collective-permute-start | bytes 73736 | tf_op jit(solution)/shard_map/ppermute | solution.py:641
  10.7 0.0 copy-start.3
  10.7 0.6 copy-done.3
  11.4 1.4 %shard_map.156 = (f32[24,32,128]{2,1,0:T(8,128)S(1)}, f32[24,32,128]{2,1,0:T(8,128)S(1)}, bf16[3,64,64]{2,1,0:T(8,128)(2,1)S(1)}, bf16[576,192]{1,0:T(8,128)(2,1...) custom-call(f32[1,6,32,128]{3,2,1,0:T(8,128)} %wave_now.3, f32[1,6,32,128]{3,2,1,0:T(8,128)} %wave_prev.3, ...), custom_call_target="tpu_custom_call" | custom-call | tf_op jit(solution)/shard_map/pallas_call | solution.py:665
  12.8 0.0 copy-start.1
  12.8 0.0 copy-start.2
  12.8 0.0 copy-start
  12.8 0.0 collective-permute-done.1.low
  12.8 1.0 collective-permute-done.high
  13.8 0.1 shard_map.157.own
  13.9 4.0 %collective-permute-start.5 = (bf16[9,32,128]{2,1,0:T(8,128)(2,1)S(1)}, bf16[9,32,128]{2,1,0:T(8,128)(2,1)S(1)}, u32[]{:S(2)}, u32[]{:S(2)}) collective-permute-start(bf16[9,32,128]{2,1,0:T(8,128)(2,1)S(1)} %shard_map.157.own), channel_id=1, source_target_pairs={{0,32},{32,64},{64,96},{96,128},{128,160},{160,192},{192,224},{224... | collective-permute-start | bytes 221192 | tf_op jit(solution)/shard_map/ppermute | solution.py:640
  17.9 1.3 %collective-permute-start.4 = (bf16[9,32,128]{2,1,0:T(8,128)(2,1)S(1)}, bf16[9,32,128]{2,1,0:T(8,128)(2,1)S(1)}, u32[]{:S(2)}, u32[]{:S(2)}) collective-permute-start(bf16[9,32,128]{2,1,0:T(8,128)(2,1)S(1)} %shard_map.157.own), channel_id=1, source_target_pairs={{32,0},{64,32},{96,64},{128,96},{160,128},{192,160},{224,192},{256... | collective-permute-start | bytes 221192 | tf_op jit(solution)/shard_map/ppermute | solution.py:641
  19.2 2.4 %collective-permute-start.2 = (f32[24,32,128]{2,1,0:T(8,128)S(1)}, f32[24,32,128]{2,1,0:T(8,128)S(1)}, u32[]{:S(2)}, u32[]{:S(2)}) collective-permute-start(f32[24,32,128]{2,1,0:T(8,128)S(1)} %get-tuple-element.27), channel_id=1, source_target_pairs={{0,1},{1,2},{2,3},{3,4},{4,5},{5,6},{6,7},{7,8},{8,9},{9,10},{10,1... | collective-permute-start | bytes 1179656 | tf_op jit(solution)/shard_map/ppermute | solution.py:640
  21.6 2.0 %collective-permute-start.3 = (f32[24,32,128]{2,1,0:T(8,128)S(1)}, f32[24,32,128]{2,1,0:T(8,128)S(1)}, u32[]{:S(2)}, u32[]{:S(2)}) collective-permute-start(f32[24,32,128]{2,1,0:T(8,128)S(1)} %get-tuple-element.28), channel_id=1, source_target_pairs={{1,0},{2,1},{3,2},{4,3},{5,4},{6,5},{7,6},{8,7},{9,8},{10,9},{11,1... | collective-permute-start | bytes 1179656 | tf_op jit(solution)/shard_map/ppermute | solution.py:641
  23.6 0.0 collective-permute-done.5.z_prev
  23.6 0.1 collective-permute-done.4.z_next
  23.6 2.8 %shard_map.158 = (f32[16,32,128]{2,1,0:T(8,128)}, bf16[3,192,640]{2,1,0:T(8,128)(2,1)S(1)}) custom-call(bf16[9,32,128]{2,1,0:T(8,128)(2,1)S(1)} %collective-permute-done.4.z_next, bf16[9,32,128]{2,1,0:T(8,128)(2,1)S(1)} %shard_map.157.own, bf16[9,32,128]{2,1,0:T(8,128)(2,1)S(1)} %collective-permute-done.5.z_prev, ...), custom_call_target="tpu_custom_call" | custom-call | flops 500000000 | tf_op jit(solution)/shard_map/pallas_call | solution.py:673
  26.5 0.0 copy-done.1
  26.5 0.0 copy-done.2
  26.5 11.5 %all-to-all-start = ((f32[16,32,128]{2,1,0:T(8,128)}), f32[16,32,128]{2,1,0:T(8,128)S(1)}, u32[]{:S(2)}, u32[]{:S(2)}) async-start(f32[16,32,128]{2,1,0:T(8,128)} %get-tuple-element.33.after), calls=%async_computation | async-start | bytes 524288 | tf_op jit(solution)/shard_map/all_to_all | solution.py:674
  38.6 0.0 collective-permute-done.2.left
  38.6 0.0 collective-permute-done.3.right
  38.6 2.5 %shard_map.159 = (f32[30,32,128]{2,1,0:T(8,128)S(1)}, f32[4,384,128]{2,1,0:T(8,128)}) custom-call(s32[1]{0:T(128)} %bitcast.place, f32[1,6,32,128]{3,2,1,0:T(8,128)} %wave_now.3, f32[1,6,32,128]{3,2,1,0:T(8,128)} %wave_prev.3, f32[1,6,32,128]{3,2,1,0:T(8,128)} %adj_next.3, f32[1,6,32,128]{3,2,1,0:T(8,128)} %adj_after.3, f32[6,32,128]{2,1,0:T(8,128)} %density.3, ...), custom_call_target="tpu_custom_call" | custom-call | flops 2000000000 | tf_op jit(solution)/shard_map/pallas_call | solution.py:676
  41.1 0.0 copy-done
  41.1 7.3 %all-to-all-done = f32[16,32,128]{2,1,0:T(8,128)S(1)} async-done(((f32[16,32,128]{2,1,0:T(8,128)}), f32[16,32,128]{2,1,0:T(8,128)S(1)}, u32[]{:S(2)}, u32[]{:S(2)}) %all-to-all-start) | async-done | bytes 262176 | tf_op jit(solution)/shard_map/all_to_all | solution.py:674
  48.4 2.9 %shard_map.160.after = f32[16,32,128]{2,1,0:T(8,128)} custom-call(s32[1]{0:T(128)} %bitcast.place, s32[1]{0:T(128)S(6)} %copy.17.source, f32[1,3]{1,0:T(1,128)} %pulses_in.1, f32[24,32,128]{2,1,0:T(8,128)S(1)} %collective-permute-done.2.left, f32[24,32,128]{2,1,0:T(8,128)S(1)} %collective-permute-done.3.right, f32[512,128]{1,0:T(8,128)S(1)} %bitcast.12, ...), custom_call_target="tpu_custom_call" | custom-call | tf_op jit(solution)/shard_map/pallas_call | solution.py:679
  51.3 4.4 %all-to-all-start.1 = ((f32[16,32,128]{2,1,0:T(8,128)}), f32[16,32,128]{2,1,0:T(8,128)S(1)}, u32[]{:S(2)}, u32[]{:S(2)}) async-start(f32[16,32,128]{2,1,0:T(8,128)} %shard_map.160.after), calls=%async_computation.1 | async-start | bytes 524288 | tf_op jit(solution)/shard_map/all_to_all | solution.py:689
  55.7 3.3 %shard_map.161 = (f32[45,64,128]{2,1,0:T(8,128)S(1)}, bf16[384,1024]{1,0:T(8,128)(2,1)S(1)}) custom-call(bf16[3,192,640]{2,1,0:T(8,128)(2,1)S(1)} %get-tuple-element.36.lines, bf16[576,192]{1,0:T(8,128)(2,1)} %copy-done, f32[64,128]{1,0:T(8,128)} %copy-done.1, f32[64,128]{1,0:T(8,128)} %copy-done.2, bf16[27,64,64]{2,1,0:T(8,128)(2,1)} %kernel_in.3, ...), custom_call_target="tpu_custom_call" | custom-call | tf_op jit(solution)/shard_map/pallas_call | solution.py:690
  59.1 5.6 %all-to-all-done.1.received = f32[16,32,128]{2,1,0:T(8,128)S(1)} async-done(((f32[16,32,128]{2,1,0:T(8,128)}), f32[16,32,128]{2,1,0:T(8,128)S(1)}, u32[]{:S(2)}, u32[]{:S(2)}) %all-to-all-start.1) | async-done | bytes 262176 | tf_op jit(solution)/shard_map/all_to_all | solution.py:689
  64.6 2.2 %shard_map.162 = (bf16[8,4,64,128]{3,2,1,0:T(8,128)(2,1)}, bf16[1024,128]{1,0:T(8,128)(2,1)}) custom-call(f32[16,32,128]{2,1,0:T(8,128)S(1)} %all-to-all-done.1.received, f32[45,64,128]{2,1,0:T(8,128)S(1)} %get-tuple-element.37.slopes, bf16[3,192,640]{2,1,0:T(8,128)(2,1)S(1)} %get-tuple-element.36.lines), custom_call_target="tpu_custom_call" | custom-call | tf_op jit(solution)/shard_map/pallas_call | solution.py:691
  66.8 9.9 %all-to-all-start.2 = ((bf16[64,16,128]{2,1,0:T(8,128)(2,1)}), bf16[64,16,128]{2,1,0:T(8,128)(2,1)S(1)}, u32[]{:S(2)}, u32[]{:S(2)}) async-start(bf16[64,16,128]{2,1,0:T(8,128)(2,1)} %bitcast.7), calls=%async_computation.2 | async-start | bytes 524288 | tf_op jit(solution)/shard_map/all_to_all | solution.py:694
  76.7 12.6 %all-to-all-done.2.received = bf16[64,16,128]{2,1,0:T(8,128)(2,1)S(1)} async-done(((bf16[64,16,128]{2,1,0:T(8,128)(2,1)}), bf16[64,16,128]{2,1,0:T(8,128)(2,1)S(1)}, u32[]{:S(2)}, u32[]{:S(2)}) %all-to-all-start.2) | async-done | bytes 262176 | tf_op jit(solution)/shard_map/all_to_all | solution.py:694
  89.4 0.1 shard_map.164
  89.4 14.4 %all_to_all.25.received = f32[8,16,128]{2,1,0:T(8,128)S(1)} all-to-all(f32[8,16,128]{2,1,0:T(8,128)S(1)} %shard_map.164), channel_id=1, replica_groups=mesh['xlo'=2,'z'=8,'y'=8,'xhi'=2,'core'=2] {'y'}, dimensions={0} | all-to-all | bytes 131072 | tf_op jit(solution)/shard_map/all_to_all | solution.py:697
  103.8 0.7 shard_map.165
  104.5 6.9 %all-to-all-start.4 = ((bf16[64,16,128]{2,1,0:T(8,128)(2,1)}), bf16[64,16,128]{2,1,0:T(8,128)(2,1)S(1)}, u32[]{:S(2)}, u32[]{:S(2)}) async-start(bf16[64,16,128]{2,1,0:T(8,128)(2,1)} %shard_map.165), calls=%async_computation.4 | async-start | bytes 524288 | tf_op jit(solution)/shard_map/all_to_all | solution.py:699
  111.4 2.8 %shard_map.163 = f32[3,1,64,64]{3,2,1,0:T(8,128)} custom-call(bf16[8,4,64,128]{3,2,1,0:T(8,128)(2,1)} %get-tuple-element.38.low_in, bf16[384,1024]{1,0:T(8,128)(2,1)S(1)} %get-tuple-element.39.folded, bf16[1024,128]{1,0:T(8,128)(2,1)} %get-tuple-element.40.after), custom_call_target="tpu_custom_call" | custom-call | tf_op jit(solution)/shard_map/pallas_call | solution.py:692
  114.2 9.9 %all-to-all-done.4 = bf16[64,16,128]{2,1,0:T(8,128)(2,1)S(1)} async-done(((bf16[64,16,128]{2,1,0:T(8,128)(2,1)}), bf16[64,16,128]{2,1,0:T(8,128)(2,1)S(1)}, u32[]{:S(2)}, u32[]{:S(2)}) %all-to-all-start.4) | async-done | bytes 262176 | tf_op jit(solution)/shard_map/all_to_all | solution.py:699
  124.1 1.0 shard_map.166
Async XLA Ops:
  0.6 12.2 %collective-permute-start.1 = (bf16[3,64,64]{2,1,0:T(8,128)(2,1)}, bf16[3,64,64]{2,1,0:T(8,128)(2,1)S(1)}, u32[]{:S(2)}, u32[]{:S(2)}) collective-permute-start(bf16[3,64,64]{2,1,0:T(8,128)(2,1)} %bitcast.14), channel_id=1, source_target_pairs={{0,1},{1,2},{2,3},{3,4},{4,5},{5,6},{6,7},{7,8},{8,9},{9,10},{10,1... | collective-permute-start | bytes 73736 | tf_op jit(solution)/shard_map/ppermute | solution.py:640
  6.7 7.1 %collective-permute-start = (bf16[3,64,64]{2,1,0:T(8,128)(2,1)}, bf16[3,64,64]{2,1,0:T(8,128)(2,1)S(1)}, u32[]{:S(2)}, u32[]{:S(2)}) collective-permute-start(bf16[3,64,64]{2,1,0:T(8,128)(2,1)} %bitcast.15), channel_id=1, source_target_pairs={{1,0},{2,1},{3,2},{4,3},{5,4},{6,5},{7,6},{8,7},{9,8},{10,9},{11,1... | collective-permute-start | bytes 73736 | tf_op jit(solution)/shard_map/ppermute | solution.py:641
  10.7 0.7 copy-start.3
  12.8 13.7 %copy-start.1 = (f32[64,128]{1,0:T(8,128)}, f32[64,128]{1,0:T(8,128)S(1)}, u32[]{:S(2)}) copy-start(f32[64,128]{1,0:T(8,128)S(1)} %get-tuple-element.31.bias.bias_in) | copy-start | bytes 98308
  12.8 13.7 %copy-start.2 = (f32[64,128]{1,0:T(8,128)}, f32[64,128]{1,0:T(8,128)S(1)}, u32[]{:S(2)}) copy-start(f32[64,128]{1,0:T(8,128)S(1)} %get-tuple-element.32.head.head_in) | copy-start | bytes 98308
  12.8 28.3 %copy-start = (bf16[576,192]{1,0:T(8,128)(2,1)}, bf16[576,192]{1,0:T(8,128)(2,1)S(1)}, u32[]{:S(2)}) copy-start(bf16[576,192]{1,0:T(8,128)(2,1)S(1)} %get-tuple-element.30.wall.wall_in) | copy-start | bytes 663556
  13.9 9.7 %collective-permute-start.5 = (bf16[9,32,128]{2,1,0:T(8,128)(2,1)S(1)}, bf16[9,32,128]{2,1,0:T(8,128)(2,1)S(1)}, u32[]{:S(2)}, u32[]{:S(2)}) collective-permute-start(bf16[9,32,128]{2,1,0:T(8,128)(2,1)S(1)} %shard_map.157.own), channel_id=1, source_target_pairs={{0,32},{32,64},{64,96},{96,128},{128,160},{160,192},{192,224},{224... | collective-permute-start | bytes 221192 | tf_op jit(solution)/shard_map/ppermute | solution.py:640
  17.9 5.7 %collective-permute-start.4 = (bf16[9,32,128]{2,1,0:T(8,128)(2,1)S(1)}, bf16[9,32,128]{2,1,0:T(8,128)(2,1)S(1)}, u32[]{:S(2)}, u32[]{:S(2)}) collective-permute-start(bf16[9,32,128]{2,1,0:T(8,128)(2,1)S(1)} %shard_map.157.own), channel_id=1, source_target_pairs={{32,0},{64,32},{96,64},{128,96},{160,128},{192,160},{224,192},{256... | collective-permute-start | bytes 221192 | tf_op jit(solution)/shard_map/ppermute | solution.py:641
  19.2 19.4 %collective-permute-start.2 = (f32[24,32,128]{2,1,0:T(8,128)S(1)}, f32[24,32,128]{2,1,0:T(8,128)S(1)}, u32[]{:S(2)}, u32[]{:S(2)}) collective-permute-start(f32[24,32,128]{2,1,0:T(8,128)S(1)} %get-tuple-element.27), channel_id=1, source_target_pairs={{0,1},{1,2},{2,3},{3,4},{4,5},{5,6},{6,7},{7,8},{8,9},{9,10},{10,1... | collective-permute-start | bytes 1179656 | tf_op jit(solution)/shard_map/ppermute | solution.py:640
  21.6 17.1 %collective-permute-start.3 = (f32[24,32,128]{2,1,0:T(8,128)S(1)}, f32[24,32,128]{2,1,0:T(8,128)S(1)}, u32[]{:S(2)}, u32[]{:S(2)}) collective-permute-start(f32[24,32,128]{2,1,0:T(8,128)S(1)} %get-tuple-element.28), channel_id=1, source_target_pairs={{1,0},{2,1},{3,2},{4,3},{5,4},{6,5},{7,6},{8,7},{9,8},{10,9},{11,1... | collective-permute-start | bytes 1179656 | tf_op jit(solution)/shard_map/ppermute | solution.py:641
  26.5 21.9 %all-to-all-start = ((f32[16,32,128]{2,1,0:T(8,128)}), f32[16,32,128]{2,1,0:T(8,128)S(1)}, u32[]{:S(2)}, u32[]{:S(2)}) async-start(f32[16,32,128]{2,1,0:T(8,128)} %get-tuple-element.33.after), calls=%async_computation | async-start | bytes 524288 | tf_op jit(solution)/shard_map/all_to_all | solution.py:674
  51.3 13.3 %all-to-all-start.1 = ((f32[16,32,128]{2,1,0:T(8,128)}), f32[16,32,128]{2,1,0:T(8,128)S(1)}, u32[]{:S(2)}, u32[]{:S(2)}) async-start(f32[16,32,128]{2,1,0:T(8,128)} %shard_map.160.after), calls=%async_computation.1 | async-start | bytes 524288 | tf_op jit(solution)/shard_map/all_to_all | solution.py:689
  66.8 22.5 %all-to-all-start.2 = ((bf16[64,16,128]{2,1,0:T(8,128)(2,1)}), bf16[64,16,128]{2,1,0:T(8,128)(2,1)S(1)}, u32[]{:S(2)}, u32[]{:S(2)}) async-start(bf16[64,16,128]{2,1,0:T(8,128)(2,1)} %bitcast.7), calls=%async_computation.2 | async-start | bytes 524288 | tf_op jit(solution)/shard_map/all_to_all | solution.py:694
  104.5 19.5 %all-to-all-start.4 = ((bf16[64,16,128]{2,1,0:T(8,128)(2,1)}), bf16[64,16,128]{2,1,0:T(8,128)(2,1)S(1)}, u32[]{:S(2)}, u32[]{:S(2)}) async-start(bf16[64,16,128]{2,1,0:T(8,128)(2,1)} %shard_map.165), calls=%async_computation.4 | async-start | bytes 524288 | tf_op jit(solution)/shard_map/all_to_all | solution.py:699

commit v8 on v7

--- a/solution.py
+++ b/solution.py
@@ -462,7 +462,7 @@
     copy.wait()
 
 
-def latent_kernel(low_in, folded, after, latent_out, low, sem):
+def latent_kernel(low_in, folded, after, latent_out, low, latent, sem):
     copy = pltpu.make_async_copy(low_in, low, sem)
     copy.start()
     copy.wait()
@@ -479,10 +479,13 @@
         term = lax.dot_general(piece, spread, NT, preferred_element_type=F32)
         result = term if result is None else result + term
     for x in range(3):
-        latent_out[x, 0] = result[64 * x : 64 * x + 64]
-
-
-def sum_kernel(place, received, out):
+        latent[x, 0] = result[64 * x : 64 * x + 64]
+    copy = pltpu.make_async_copy(latent, latent_out, sem)
+    copy.start()
+    copy.wait()
+
+
+def sum_kernel(place, received, after, out):
     total = received[0].astype(F32)
     for s in range(1, received.shape[0]):
         total = total + received[s].astype(F32)
@@ -526,7 +529,7 @@
         kernel,
         out_shape=out_shape,
         in_specs=list(in_specs),
-        out_specs=specs if isinstance(out_shape, tuple) else VMEM,
+        out_specs=specs if isinstance(out_shape, tuple) else specs[0],
         scratch_shapes=list(scratch),
         compiler_params=pltpu.CompilerParams(vmem_limit_bytes=megabytes << 20),
         cost_estimate=flops and pl.CostEstimate(flops=flops, bytes_accessed=0, transcendentals=0),
@@ -625,9 +628,13 @@
 )
 latent_part = call(
     latent_kernel,
-    shape((3, 1, 64, 64)),
+    pltpu.HBM((3, 1, 64, 64), F32),
     [HBM, VMEM, ANY],
-    [pltpu.VMEM((8, 4, 64, 128), BF16), pltpu.SemaphoreType.DMA],
+    [
+        pltpu.VMEM((8, 4, 64, 128), BF16),
+        pltpu.VMEM((3, 1, 64, 64), F32),
+        pltpu.SemaphoreType.DMA,
+    ],
     14,
 )
 
@@ -693,9 +700,9 @@
 
     pieces = lax.all_to_all(parts.reshape(64, 16, 128), NEAR, 0, 0, tiled=True)
     piece = lax.axis_index(NEAR).astype(jnp.int32).reshape(1)
-    pieces = call(sum_kernel, shape((8, 16, 128)), [SMEM, VMEM])(piece, pieces)
+    pieces = call(sum_kernel, shape((8, 16, 128)), [SMEM, VMEM, ANY])(piece, pieces, in_hbm(latent_grad))
     pieces = lax.all_to_all(pieces, "y", 0, 0, tiled=True)
-    pieces = call(sum_kernel, shape((64, 16, 128), BF16), [SMEM, VMEM])(piece, pieces)
+    pieces = call(sum_kernel, shape((64, 16, 128), BF16), [SMEM, VMEM, ANY])(piece, pieces, in_hbm(latent_grad))
     whole = lax.all_to_all(pieces, NEAR, 0, 0, tiled=True)
     kernel_grad, head_grad, bias_grad = call(
         unpack_kernel, (shape((27, 64, 64)), shape((1, 64)), shape((1, 64))), [VMEM]

time: 126 us -> 125 us (level)
  blocking collectives: 14.4 us -> 33.7 us
  waiting for transfers between devices: 36.4 us -> 23.8 us
  starting transfers between devices: 52.4 us -> 45.5 us
    all_to_all x0 -> x1, blocking collectives: none -> 19.3 us  [per_device(): whole = lax.all_to_all(pieces, NEAR, 0, 0, tiled=True)]
    all_to_all x1 -> x0, waiting for transfers between devices: 9.87 us -> none  [per_device(): whole = lax.all_to_all(pieces, NEAR, 0, 0, tiled=True)]
    all_to_all x1 -> x0, starting transfers between devices: 6.87 us -> none  [per_device(): whole = lax.all_to_all(pieces, NEAR, 0, 0, tiled=True)]
    all_to_all x1, waiting for transfers between devices: 12.6 us -> 9.86 us  [per_device(): pieces = lax.all_to_all(parts.reshape(64, 16, 128), NEAR, 0, 0, tiled=True)]
  transfers between devices with their start and end apart: 10 -> 9, of which waited for: 6 -> 5; matrix products, arithmetic and copies ran while one was open for 0% -> 0% of each run, Pallas kernels for 10% -> 10%
where the time goes in v8:
time: 125 us; the launch traced here: 124 us
  starting transfers between devices  45.5 us (36%)
  blocking collectives  33.7 us (27%)
  waiting for transfers between devices  23.8 us (19%)
  Pallas kernels  19.1 us (15%)
  between operations  1.51 us (1%)
    all_to_all x1, blocking collectives, per_device(): whole = lax.all_to_all(pieces, NEAR, 0, 0, tiled=True)  19.3 us
    all_to_all x1, blocking collectives, per_device(): pieces = lax.all_to_all(pieces, 'y', 0, 0, tiled=True)  14.4 us
    ppermute x3, starting transfers between devices, shifted(): low = lax.ppermute(block[0], axes, [(i, i + 1) for i in range(size - 1)])  12.4 us
    all_to_all x1, starting transfers between devices, per_device(): speeds = lax.all_to_all(speed, SHOT, 0, 0, tiled=True)  11.5 us
    all_to_all x1, starting transfers between devices, per_device(): pieces = lax.all_to_all(parts.reshape(64, 16, 128), NEAR, 0, 0, tiled=True)  9.89 us
    all_to_all x1, waiting for transfers between devices, per_device(): pieces = lax.all_to_all(parts.reshape(64, 16, 128), NEAR, 0, 0, tiled=True)  9.86 us
    ppermute x3, starting transfers between devices, shifted(): high = lax.ppermute(block[1], axes, [(i + 1, i) for i in range(size - 1)])  7.32 us
    all_to_all x1, waiting for transfers between devices, per_device(): speeds = lax.all_to_all(speed, SHOT, 0, 0, tiled=True)  7.26 us
  transfers between devices with their start and end apart: 9, of which 5 were waited for; matrix products, arithmetic and copies ran while one was open for 0% of the time, Pallas kernels for 10%

profile of v8, /device:TPU:1, one launch (start us, length us, event | category | flops | bytes accessed | tf_op | source)
XLA Modules:
  0.0 124.2 jit_solution(8028733891156730013)
XLA Ops:
  0.6 6.0 %collective-permute-start.1 = (bf16[3,64,64]{2,1,0:T(8,128)(2,1)}, bf16[3,64,64]{2,1,0:T(8,128)(2,1)S(1)}, u32[]{:S(2)}, u32[]{:S(2)}) collective-permute-start(bf16[3,64,64]{2,1,0:T(8,128)(2,1)} %bitcast.14), channel_id=1, source_target_pairs={{0,1},{1,2},{2,3},{3,4},{4,5},{5,6},{6,7},{7,8},{8,9},{9,10},{10,1... | collective-permute-start | bytes 73736 | tf_op jit(solution)/shard_map/ppermute | solution.py:647
  6.7 4.0 %collective-permute-start = (bf16[3,64,64]{2,1,0:T(8,128)(2,1)}, bf16[3,64,64]{2,1,0:T(8,128)(2,1)S(1)}, u32[]{:S(2)}, u32[]{:S(2)}) collective-permute-start(bf16[3,64,64]{2,1,0:T(8,128)(2,1)} %bitcast.15), channel_id=1, source_target_pairs={{1,0},{2,1},{3,2},{4,3},{5,4},{6,5},{7,6},{8,7},{9,8},{10,9},{11,1... | collective-permute-start | bytes 73736 | tf_op jit(solution)/shard_map/ppermute | solution.py:648
  10.7 0.0 copy-start.3
  10.7 0.6 copy-done.3
  11.4 1.4 %shard_map.156 = (f32[24,32,128]{2,1,0:T(8,128)S(1)}, f32[24,32,128]{2,1,0:T(8,128)S(1)}, bf16[3,64,64]{2,1,0:T(8,128)(2,1)S(1)}, bf16[576,192]{1,0:T(8,128)(2,1...) custom-call(f32[1,6,32,128]{3,2,1,0:T(8,128)} %wave_now.3, f32[1,6,32,128]{3,2,1,0:T(8,128)} %wave_prev.3, ...), custom_call_target="tpu_custom_call" | custom-call | tf_op jit(solution)/shard_map/pallas_call | solution.py:672
  12.8 0.0 copy-start.1
  12.8 0.0 copy-start.2
  12.8 0.0 copy-start
  12.8 0.0 collective-permute-done.1.low
  12.8 1.0 collective-permute-done.high
  13.8 0.1 shard_map.157.own
  13.9 4.0 %collective-permute-start.5 = (bf16[9,32,128]{2,1,0:T(8,128)(2,1)S(1)}, bf16[9,32,128]{2,1,0:T(8,128)(2,1)S(1)}, u32[]{:S(2)}, u32[]{:S(2)}) collective-permute-start(bf16[9,32,128]{2,1,0:T(8,128)(2,1)S(1)} %shard_map.157.own), channel_id=1, source_target_pairs={{0,32},{32,64},{64,96},{96,128},{128,160},{160,192},{192,224},{224... | collective-permute-start | bytes 221192 | tf_op jit(solution)/shard_map/ppermute | solution.py:647
  17.9 1.3 %collective-permute-start.4 = (bf16[9,32,128]{2,1,0:T(8,128)(2,1)S(1)}, bf16[9,32,128]{2,1,0:T(8,128)(2,1)S(1)}, u32[]{:S(2)}, u32[]{:S(2)}) collective-permute-start(bf16[9,32,128]{2,1,0:T(8,128)(2,1)S(1)} %shard_map.157.own), channel_id=1, source_target_pairs={{32,0},{64,32},{96,64},{128,96},{160,128},{192,160},{224,192},{256... | collective-permute-start | bytes 221192 | tf_op jit(solution)/shard_map/ppermute | solution.py:648
  19.2 2.4 %collective-permute-start.2 = (f32[24,32,128]{2,1,0:T(8,128)S(1)}, f32[24,32,128]{2,1,0:T(8,128)S(1)}, u32[]{:S(2)}, u32[]{:S(2)}) collective-permute-start(f32[24,32,128]{2,1,0:T(8,128)S(1)} %get-tuple-element.27), channel_id=1, source_target_pairs={{0,1},{1,2},{2,3},{3,4},{4,5},{5,6},{6,7},{7,8},{8,9},{9,10},{10,1... | collective-permute-start | bytes 1179656 | tf_op jit(solution)/shard_map/ppermute | solution.py:647
  21.6 2.0 %collective-permute-start.3 = (f32[24,32,128]{2,1,0:T(8,128)S(1)}, f32[24,32,128]{2,1,0:T(8,128)S(1)}, u32[]{:S(2)}, u32[]{:S(2)}) collective-permute-start(f32[24,32,128]{2,1,0:T(8,128)S(1)} %get-tuple-element.28), channel_id=1, source_target_pairs={{1,0},{2,1},{3,2},{4,3},{5,4},{6,5},{7,6},{8,7},{9,8},{10,9},{11,1... | collective-permute-start | bytes 1179656 | tf_op jit(solution)/shard_map/ppermute | solution.py:648
  23.6 0.0 collective-permute-done.5.z_prev
  23.6 0.1 collective-permute-done.4.z_next
  23.6 2.8 %shard_map.158 = (f32[16,32,128]{2,1,0:T(8,128)}, bf16[3,192,640]{2,1,0:T(8,128)(2,1)S(1)}) custom-call(bf16[9,32,128]{2,1,0:T(8,128)(2,1)S(1)} %collective-permute-done.4.z_next, bf16[9,32,128]{2,1,0:T(8,128)(2,1)S(1)} %shard_map.157.own, bf16[9,32,128]{2,1,0:T(8,128)(2,1)S(1)} %collective-permute-done.5.z_prev, ...), custom_call_target="tpu_custom_call" | custom-call | flops 500000000 | tf_op jit(solution)/shard_map/pallas_call | solution.py:680
  26.5 0.0 copy-done.1
  26.5 0.0 copy-done.2
  26.5 11.5 %all-to-all-start = ((f32[16,32,128]{2,1,0:T(8,128)}), f32[16,32,128]{2,1,0:T(8,128)S(1)}, u32[]{:S(2)}, u32[]{:S(2)}) async-start(f32[16,32,128]{2,1,0:T(8,128)} %get-tuple-element.33.after), calls=%async_computation | async-start | bytes 524288 | tf_op jit(solution)/shard_map/all_to_all | solution.py:681
  38.6 0.0 collective-permute-done.2.left
  38.6 0.0 collective-permute-done.3.right
  38.6 2.5 %shard_map.159 = (f32[30,32,128]{2,1,0:T(8,128)S(1)}, f32[4,384,128]{2,1,0:T(8,128)}) custom-call(s32[1]{0:T(128)} %bitcast.place, f32[1,6,32,128]{3,2,1,0:T(8,128)} %wave_now.3, f32[1,6,32,128]{3,2,1,0:T(8,128)} %wave_prev.3, f32[1,6,32,128]{3,2,1,0:T(8,128)} %adj_next.3, f32[1,6,32,128]{3,2,1,0:T(8,128)} %adj_after.3, f32[6,32,128]{2,1,0:T(8,128)} %density.3, ...), custom_call_target="tpu_custom_call" | custom-call | flops 2000000000 | tf_op jit(solution)/shard_map/pallas_call | solution.py:683
  41.1 0.0 copy-done
  41.1 7.3 %all-to-all-done = f32[16,32,128]{2,1,0:T(8,128)S(1)} async-done(((f32[16,32,128]{2,1,0:T(8,128)}), f32[16,32,128]{2,1,0:T(8,128)S(1)}, u32[]{:S(2)}, u32[]{:S(2)}) %all-to-all-start) | async-done | bytes 262176 | tf_op jit(solution)/shard_map/all_to_all | solution.py:681
  48.4 2.9 %shard_map.160.after = f32[16,32,128]{2,1,0:T(8,128)} custom-call(s32[1]{0:T(128)} %bitcast.place, s32[1]{0:T(128)S(6)} %copy.17.source, f32[1,3]{1,0:T(1,128)} %pulses_in.1, f32[24,32,128]{2,1,0:T(8,128)S(1)} %collective-permute-done.2.left, f32[24,32,128]{2,1,0:T(8,128)S(1)} %collective-permute-done.3.right, f32[512,128]{1,0:T(8,128)S(1)} %bitcast.12, ...), custom_call_target="tpu_custom_call" | custom-call | tf_op jit(solution)/shard_map/pallas_call | solution.py:686
  51.3 4.4 %all-to-all-start.1 = ((f32[16,32,128]{2,1,0:T(8,128)}), f32[16,32,128]{2,1,0:T(8,128)S(1)}, u32[]{:S(2)}, u32[]{:S(2)}) async-start(f32[16,32,128]{2,1,0:T(8,128)} %shard_map.160.after), calls=%async_computation.1 | async-start | bytes 524288 | tf_op jit(solution)/shard_map/all_to_all | solution.py:696
  55.7 3.3 %shard_map.161 = (f32[45,64,128]{2,1,0:T(8,128)S(1)}, bf16[384,1024]{1,0:T(8,128)(2,1)S(1)}) custom-call(bf16[3,192,640]{2,1,0:T(8,128)(2,1)S(1)} %get-tuple-element.36.lines, bf16[576,192]{1,0:T(8,128)(2,1)} %copy-done, f32[64,128]{1,0:T(8,128)} %copy-done.1, f32[64,128]{1,0:T(8,128)} %copy-done.2, bf16[27,64,64]{2,1,0:T(8,128)(2,1)} %kernel_in.3, ...), custom_call_target="tpu_custom_call" | custom-call | tf_op jit(solution)/shard_map/pallas_call | solution.py:697
  59.0 5.6 %all-to-all-done.1.received = f32[16,32,128]{2,1,0:T(8,128)S(1)} async-done(((f32[16,32,128]{2,1,0:T(8,128)}), f32[16,32,128]{2,1,0:T(8,128)S(1)}, u32[]{:S(2)}, u32[]{:S(2)}) %all-to-all-start.1) | async-done | bytes 262176 | tf_op jit(solution)/shard_map/all_to_all | solution.py:696
  64.6 2.2 %shard_map.162 = (bf16[8,4,64,128]{3,2,1,0:T(8,128)(2,1)}, bf16[1024,128]{1,0:T(8,128)(2,1)}) custom-call(f32[16,32,128]{2,1,0:T(8,128)S(1)} %all-to-all-done.1.received, f32[45,64,128]{2,1,0:T(8,128)S(1)} %get-tuple-element.37.slopes, bf16[3,192,640]{2,1,0:T(8,128)(2,1)S(1)} %get-tuple-element.36.lines), custom_call_target="tpu_custom_call" | custom-call | tf_op jit(solution)/shard_map/pallas_call | solution.py:698
  66.8 9.9 %all-to-all-start.2 = ((bf16[64,16,128]{2,1,0:T(8,128)(2,1)}), bf16[64,16,128]{2,1,0:T(8,128)(2,1)S(1)}, u32[]{:S(2)}, u32[]{:S(2)}) async-start(bf16[64,16,128]{2,1,0:T(8,128)(2,1)} %bitcast.7), calls=%async_computation.2 | async-start | bytes 524288 | tf_op jit(solution)/shard_map/all_to_all | solution.py:701
  76.7 2.8 %shard_map.163.after = f32[3,1,64,64]{3,2,1,0:T(8,128)} custom-call(bf16[8,4,64,128]{3,2,1,0:T(8,128)(2,1)} %get-tuple-element.38.low_in, bf16[384,1024]{1,0:T(8,128)(2,1)S(1)} %get-tuple-element.39.folded, bf16[1024,128]{1,0:T(8,128)(2,1)} %get-tuple-element.40.after), custom_call_target="tpu_custom_call" | custom-call | tf_op jit(solution)/shard_map/pallas_call | solution.py:699
  79.5 9.9 %all-to-all-done.2.received = bf16[64,16,128]{2,1,0:T(8,128)(2,1)S(1)} async-done(((bf16[64,16,128]{2,1,0:T(8,128)(2,1)}), bf16[64,16,128]{2,1,0:T(8,128)(2,1)S(1)}, u32[]{:S(2)}, u32[]{:S(2)}) %all-to-all-start.2) | async-done | bytes 262176 | tf_op jit(solution)/shard_map/all_to_all | solution.py:701
  89.3 0.1 shard_map.164
  89.4 14.4 %all_to_all.25.received = f32[8,16,128]{2,1,0:T(8,128)S(1)} all-to-all(f32[8,16,128]{2,1,0:T(8,128)S(1)} %shard_map.164), channel_id=1, replica_groups=mesh['xlo'=2,'z'=8,'y'=8,'xhi'=2,'core'=2] {'y'}, dimensions={0} | all-to-all | bytes 131072 | tf_op jit(solution)/shard_map/all_to_all | solution.py:704
  103.8 19.3 %all_to_all.26 = bf16[64,16,128]{2,1,0:T(8,128)(2,1)S(1)} all-to-all(bf16[64,16,128]{2,1,0:T(8,128)(2,1)S(1)} %shard_map.165), channel_id=1, replica_groups=mesh['xlo'=2,'z'=8,'y'=8,'xhi'=2,'core'=2] {'xlo','z','xhi','core'}, dimensions={0} | all-to-all | bytes 524288 | tf_op jit(solution)/shard_map/all_to_all | solution.py:706
  123.1 1.0 shard_map.166
  (1 shorter events, 0.0 us)
Async XLA Ops:
  0.6 12.2 %collective-permute-start.1 = (bf16[3,64,64]{2,1,0:T(8,128)(2,1)}, bf16[3,64,64]{2,1,0:T(8,128)(2,1)S(1)}, u32[]{:S(2)}, u32[]{:S(2)}) collective-permute-start(bf16[3,64,64]{2,1,0:T(8,128)(2,1)} %bitcast.14), channel_id=1, source_target_pairs={{0,1},{1,2},{2,3},{3,4},{4,5},{5,6},{6,7},{7,8},{8,9},{9,10},{10,1... | collective-permute-start | bytes 73736 | tf_op jit(solution)/shard_map/ppermute | solution.py:647
  6.7 7.1 %collective-permute-start = (bf16[3,64,64]{2,1,0:T(8,128)(2,1)}, bf16[3,64,64]{2,1,0:T(8,128)(2,1)S(1)}, u32[]{:S(2)}, u32[]{:S(2)}) collective-permute-start(bf16[3,64,64]{2,1,0:T(8,128)(2,1)} %bitcast.15), channel_id=1, source_target_pairs={{1,0},{2,1},{3,2},{4,3},{5,4},{6,5},{7,6},{8,7},{9,8},{10,9},{11,1... | collective-permute-start | bytes 73736 | tf_op jit(solution)/shard_map/ppermute | solution.py:648
  10.7 0.7 copy-start.3
  12.8 13.7 %copy-start.1 = (f32[64,128]{1,0:T(8,128)}, f32[64,128]{1,0:T(8,128)S(1)}, u32[]{:S(2)}) copy-start(f32[64,128]{1,0:T(8,128)S(1)} %get-tuple-element.31.bias.bias_in) | copy-start | bytes 98308
  12.8 13.7 %copy-start.2 = (f32[64,128]{1,0:T(8,128)}, f32[64,128]{1,0:T(8,128)S(1)}, u32[]{:S(2)}) copy-start(f32[64,128]{1,0:T(8,128)S(1)} %get-tuple-element.32.head.head_in) | copy-start | bytes 98308
  12.8 28.3 %copy-start = (bf16[576,192]{1,0:T(8,128)(2,1)}, bf16[576,192]{1,0:T(8,128)(2,1)S(1)}, u32[]{:S(2)}) copy-start(bf16[576,192]{1,0:T(8,128)(2,1)S(1)} %get-tuple-element.30.wall.wall_in) | copy-start | bytes 663556
  13.9 9.7 %collective-permute-start.5 = (bf16[9,32,128]{2,1,0:T(8,128)(2,1)S(1)}, bf16[9,32,128]{2,1,0:T(8,128)(2,1)S(1)}, u32[]{:S(2)}, u32[]{:S(2)}) collective-permute-start(bf16[9,32,128]{2,1,0:T(8,128)(2,1)S(1)} %shard_map.157.own), channel_id=1, source_target_pairs={{0,32},{32,64},{64,96},{96,128},{128,160},{160,192},{192,224},{224... | collective-permute-start | bytes 221192 | tf_op jit(solution)/shard_map/ppermute | solution.py:647
  17.9 5.7 %collective-permute-start.4 = (bf16[9,32,128]{2,1,0:T(8,128)(2,1)S(1)}, bf16[9,32,128]{2,1,0:T(8,128)(2,1)S(1)}, u32[]{:S(2)}, u32[]{:S(2)}) collective-permute-start(bf16[9,32,128]{2,1,0:T(8,128)(2,1)S(1)} %shard_map.157.own), channel_id=1, source_target_pairs={{32,0},{64,32},{96,64},{128,96},{160,128},{192,160},{224,192},{256... | collective-permute-start | bytes 221192 | tf_op jit(solution)/shard_map/ppermute | solution.py:648
  19.2 19.4 %collective-permute-start.2 = (f32[24,32,128]{2,1,0:T(8,128)S(1)}, f32[24,32,128]{2,1,0:T(8,128)S(1)}, u32[]{:S(2)}, u32[]{:S(2)}) collective-permute-start(f32[24,32,128]{2,1,0:T(8,128)S(1)} %get-tuple-element.27), channel_id=1, source_target_pairs={{0,1},{1,2},{2,3},{3,4},{4,5},{5,6},{6,7},{7,8},{8,9},{9,10},{10,1... | collective-permute-start | bytes 1179656 | tf_op jit(solution)/shard_map/ppermute | solution.py:647
  21.6 17.1 %collective-permute-start.3 = (f32[24,32,128]{2,1,0:T(8,128)S(1)}, f32[24,32,128]{2,1,0:T(8,128)S(1)}, u32[]{:S(2)}, u32[]{:S(2)}) collective-permute-start(f32[24,32,128]{2,1,0:T(8,128)S(1)} %get-tuple-element.28), channel_id=1, source_target_pairs={{1,0},{2,1},{3,2},{4,3},{5,4},{6,5},{7,6},{8,7},{9,8},{10,9},{11,1... | collective-permute-start | bytes 1179656 | tf_op jit(solution)/shard_map/ppermute | solution.py:648
  26.5 21.9 %all-to-all-start = ((f32[16,32,128]{2,1,0:T(8,128)}), f32[16,32,128]{2,1,0:T(8,128)S(1)}, u32[]{:S(2)}, u32[]{:S(2)}) async-start(f32[16,32,128]{2,1,0:T(8,128)} %get-tuple-element.33.after), calls=%async_computation | async-start | bytes 524288 | tf_op jit(solution)/shard_map/all_to_all | solution.py:681
  51.3 13.3 %all-to-all-start.1 = ((f32[16,32,128]{2,1,0:T(8,128)}), f32[16,32,128]{2,1,0:T(8,128)S(1)}, u32[]{:S(2)}, u32[]{:S(2)}) async-start(f32[16,32,128]{2,1,0:T(8,128)} %shard_map.160.after), calls=%async_computation.1 | async-start | bytes 524288 | tf_op jit(solution)/shard_map/all_to_all | solution.py:696
  66.8 22.5 %all-to-all-start.2 = ((bf16[64,16,128]{2,1,0:T(8,128)(2,1)}), bf16[64,16,128]{2,1,0:T(8,128)(2,1)S(1)}, u32[]{:S(2)}, u32[]{:S(2)}) async-start(bf16[64,16,128]{2,1,0:T(8,128)(2,1)} %bitcast.7), calls=%async_computation.2 | async-start | bytes 524288 | tf_op jit(solution)/shard_map/all_to_all | solution.py:701
